TPU v7x, 32 devices: a whole 2x2x4 slice. The times are simulated.
32 devices in a mesh: seq: 8 (over z, y), chan: 4 (over x, core).
Axes of the slice: x: 2, y: 2, z: 4, core: 2. Of those that a mesh axis runs over, the one named last changes fastest.
Arguments:
- tokens: bfloat16 [4, 1024, 1152], P(None, 'seq'), may hold values from -6 to 6
- teacher: bfloat16 [4, 1024, 1152], P(None, 'seq'), may hold values from -6 to 6
- true_lengths: int32 [4], replicated, may hold values from 512 to 1024
- doc_lengths: int32 [4, 3], replicated, may hold values from 1 to 960, 1024 in all within a row
- routes: int32 [4, 1024], P(None, 'seq'), may hold values from 0 to 7, as said below
- norm1_gain: bfloat16 [1152], replicated, may hold values from 0.5 to 1.5
- in_weight: bfloat16 [1152, 2, 2304], P(None, None, 'chan'), may hold values from -0.1875 to 0.1875
- conv_weight: bfloat16 [4, 2304], P(None, 'chan'), may hold values from -3 to 3
- conv_bias: bfloat16 [2304], P('chan'), may hold values from -3 to 3
- xproj_weight: bfloat16 [2304, 104], P('chan'), may hold values from -0.125 to 0.125
- dt_weight: bfloat16 [72, 2304], P(None, 'chan'), may hold values from -0.75 to 0.75
- dt_bias: float32 [2304], P('chan'), may hold values from -6 to -2
- a_log: float32 [2304, 16], P('chan'), may hold values from -9 to 0
- skip_weight: float32 [2304], P('chan'), may hold values from 0.5 to 1.5
- out_weight: bfloat16 [2304, 1152], P('chan'), may hold values from -0.25 to 0.25
- norm2_gain: bfloat16 [1152], replicated, may hold values from 0.5 to 1.5
- router_weight: bfloat16 [1152, 8], replicated, may hold values from -0.109375 to 0.109375
- expert_in: bfloat16 [8, 1152, 3072], P('seq'), may hold values from -0.1875 to 0.1875
- expert_out: bfloat16 [8, 3072, 1152], P('seq'), may hold values from -0.3125 to 0.3125
Outputs:
- layer_out: bfloat16 [4, 1024, 1152], P(None, 'seq')
- loss: float32 [], replicated
- grad_tokens: float32 [4, 1024, 1152], P(None, 'seq')
- grad_norm1_gain: float32 [1152], replicated
- grad_in_weight: float32 [1152, 2, 2304], P(None, None, 'chan')
- grad_conv_weight: float32 [4, 2304], P(None, 'chan')
- grad_conv_bias: float32 [2304], P('chan')
- grad_xproj_weight: float32 [2304, 104], P('chan')
- grad_dt_weight: float32 [72, 2304], P(None, 'chan')
- grad_dt_bias: float32 [2304], P('chan')
- grad_a_log: float32 [2304, 16], P('chan')
- grad_skip_weight: float32 [2304], P('chan')
- grad_out_weight: float32 [2304, 1152], P('chan')
- grad_norm2_gain: float32 [1152], replicated
- grad_router_weight: float32 [1152, 8], replicated
- grad_expert_in: float32 [8, 1152, 3072], P('seq', None, 'chan')
- grad_expert_out: float32 [8, 3072, 1152], P('seq', 'chan')
Inputs may be any that keep to these rules, and one draw needn't show every extreme that they name: `routes`: each position names one expert. In every aligned block of 128 positions of a sequence no expert is named more than 32 times, and one expert, the same in all blocks, is named exactly 32 times in every block. `doc_lengths`: the documents of each sequence, in order; their lengths sum to 1024.
All inputs are finite; a program needn't handle non-finite values.
Results may differ from a plain program's by a relative error of at most 0.013.
Values may be sent and summed in bfloat16 or wider, within the bound.
A program may use at most 448 MiB of HBM per device.

v0:
```python
import functools

import jax
import jax.numpy as jnp
from jax import lax
from jax.experimental import pallas as pl
from jax.experimental.pallas import tpu as pltpu
from jax.sharding import PartitionSpec as P

epsilon = 1e-05
log2e = 1.4426950408889634
cut = 1e30
MESH = pl.DeviceIdType.MESH
f32 = jnp.float32
bf16 = jnp.bfloat16
LANES = 128
MIB = 1024 * 1024


def exchange_kernel(axis, count, gather, x_ref, o_ref, own_sem, send_sem, recv_sem):
    me = lax.axis_index(axis)
    barrier = pltpu.get_barrier_semaphore()
    for k in range(1, count):
        pl.semaphore_signal(
            barrier, inc=1, device_id={axis: lax.rem(me + k, count)}, device_id_type=MESH
        )
    own = pltpu.make_async_copy(x_ref if gather else x_ref.at[me], o_ref.at[me], own_sem)
    own.start()
    pl.semaphore_wait(barrier, count - 1)
    copies = []
    for k in range(1, count):
        to = lax.rem(me + k, count)
        copies.append(
            pltpu.make_async_remote_copy(
                src_ref=x_ref if gather else x_ref.at[to],
                dst_ref=o_ref.at[me],
                send_sem=send_sem.at[k - 1],
                recv_sem=recv_sem.at[k - 1],
                device_id={axis: to},
                device_id_type=MESH,
            )
        )
        copies[-1].start()
    own.wait()
    for copy in copies:
        copy.wait()


def exchange(x, axis, gather, number):
    count = lax.axis_size(axis)
    shape = (count,) + x.shape if gather else x.shape
    return pl.pallas_call(
        functools.partial(exchange_kernel, axis, count, gather),
        out_shape=jax.ShapeDtypeStruct(shape, x.dtype),
        in_specs=[pl.BlockSpec(memory_space=pl.ANY)],
        out_specs=pl.BlockSpec(memory_space=pl.ANY),
        scratch_shapes=[
            pltpu.SemaphoreType.DMA,
            pltpu.SemaphoreType.DMA((count - 1,)),
            pltpu.SemaphoreType.DMA((count - 1,)),
        ],
        compiler_params=pltpu.CompilerParams(
            collective_id=number, has_side_effects=True, vmem_limit_bytes=16 * MIB
        ),
    )(x)


def turned(value):
    return pltpu.roll(value, value.shape[0] // 2, 0)


def carry_kernel(axis, count, back, local_ref, sums_ref, rate_ref, o_ref, send, got, send_sum, got_sum, total, enter,
                 send_sem, recv_sem, send_sum_sem, recv_sum_sem):
    me = lax.axis_index(axis)
    states, rows, width = local_ref.shape
    half = rows // 2
    spans = []
    span = 1
    while span < count:
        spans.append(span)
        span *= 2
    sign = -1 if back else 1
    barrier = pltpu.get_barrier_semaphore()
    greeted = 0
    for span in spans:
        for by in (span, -span):
            there = me + by
            greeted = greeted + jnp.where((there >= 0) & (there < count), 1, 0)

            @pl.when((there >= 0) & (there < count))
            def _():
                pl.semaphore_signal(barrier, inc=1, device_id={axis: there}, device_id_type=MESH)

    upper = lax.broadcasted_iota(jnp.int32, (rows, width), 0) >= half
    first = upper if back else jnp.logical_not(upper)
    sums = sums_ref[...]
    sums_turned = turned(sums)
    sums_both = sums + sums_turned
    sums_first = jnp.where(first, sums, sums_turned)
    sums_last = jnp.where(first, sums_turned, sums)

    def packed_rate(j):
        return jnp.where(upper, rate_ref[pl.ds(2 * j + 1, 1), :], rate_ref[pl.ds(2 * j, 1), :])

    def both(j):
        even, odd = local_ref[2 * j], local_ref[2 * j + 1]
        low = jnp.where(upper, turned(odd), even)
        high = jnp.where(upper, odd, turned(even))
        return (high, low) if back else (low, high)

    for j in range(states // 2):
        begin, end = both(j)
        total[j] = jnp.exp2(packed_rate(j) * sums_last) * begin + end
        enter[j] = jnp.zeros((rows, width), f32)

    pl.semaphore_wait(barrier, greeted)

    sums_total = sums_both
    sums_enter = jnp.zeros((rows, width), f32)
    for turn, span in enumerate(spans):
        to = me + sign * span
        origin = me - sign * span
        sends = (to >= 0) & (to < count)
        takes = (origin >= 0) & (origin < count)
        for j in range(0, states // 2, 2):
            send[turn, pl.ds(j * rows, 2 * rows), :] = jnp.concatenate([total[j], total[j + 1]], axis=0).astype(bf16)
        send_sum[turn] = sums_total
        copies = [
            pltpu.make_async_remote_copy(
                src_ref=source.at[turn],
                dst_ref=target.at[turn],
                send_sem=ssem.at[turn],
                recv_sem=rsem.at[turn],
                device_id={axis: to},
                device_id_type=MESH,
            )
            for source, target, ssem, rsem in (
                (send, got, send_sem, recv_sem),
                (send_sum, got_sum, send_sum_sem, recv_sum_sem),
            )
        ]

        @pl.when(sends)
        def _():
            for copy in copies:
                copy.start()

        @pl.when(jnp.logical_not(takes))
        def _():
            got[turn] = jnp.zeros(got.shape[1:], bf16)
            got_sum[turn] = jnp.zeros(got_sum.shape[1:], f32)

        @pl.when(takes)
        def _():
            for copy in copies:
                copy.wait_recv()

        for j in range(0, states // 2, 2):
            pair = got[turn, pl.ds(j * rows, 2 * rows), :].astype(f32)
            for i in (j, j + 1):
                came = pair[(i - j) * rows : (i - j + 1) * rows]
                rate = packed_rate(i)
                enter[i] = jnp.exp2(rate * sums_enter) * came + enter[i]
                total[i] = jnp.exp2(rate * sums_total) * came + total[i]
        sums_enter = sums_enter + got_sum[turn]
        sums_total = sums_total + got_sum[turn]

        @pl.when(sends)
        def _():
            for copy in copies:
                copy.wait_send()

    for j in range(states // 2):
        begin, _ = both(j)
        outer = enter[j]
        inner = jnp.exp2(packed_rate(j) * sums_first) * outer + begin
        low, high = (inner, outer) if back else (outer, inner)
        o_ref[2 * j] = jnp.where(upper, turned(high), low)
        o_ref[2 * j + 1] = jnp.where(upper, high, turned(low))


def carried(local, sums, rate, axis, back, number):
    count = lax.axis_size(axis)
    states, rows, width = local.shape
    turns = max(1, (count - 1).bit_length())
    return pl.pallas_call(
        functools.partial(carry_kernel, axis, count, back),
        out_shape=jax.ShapeDtypeStruct(local.shape, f32),
        in_specs=[pl.BlockSpec(memory_space=pltpu.VMEM)] * 3,
        out_specs=pl.BlockSpec(memory_space=pltpu.VMEM),
        scratch_shapes=[
            pltpu.VMEM((turns, states // 2 * rows, width), bf16),
            pltpu.VMEM((turns, states // 2 * rows, width), bf16),
            pltpu.VMEM((turns, rows, width), f32),
            pltpu.VMEM((turns, rows, width), f32),
            pltpu.VMEM((states // 2, rows, width), f32),
            pltpu.VMEM((states // 2, rows, width), f32),
            pltpu.SemaphoreType.DMA((turns,)),
            pltpu.SemaphoreType.DMA((turns,)),
            pltpu.SemaphoreType.DMA((turns,)),
            pltpu.SemaphoreType.DMA((turns,)),
        ],
        compiler_params=pltpu.CompilerParams(
            collective_id=number, has_side_effects=True, vmem_limit_bytes=24 * MIB
        ),
    )(local, sums, rate)


def spread(mapped_ref, first, wide_ref):
    steps, count, rows, lanes = wide_ref.shape

    def one(p, _):
        values = mapped_ref[p]
        for n in range(count):
            wide_ref[p, n] = jnp.broadcast_to(values[:, first + n : first + n + 1], (rows, lanes))
        return 0

    lax.fori_loop(0, steps, one, 0)


def rows_of(rate_ref, n, rows):
    return jnp.broadcast_to(rate_ref[n : n + 1, :], (rows, rate_ref.shape[1]))


def totals_kernel(rank, delta_ref, drive_ref, mapped_ref, rate_ref, last_ref, sums_ref, wide):
    steps, count, rows, lanes = wide.shape

    @pl.when(pl.program_id(0) == 0)
    def _():
        spread(mapped_ref, rank, wide)

    rates = [rows_of(rate_ref, n, rows) for n in range(count)]
    zero = jnp.zeros((rows, lanes), f32)

    def one(p, held):
        states, sums = held
        step, drive = delta_ref[p], drive_ref[p]
        states = tuple(
            jnp.exp2(step * rates[n]) * states[n] + drive * wide[p, n] for n in range(count)
        )
        return states, sums + step

    states, sums = lax.fori_loop(0, steps, one, ((zero,) * count, zero))
    for n in range(count):
        last_ref[n] = states[n]
    sums_ref[...] = sums


def states_kernel(rank, delta_ref, drive_ref, mapped_ref, rate_ref, enter_ref, y_ref, state_ref, wide_in, wide_read):
    steps, count, rows, lanes = wide_in.shape

    @pl.when(pl.program_id(0) == 0)
    def _():
        spread(mapped_ref, rank, wide_in)
        spread(mapped_ref, rank + count, wide_read)

    rates = [rows_of(rate_ref, n, rows) for n in range(count)]

    def one(p, states):
        step, drive = delta_ref[p], drive_ref[p]
        states = tuple(
            jnp.exp2(step * rates[n]) * states[n] + drive * wide_in[p, n] for n in range(count)
        )
        terms = [states[n] * wide_read[p, n] for n in range(count)]
        while len(terms) > 1:
            terms = [a + b for a, b in zip(terms[::2], terms[1::2])]
        y_ref[p] = terms[0]
        for n in range(count):
            state_ref[p, n] = states[n]
        return states

    lax.fori_loop(0, steps, one, tuple(enter_ref[n] for n in range(count)))


def back_totals_kernel(rank, delta_ref, grad_y_ref, mapped_ref, rate_ref, last_ref, wide):
    steps, count, rows, lanes = wide.shape

    @pl.when(pl.program_id(0) == 0)
    def _():
        spread(mapped_ref, rank + count, wide)

    rates = [rows_of(rate_ref, n, rows) for n in range(count)]
    zero = jnp.zeros((rows, lanes), f32)

    def one(turn, held):
        p = steps - 1 - turn
        step, grad_y = delta_ref[p], grad_y_ref[p]
        return tuple(
            jnp.exp2(step * rates[n]) * (held[n] + grad_y * wide[p, n]) for n in range(count)
        )

    held = lax.fori_loop(0, steps, one, (zero,) * count)
    for n in range(count):
        last_ref[n] = held[n]


def back_kernel(rank, width, delta_ref, drive_ref, grad_y_ref, mapped_ref, rate_ref, first_ref, state_ref, enter_ref,
                input_ref, decay_ref, log_ref, maps_ref, wide_in, wide_read, sum_in, sum_read):
    steps, count, rows, lanes = wide_in.shape
    place = pl.program_id(0)

    @pl.when(place == 0)
    def _():
        spread(mapped_ref, rank, wide_in)
        spread(mapped_ref, rank + count, wide_read)

    rates = [rows_of(rate_ref, n, rows) for n in range(count)]
    held = lax.broadcasted_iota(jnp.int32, (rows, lanes), 1) < width - place * lanes
    fresh = place == 0
    for n in range(count):
        log_ref[n] = jnp.zeros((rows, lanes), f32)

    def one(turn, carry):
        p = steps - 1 - turn
        before = jnp.maximum(p - 1, 0)
        opening = p == 0
        step, drive, grad_y = delta_ref[p], drive_ref[p], grad_y_ref[p]
        to_input = jnp.zeros((rows, lanes), f32)
        to_decay = jnp.zeros((rows, lanes), f32)
        new = []
        for n in range(count):
            grad = grad_y * wide_read[p, n] + carry[n]
            passed = jnp.exp2(step * rates[n]) * grad
            new.append(passed)
            prior = jnp.where(opening, first_ref[n], state_ref[before, n])
            grad_decay = passed * prior
            to_decay = to_decay + grad_decay * rates[n]
            log_ref[n] += grad_decay * step
            to_input = to_input + grad * wide_in[p, n]
            part_in = jnp.where(held, grad * drive, 0.0)
            part_read = jnp.where(held, grad_y * state_ref[p, n], 0.0)
            sum_in[p, n] = jnp.where(fresh, 0.0, sum_in[p, n]) + part_in
            sum_read[p, n] = jnp.where(fresh, 0.0, sum_read[p, n]) + part_read
        input_ref[p] = to_input
        decay_ref[p] = to_decay
        return tuple(new)

    lax.fori_loop(0, steps, one, tuple(enter_ref[n] for n in range(count)))

    @pl.when(place == pl.num_programs(0) - 1)
    def _():
        ones = jnp.ones((8, lanes), bf16)

        def flat(p, _):
            for which, source in enumerate((sum_in, sum_read)):
                block = source[p].reshape(count * rows, lanes).astype(bf16)
                out = lax.dot_general(ones, block, (((1,), (1,)), ((), ())), preferred_element_type=f32)
                maps_ref[which, p] = out
            return 0

        lax.fori_loop(0, steps, flat, 0)


def tiles(shape, last):
    return pl.BlockSpec(shape[:-1] + (last,), lambda i: (0,) * (len(shape) - 1) + (i,))


def whole(shape):
    return pl.BlockSpec(shape, lambda i: (0,) * len(shape))


def scan_call(kernel, ins, outs, scratch, cost):
    width = ins[0][0].shape[-1]
    return pl.pallas_call(
        kernel,
        grid=(pl.cdiv(width, LANES),),
        in_specs=[whole(a.shape) if full else tiles(a.shape, LANES) for a, full in ins],
        out_specs=[whole(s) if full else tiles(s, LANES) for s, full in outs],
        out_shape=[jax.ShapeDtypeStruct(s, f32) for s, _ in outs],
        scratch_shapes=[pltpu.VMEM(s, f32) for s in scratch],
        compiler_params=pltpu.CompilerParams(vmem_limit_bytes=56 * MIB),
        cost_estimate=cost,
    )(*[a for a, _ in ins])


def dot(a, b):
    return jnp.dot(a, b, preferred_element_type=f32)


def dot_nt(a, b):
    return lax.dot_general(a, b, (((1,), (1,)), ((), ())), preferred_element_type=f32)


def dot_tn(a, b):
    return lax.dot_general(a, b, (((0,), (0,)), ((), ())), preferred_element_type=f32)


def shifted(x, axis, by):
    length = lax.axis_size(axis)
    pairs = [(i, i + by) for i in range(length) if 0 <= i + by < length]
    return lax.ppermute(x, axis, pairs)


def turns_of(x, axis):
    count = lax.axis_size(axis)
    return [
        lax.ppermute(x, axis, [(i, (i + k) % count) for i in range(count)]) for k in range(1, count)
    ]


def turned_parts(x, axis):
    count = lax.axis_size(axis)
    me = lax.axis_index(axis)
    parts = [lax.dynamic_index_in_dim(x, me, 0, False)]
    for k in range(1, count):
        mine = lax.dynamic_index_in_dim(x, lax.rem(me + k, count), 0, False)
        parts.append(lax.ppermute(mine, axis, [(i, (i + k) % count) for i in range(count)]))
    return parts


def silu_slope(values):
    sigma = jax.nn.sigmoid(values)
    return sigma * (1.0 + values * (1.0 - sigma))


def norm_back(grad_normed, unit_rows, inverse, weight_gain):
    scaled = grad_normed * weight_gain
    return inverse * (scaled - unit_rows * jnp.mean(scaled * unit_rows, axis=-1, keepdims=True))


def local(
    tokens,
    teacher,
    true_lengths,
    doc_lengths,
    routes,
    norm1_gain,
    in_weight,
    conv_weight,
    conv_bias,
    xproj_weight,
    dt_weight,
    dt_bias,
    a_log,
    skip_weight,
    out_weight,
    norm2_gain,
    router_weight,
    expert_in,
    expert_out,
):
    seqs, group, width = tokens.shape
    inner = in_weight.shape[2]
    rank = dt_weight.shape[0]
    states = a_log.shape[1]
    experts = router_weight.shape[1]
    n_seq = lax.axis_size("seq")
    n_chan = lax.axis_size("chan")
    shards = n_seq // experts
    most = group // 4
    taps = conv_weight.shape[0]
    rim = taps - 1
    lines = 8
    chunks = lines // seqs
    steps = group // chunks
    owned = seqs * group // n_chan
    part = min(group, owned)
    most = min(most, part)
    parts = owned // part
    place = lax.axis_index("chan")
    first_pos = lax.axis_index("seq") * group

    def laid(x):
        x = x.reshape((seqs, chunks, steps) + x.shape[2:])
        return x.transpose((2, 1, 0) + tuple(range(3, x.ndim))).reshape((steps, lines) + x.shape[3:])

    def unlaid(x):
        x = x.reshape((steps, chunks, seqs) + x.shape[2:])
        return x.transpose((2, 1, 0) + tuple(range(3, x.ndim))).reshape((seqs, group) + x.shape[3:])

    at = (
        first_pos
        + jnp.arange(steps, dtype=jnp.int32)[:, None]
        + (jnp.arange(lines, dtype=jnp.int32) // seqs * steps)[None, :]
    )
    ends = []
    for k in range(doc_lengths.shape[1] - 1):
        ends.append(doc_lengths[:, k] + (ends[-1] if ends else 0))
    ends = [jnp.tile(end, chunks)[None, :] for end in ends]

    def doc_at(pos):
        return sum((pos >= end).astype(jnp.int32) for end in ends)

    doc_ids = doc_at(at)
    keep = (doc_ids == doc_at(at - 1)) & (at > 0)
    valid = [(doc_at(at - rim + k) == doc_ids).astype(f32)[..., None] for k in range(taps)]

    gain_one = norm1_gain.astype(f32)

    def normed_of(rows):
        full = rows.astype(f32)
        inverse = lax.rsqrt(jnp.mean(full * full, axis=-1, keepdims=True) + epsilon)
        return (full * inverse * gain_one).astype(bf16)

    conv_w_in, gate_w_in = in_weight[:, 0, :], in_weight[:, 1, :]
    prior_rows = shifted(tokens[:, group - rim :, :], "seq", 1)
    normed_one = normed_of(laid(tokens)).reshape(steps * lines, width)
    conv_in = dot(normed_one, conv_w_in).astype(bf16).reshape(steps, lines, inner)
    gate_z = dot(normed_one, gate_w_in).reshape(steps, lines, inner)
    prior_normed = normed_of(prior_rows.transpose(1, 0, 2)).reshape(rim * seqs, width)
    prior_in = dot(prior_normed, conv_w_in).astype(bf16).reshape(rim, seqs, inner)
    halo = jnp.concatenate([prior_in, conv_in[steps - rim :, : lines - seqs]], axis=1)
    extended = jnp.concatenate([halo, conv_in], axis=0)
    taps_full = conv_weight.astype(f32)

    def tapped(k):
        return extended[k : k + steps].astype(f32) * valid[k]

    pre_act = conv_bias.astype(f32) + sum(taps_full[k] * tapped(k) for k in range(taps))
    act = pre_act * jax.nn.sigmoid(pre_act)
    act_low = act.astype(bf16).reshape(steps * lines, inner)
    mapped_part = dot(act_low, xproj_weight).astype(bf16)
    mapped = jnp.sum(exchange(mapped_part, "chan", True, 1).astype(f32), axis=0)
    dt_low = mapped[:, :rank].astype(bf16)
    mapped_laid = mapped.reshape(steps, lines, rank + 2 * states)
    dt_pre = (dot(dt_low, dt_weight) + dt_bias).reshape(steps, lines, inner)
    delta = jax.nn.softplus(dt_pre)
    rate = -jnp.exp(a_log).T
    rate_two = rate * log2e
    step_size = jnp.where(keep[..., None], delta, cut)
    drive = delta * act

    flat = steps * lines * states * inner
    wide_shape = (steps, states, lines, LANES)
    last, sums = scan_call(
        functools.partial(totals_kernel, rank),
        [(step_size, False), (drive, False), (mapped_laid, True), (rate_two, False)],
        [((states, lines, inner), False), ((lines, inner), False)],
        [wide_shape],
        pl.CostEstimate(flops=5 * flat, bytes_accessed=8 * steps * lines * inner, transcendentals=flat),
    )
    enter = carried(last, sums, rate_two, "seq", False, 2)
    y_scan, state = scan_call(
        functools.partial(states_kernel, rank),
        [
            (step_size, False),
            (drive, False),
            (mapped_laid, True),
            (rate_two, False),
            (enter, False),
        ],
        [((steps, lines, inner), False), ((steps, states, lines, inner), False)],
        [wide_shape] * 2,
        pl.CostEstimate(flops=7 * flat, bytes_accessed=4 * flat, transcendentals=flat),
    )
    y_full = y_scan + skip_weight * act
    silu_z = gate_z * jax.nn.sigmoid(gate_z)
    gated = (y_full * silu_z).astype(bf16)
    gated_rows = gated.reshape(steps * lines, inner)
    out_part = dot(unlaid(gated).reshape(seqs * group, inner), out_weight).astype(bf16)
    mixed = jnp.sum(
        exchange(out_part.reshape(n_chan, owned, width), "chan", False, 3).astype(f32), axis=0
    )

    def own(x):
        rows = x.reshape((seqs * group,) + x.shape[2:])
        return lax.dynamic_slice_in_dim(rows, place * owned, owned, 0)

    tokens_own = own(tokens).astype(f32)
    inverse_one = lax.rsqrt(jnp.mean(tokens_own * tokens_own, axis=-1, keepdims=True) + epsilon)
    unit_one = tokens_own * inverse_one
    hidden_one = tokens_own + mixed
    inverse_two = lax.rsqrt(jnp.mean(hidden_one * hidden_one, axis=-1, keepdims=True) + epsilon)
    unit_two = hidden_one * inverse_two
    gain_two = norm2_gain.astype(f32)
    normed_two = (unit_two * gain_two).astype(bf16)
    probs = jax.nn.softmax(dot(normed_two, router_weight), axis=-1)
    routes_own = own(routes)
    chosen = routes_own[..., None] == jnp.arange(experts, dtype=jnp.int32)
    chosen_rows = chosen.astype(f32)
    gate_value = jnp.sum(probs * chosen_rows, axis=-1, keepdims=True)
    row = jnp.arange(owned, dtype=jnp.int32)
    earlier = (row[None, :] < row[:, None]) & (row[None, :] // part == row[:, None] // part)
    rank_in = dot(earlier.astype(bf16), chosen.astype(bf16))
    slots = parts * most
    wanted = rank_in + (row // part * most).astype(f32)[:, None]
    hit = (wanted[..., None] == jnp.arange(slots, dtype=f32)) & chosen[..., None]
    hit = hit.astype(bf16)
    hit_send = hit.reshape(owned, experts * slots)
    hit_back = jnp.repeat(hit, shards, axis=1).reshape(owned, n_seq * slots)

    def to_slabs(rows, number):
        packed = dot_tn(hit_send, rows).astype(bf16).reshape(experts, slots, width)
        came = exchange(jnp.repeat(packed, shards, axis=0), "seq", False, number)
        return came.reshape(n_seq * slots, width)

    def from_slabs(rows, number):
        came = exchange(rows.reshape(n_seq, slots, width), "seq", False, number)
        return dot(hit_back, came.reshape(n_seq * slots, width))

    first_slab, second_slab = expert_in[0], expert_out[0]
    units = first_slab.shape[1] // n_chan
    arrived = to_slabs(normed_two, 4)
    pre_hidden = dot(arrived, first_slab)
    cdf = 0.5 * (1.0 + lax.erf(pre_hidden * 0.7071067811865476))
    hidden_low = (pre_hidden * cdf).astype(bf16)
    density = jnp.exp(-0.5 * pre_hidden * pre_hidden) * 0.3989422804014327
    slope = cdf + pre_hidden * density
    result = dot(hidden_low, second_slab).astype(bf16)
    expert_total = from_slabs(result, 5)
    layer = hidden_one + gate_value * expert_total
    layer_low = layer.astype(bf16)

    flat_row = place * owned + row
    seq_of = flat_row // group
    lengths_own = sum(
        jnp.where(seq_of == s, true_lengths[s], 0) for s in range(seqs)
    )
    total_true = jnp.sum(true_lengths).astype(f32)
    loss_mask = (first_pos + flat_row % group < lengths_own).astype(f32)[:, None]
    error = layer - own(teacher).astype(f32)
    loss_part = jnp.sum(loss_mask * error * error) / total_true
    grad_layer = 2.0 / total_true * loss_mask * error
    grad_gate = jnp.sum(grad_layer * expert_total, axis=-1, keepdims=True)
    grad_result = (gate_value * grad_layer).astype(bf16)
    grad_rows = to_slabs(grad_result, 6)
    grad_pre = (dot_nt(grad_rows, second_slab) * slope).astype(bf16)
    grad_slab_rows = dot_nt(grad_pre, first_slab).astype(bf16)
    grad_expert = from_slabs(grad_slab_rows, 7)

    def by_units(x):
        return x.reshape(n_seq * slots, n_chan, units).transpose(1, 0, 2)

    rows_all = jnp.concatenate([arrived] + turns_of(arrived, "chan"), axis=0)
    hidden_all = jnp.concatenate(turned_parts(by_units(hidden_low), "chan"), axis=0)
    grad_rows_all = jnp.concatenate([grad_rows] + turns_of(grad_rows, "chan"), axis=0)
    grad_pre_all = jnp.concatenate(turned_parts(by_units(grad_pre), "chan"), axis=0)
    grad_first = dot_tn(rows_all, grad_pre_all)
    grad_second = dot_tn(hidden_all, grad_rows_all)

    grad_logit = grad_gate * gate_value * (chosen_rows - probs)
    grad_router = dot_tn(normed_two, grad_logit.astype(bf16))
    grad_normed_two = grad_expert + dot_nt(grad_logit.astype(bf16), router_weight)
    grad_gain_two = jnp.sum(grad_normed_two * unit_two, axis=0)
    grad_hidden_one = grad_layer + norm_back(grad_normed_two, unit_two, inverse_two, gain_two)

    grad_mixed = exchange(grad_hidden_one.astype(bf16), "chan", True, 8)
    grad_mixed = laid(grad_mixed.reshape(seqs, group, width)).reshape(steps * lines, width)
    grad_out_w = dot_tn(gated_rows, grad_mixed)
    grad_gated = dot_nt(grad_mixed, out_weight).reshape(steps, lines, inner)
    grad_y = grad_gated * silu_z
    grad_z = (grad_gated * y_full * silu_slope(gate_z)).astype(bf16)
    grad_z_rows = grad_z.reshape(steps * lines, inner)
    grad_in_gate = dot_tn(normed_one, grad_z_rows)
    grad_skip = jnp.sum(grad_y * act, axis=(0, 1))
    (back_last,) = scan_call(
        functools.partial(back_totals_kernel, rank),
        [(step_size, False), (grad_y, False), (mapped_laid, True), (rate_two, False)],
        [((states, lines, inner), False)],
        [wide_shape],
        pl.CostEstimate(flops=5 * flat, bytes_accessed=8 * steps * lines * inner, transcendentals=flat),
    )
    back_enter = carried(back_last, sums, rate_two, "seq", True, 9)
    state_input, from_decay, log_sums, maps = scan_call(
        functools.partial(back_kernel, rank, inner),
        [
            (step_size, False),
            (drive, False),
            (grad_y, False),
            (mapped_laid, True),
            (rate_two, False),
            (enter, False),
            (state, False),
            (back_enter, False),
        ],
        [
            ((steps, lines, inner), False),
            ((steps, lines, inner), False),
            ((states, lines, inner), False),
            ((2, steps, 8, states * lines), True),
        ],
        [wide_shape] * 4,
        pl.CostEstimate(flops=17 * flat, bytes_accessed=4 * flat, transcendentals=flat),
    )
    grad_a_log = (jnp.sum(log_sums, axis=1) * rate).T
    grad_maps = maps[:, :, 0].reshape(2, steps, states, lines).transpose(1, 3, 0, 2)
    grad_maps = grad_maps.reshape(steps * lines, 2 * states)
    grad_delta = from_decay * (1.0 / log2e) + state_input * act
    grad_dt_pre = grad_delta * jax.nn.sigmoid(dt_pre)
    grad_dt_bias = jnp.sum(grad_dt_pre, axis=(0, 1))
    grad_dt_low = grad_dt_pre.astype(bf16).reshape(steps * lines, inner)
    grad_dt_w = dot_tn(dt_low, grad_dt_low)
    low_part = jnp.concatenate([dot_nt(grad_dt_low, dt_weight), grad_maps], axis=1).astype(bf16)
    grad_mapped = jnp.sum(exchange(low_part, "chan", True, 10).astype(f32), axis=0).astype(bf16)
    grad_xproj = dot_tn(act_low, grad_mapped)
    grad_act = (
        grad_y * skip_weight
        + state_input * delta
        + dot_nt(grad_mapped, xproj_weight).reshape(steps, lines, inner)
    )
    grad_pre_act = grad_act * silu_slope(pre_act)
    grad_conv_b = jnp.sum(grad_pre_act, axis=(0, 1))
    grad_conv_w = jnp.stack([jnp.sum(grad_pre_act * tapped(k), axis=(0, 1)) for k in range(taps)])
    rims = sum(
        jnp.pad(
            (grad_pre_act[: rim - k] * taps_full[k] * valid[k][: rim - k]),
            ((k, 0), (0, 0), (0, 0)),
        )
        for k in range(rim)
    )
    next_rims = shifted(rims[:, :seqs], "seq", -1)
    after = jnp.concatenate([rims[:, seqs:], next_rims], axis=1)
    grad_conv_in = sum(
        jnp.pad(
            (grad_pre_act * taps_full[k] * valid[k])[rim - k :],
            ((0, rim - k), (0, 0), (0, 0)),
        )
        for k in range(taps)
    ) + jnp.pad(after, ((steps - rim, 0), (0, 0), (0, 0)))
    grad_conv_low = grad_conv_in.astype(bf16)
    grad_in_conv = dot_tn(normed_one, grad_conv_low.reshape(steps * lines, inner))

    def natural(x):
        return unlaid(x).reshape(seqs * group, inner)

    normed_part = dot_nt(natural(grad_conv_low), conv_w_in) + dot_nt(natural(grad_z), gate_w_in)
    normed_part = normed_part.astype(bf16).reshape(n_chan, owned, width)
    grad_normed_one = jnp.sum(exchange(normed_part, "chan", False, 11).astype(f32), axis=0)
    grad_gain_one = jnp.sum(grad_normed_one * unit_one, axis=0)
    grad_own = grad_hidden_one + norm_back(grad_normed_one, unit_one, inverse_one, gain_one)
    grad_tokens = exchange(grad_own.astype(bf16), "chan", True, 12)
    layer_out = exchange(layer_low, "chan", True, 13)

    summed_out, summed_gate = lax.psum((grad_out_w.astype(bf16), grad_in_gate.astype(bf16)), "seq")
    summed_conv, summed_xproj, summed_dt = lax.psum(
        (grad_in_conv.astype(bf16), grad_xproj.astype(bf16), grad_dt_w.astype(bf16)), "seq"
    )
    small = lax.psum(
        (grad_conv_w, grad_conv_b, grad_dt_bias, grad_a_log, grad_skip), "seq"
    )
    tiny = lax.psum((grad_gain_one, grad_gain_two, grad_router, loss_part), ("seq", "chan"))
    return (
        layer_out.reshape(seqs, group, width),
        tiny[3],
        grad_tokens.reshape(seqs, group, width).astype(f32),
        tiny[0],
        jnp.stack([summed_conv.astype(f32), summed_gate.astype(f32)], axis=1),
        small[0],
        small[1],
        summed_xproj.astype(f32),
        summed_dt.astype(f32),
        small[2],
        small[3],
        small[4],
        summed_out.astype(f32),
        tiny[1],
        tiny[2],
        grad_first[None],
        grad_second[None],
    )


def solution(mesh):
    placed = (
        P(None, "seq", None),
        P(None, "seq", None),
        P(),
        P(),
        P(None, "seq"),
        P(),
        P(None, None, "chan"),
        P(None, "chan"),
        P("chan"),
        P("chan", None),
        P(None, "chan"),
        P("chan"),
        P("chan", None),
        P("chan"),
        P("chan", None),
        P(),
        P(),
        P("seq", None, None),
        P("seq", None, None),
    )
    return jax.shard_map(
        local,
        mesh=mesh,
        in_specs=placed,
        out_specs=(
            P(None, "seq", None),
            P(),
            P(None, "seq", None),
            P(),
            P(None, None, "chan"),
            P(None, "chan"),
            P("chan"),
            P("chan", None),
            P(None, "chan"),
            P("chan"),
            P("chan", None),
            P("chan"),
            P("chan", None),
            P(),
            P(),
            P("seq", None, "chan"),
            P("seq", "chan", None),
        ),
        check_vma=False,
    )
```

profile of v0, /device:TPU:0, one launch (start us, length us, event | category | flops | bytes accessed | tf_op | source)
XLA Modules:
  0.0 615.1 jit_solution(1398007859284257340)
XLA Ops:
  55.6 7.7 %shard_map.314 = bf16[4,512,104]{2,1,0:T(8,128)(2,1)S(1)} custom-call(bf16[512,104]{1,0:T(8,128)(2,1)S(1)} %copy.159.x_ref), custom_call_target="tpu_custom_call" | custom-call | tf_op jit(solution)/shard_map/pallas_call | solution.py:52
  71.6 14.3 %shard_map.315 = (f32[16,8,576]{2,1,0:T(8,128)}, f32[8,576]{1,0:T(8,128)}) custom-call(f32[64,8,576]{2,1,0:T(8,128)} %get-tuple-element.89.delta_ref, f32[64,8,576]{2,1,0:T(8,128)} %get-tuple-element.88.drive_ref, f32[64,8,104]{2,1,0:T(8,128)} %bitcast.269, f32[16,576]{1,0:T(8,128)} %multiply_bitcast_fusion.rate_ref), custom_call_target="tpu_custom_call" | custom-call | flops 23592960 | bytes 2359296 | tf_op jit(solution)/shard_map/pallas_call | solution.py:364
  87.6 10.9 %shard_map.316.enter_ref.first_ref = f32[16,8,576]{2,1,0:T(8,128)S(1)} custom-call(f32[16,8,576]{2,1,0:T(8,128)S(1)} %copy-done.6, f32[8,576]{1,0:T(8,128)S(1)} %copy-done.8, f32[16,576]{1,0:T(8,128)S(1)} %copy-done.4), custom_call_target="tpu_custom_call" | custom-call | tf_op jit(solution)/shard_map/pallas_call | solution.py:186
  99.2 24.6 %shard_map.317 = (f32[64,8,576]{2,1,0:T(8,128)}, f32[64,16,8,576]{3,2,1,0:T(8,128)}) custom-call(f32[64,8,576]{2,1,0:T(8,128)} %get-tuple-element.89.delta_ref, f32[64,8,576]{2,1,0:T(8,128)} %get-tuple-element.88.drive_ref, f32[64,8,104]{2,1,0:T(8,128)} %bitcast.270, f32[16,576]{1,0:T(8,128)} %multiply_bitcast_fusion.rate_ref, f32[16,8,576]{2,1,0:T(8,128)} %copy-done.2), custom_call_target="tpu_custom_call" | custom-call | flops 33030144 | bytes 18874368 | tf_op jit(solution)/shard_map/pallas_call | solution.py:364
  129.9 14.3 %shard_map.318 = bf16[4,128,1152]{2,1,0:T(8,128)(2,1)S(1)} custom-call(bf16[4,128,1152]{2,1,0:T(8,128)(2,1)S(1)} %bitcast.256), custom_call_target="tpu_custom_call" | custom-call | tf_op jit(solution)/shard_map/pallas_call | solution.py:52
  147.0 19.8 %shard_map.319 = bf16[8,32,1152]{2,1,0:T(8,128)(2,1)S(1)} custom-call(bf16[8,32,1152]{2,1,0:T(8,128)(2,1)S(1)} %bitcast.254), custom_call_target="tpu_custom_call" | custom-call | tf_op jit(solution)/shard_map/pallas_call | solution.py:52
  173.8 16.8 %shard_map.320 = bf16[8,32,1152]{2,1,0:T(8,128)(2,1)S(1)} custom-call(bf16[8,32,1152]{2,1,0:T(8,128)(2,1)S(1)} %bitcast.262), custom_call_target="tpu_custom_call" | custom-call | tf_op jit(solution)/shard_map/pallas_call | solution.py:52
  192.1 16.8 %shard_map.322 = bf16[8,32,1152]{2,1,0:T(8,128)(2,1)} custom-call(bf16[8,32,1152]{2,1,0:T(8,128)(2,1)S(1)} %bitcast.253), custom_call_target="tpu_custom_call" | custom-call | tf_op jit(solution)/shard_map/pallas_call | solution.py:52
  215.5 16.4 %shard_map.323 = bf16[8,32,1152]{2,1,0:T(8,128)(2,1)S(1)} custom-call(bf16[8,32,1152]{2,1,0:T(8,128)(2,1)S(1)} %bitcast.263), custom_call_target="tpu_custom_call" | custom-call | tf_op jit(solution)/shard_map/pallas_call | solution.py:52
  234.3 13.6 %shard_map.324 = bf16[4,128,1152]{2,1,0:T(8,128)(2,1)S(1)} custom-call(bf16[128,1152]{1,0:T(8,128)(2,1)S(1)} %get-tuple-element.71.x_ref), custom_call_target="tpu_custom_call" | custom-call | tf_op jit(solution)/shard_map/pallas_call | solution.py:52
  253.1 5.8 multiply_reduce_fusion.1
  258.9 14.1 %shard_map.325.local_ref = f32[16,8,576]{2,1,0:T(8,128)} custom-call(f32[64,8,576]{2,1,0:T(8,128)} %get-tuple-element.89.delta_ref, f32[64,8,576]{2,1,0:T(8,128)} %get-tuple-element.68.grad_y_ref, f32[64,8,104]{2,1,0:T(8,128)} %bitcast.271, f32[16,576]{1,0:T(8,128)} %multiply_bitcast_fusion.rate_ref), custom_call_target="tpu_custom_call" | custom-call | flops 23592960 | bytes 2359296 | tf_op jit(solution)/shard_map/pallas_call | solution.py:364
  273.9 19.9 %shard_map.326.enter_ref = f32[16,8,576]{2,1,0:T(8,128)S(1)} custom-call(f32[16,8,576]{2,1,0:T(8,128)S(1)} %copy-done.7, f32[8,576]{1,0:T(8,128)S(1)} %copy-done.9, f32[16,576]{1,0:T(8,128)S(1)} %copy-done.5), custom_call_target="tpu_custom_call" | custom-call | tf_op jit(solution)/shard_map/pallas_call | solution.py:186
  294.6 42.4 %shard_map.327 = (f32[64,8,576]{2,1,0:T(8,128)}, f32[64,8,576]{2,1,0:T(8,128)}, f32[16,8,576]{2,1,0:T(8,128)}, f32[2,64,8,128]{3,2,1,0:T(8,128)}) custom-call(f32[64,8,576]{2,1,0:T(8,128)} %get-tuple-element.89.delta_ref, f32[64,8,576]{2,1,0:T(8,128)} %get-tuple-element.88.drive_ref, f32[64,8,576]{2,1,0:T(8,128)} %get-tuple-element.68.grad_y_ref, ...), custom_call_target="tpu_custom_call" | custom-call | flops 80216064 | bytes 18874368 | tf_op jit(solution)/shard_map/pallas_call | solution.py:364
  343.0 7.0 %shard_map.328 = bf16[4,512,104]{2,1,0:T(8,128)(2,1)S(1)} custom-call(bf16[512,104]{1,0:T(8,128)(2,1)S(1)} %pad_maximum_fusion.1.x_ref), custom_call_target="tpu_custom_call" | custom-call | tf_op jit(solution)/shard_map/pallas_call | solution.py:52
  350.8 5.3 fusion.59
  392.0 33.2 %shard_map.321 = bf16[4,128,1152]{2,1,0:T(8,128)(2,1)S(1)} custom-call(bf16[128,1152]{1,0:T(8,128)(2,1)S(1)} %get-tuple-element.91.x_ref), custom_call_target="tpu_custom_call" | custom-call | tf_op jit(solution)/shard_map/pallas_call | solution.py:52
  426.7 6.3 %constant_dynamic-slice_fusion.7 = (bf16[256,1,768]{2,1,0:T(2,128)(2,1)S(1)}, bf16[256,1,768]{2,1,0:T(2,128)(2,1)S(1)}, bf16[256,1,768]{2,1,0:T(2,128)(2,1)S(1)}, bf16[256,1,768]{2,1,0:T(2,128)(2,1)S(1)}) fusion(bf16[256,4,768]{2,1,0:T(4,128)(2,1)} %reshape.896, s32[]{:T(128)S(6)} %select_n.141, s32[]{:T(128)S(6)} %select_n.143, s32[]{:T(128)S(6)} %select_n.142, ...), kind=kLoop, calls=%fused_computation.267 | loop fusion | bytes 3145744 | tf_op jit(solution)/shard_map/dynamic-slice
  451.2 14.6 %shard_map.329 = bf16[4,128,1152]{2,1,0:T(8,128)(2,1)S(1)} custom-call(bf16[4,128,1152]{2,1,0:T(8,128)(2,1)S(1)} %bitcast.255), custom_call_target="tpu_custom_call" | custom-call | tf_op jit(solution)/shard_map/pallas_call | solution.py:52
  467.8 45.5 %all-reduce.6 = (f32[]{:T(128)}, f32[1152]{0:T(1024)}, f32[1152]{0:T(1024)}, f32[1152,8]{0,1:T(8,128)}) all-reduce(f32[]{:T(128)S(6)} %div.95, f32[1152]{0:T(1024)S(1)} %get-tuple-element.36, f32[1152]{0:T(1024)S(1)} %copy-done.76, f32[1152,8]{0,1:T(8,128)S(1)} %fusion.173), channel_id=1, replica_groups=mesh['seq'=8,'chan'=4] {'seq','chan'}, use_global_device_ids=true, to_apply=%region_10.11 | all-reduce | flops 11521 | bytes 92168 | tf_op jit(solution)/shard_map/psum | solution.py:731
  516.7 21.3 %shard_map.330 = bf16[4,128,1152]{2,1,0:T(8,128)(2,1)S(1)} custom-call(bf16[128,1152]{1,0:T(8,128)(2,1)S(1)} %fusion.115.x_ref), custom_call_target="tpu_custom_call" | custom-call | tf_op jit(solution)/shard_map/pallas_call | solution.py:52
  544.6 35.7 %all-reduce.7 = (f32[4,576]{1,0:T(4,128)}, f32[576]{0:T(1024)}, f32[576]{0:T(1024)}, f32[576,16]{0,1:T(8,128)}, f32[576]{0:T(1024)}) all-reduce(f32[4,576]{1,0:T(4,128)S(1)} %pad_maximum_fusion.2, f32[576]{0:T(1024)S(1)} %get-tuple-element.40, f32[576]{0:T(1024)S(1)} %copy-done.77, ...), channel_id=1, replica_groups=mesh['seq'=8,'chan'=4] {'seq'}, use_global_device_ids=true, to_apply=%region_25.26 | all-reduce | flops 13248 | bytes 105984 | tf_op jit(solution)/shard_map/psum | solution.py:728
  581.0 6.2 %convolution_bitcast_fusion = f32[1,768,1152]{2,1,0:T(8,128)} fusion(bf16[256,1152]{1,0:T(8,128)(2,1)} %collective-permute-done.13, bf16[256,1152]{1,0:T(8,128)(2,1)} %collective-permute-done.12, bf16[256,1152]{1,0:T(8,128)(2,1)} %collective-permute-done.11, bf16[256,1152]{1,0:T(8,128)(2,1)} %bitcast.30, bf16[256,768]{1,0:T(8,128)(2,1)} %collective-permute-done.10, ...), kind=kOutput, calls=%fused_computation.12 | convolution fusion | flops 1827667968 | bytes 7471104 | tf_op jit(solution)/shard_map/dot_general | solution.py:385
  587.1 5.3 collective-permute-done.6
  (408 shorter events, 179.9 us)
Async XLA Ops:
  7.2 121.6 %copy-start = (bf16[576,1152]{1,0:T(8,128)(2,1)S(1)}, bf16[576,1152]{1,0:T(8,128)(2,1)}, u32[]{:S(2)}) copy-start(bf16[576,1152]{1,0:T(8,128)(2,1)} %param.33) | copy-start | bytes 3981316
  7.2 590.5 %all-reduce.11.cloned.1.call-start = ((), (), s32[]{:S(2)}) async-start(), calls=%async_computation | async-start | bytes 8413184 | tf_op jit(solution)/shard_map/psum | solution.py:724
  8.9 40.8 %collective-permute-start = (bf16[4,3,1152]{2,1,0:T(4,128)(2,1)}, bf16[4,3,1152]{2,1,0:T(4,128)(2,1)S(1)}, u32[]{:S(2)}, u32[]{:S(2)}) collective-permute-start(bf16[4,3,1152]{2,1,0:T(4,128)(2,1)} %slice.108), channel_id=1, source_target_pairs={{0,4},{4,8},{8,12},{12,16},{16,20},{20,24},{24,28},{1,5},{5,9},{9,... | collective-permute-start | bytes 82952 | tf_op jit(solution)/shard_map/ppermute | solution.py:391
  146.5 85.7 %copy-start.64 = (f32[128,8]{0,1:T(8,128)}, f32[128,8]{0,1:T(8,128)S(1)}, u32[]{:S(2)}) copy-start(f32[128,8]{0,1:T(8,128)S(1)} %get-tuple-element.107) | copy-start | bytes 12292
  146.5 85.7 %copy-start.78 = (f32[128]{0:T(128)}, f32[128]{0:T(128)S(1)}, u32[]{:S(2)}) copy-start(f32[128]{0:T(128)S(1)} %get-tuple-element.106) | copy-start | bytes 1540
  146.6 85.6 %copy-start.83 = (f32[128]{0:T(128)}, f32[128]{0:T(128)S(1)}, u32[]{:S(2)}) copy-start(f32[128]{0:T(128)S(1)} %fusion.162) | copy-start | bytes 1540
  294.5 44.2 %copy-start.55 = (f32[576]{0:T(1024)S(1)}, f32[576]{0:T(1024)}, u32[]{:S(2)}) copy-start(f32[576]{0:T(1024)} %copy-done.54) | copy-start | bytes 6916
  294.5 44.2 %copy-start.57 = (f32[576]{0:T(1024)S(1)}, f32[576]{0:T(1024)}, u32[]{:S(2)}) copy-start(f32[576]{0:T(1024)} %copy-done.56) | copy-start | bytes 6916
  294.5 44.2 %copy-start.67 = (f32[576]{0:T(1024)S(1)}, f32[576]{0:T(1024)}, u32[]{:S(2)}) copy-start(f32[576]{0:T(1024)} %copy-done.66) | copy-start | bytes 6916
  294.6 44.2 %copy-start.71 = (f32[576]{0:T(1024)S(1)}, f32[576]{0:T(1024)}, u32[]{:S(2)}) copy-start(f32[576]{0:T(1024)} %copy-done.70) | copy-start | bytes 6916
  364.1 10.2 %collective-permute-start.1 = (f32[3,4,576]{2,1,0:T(4,128)S(1)}, f32[3,4,576]{2,1,0:T(4,128)S(1)}, u32[]{:S(2)}, u32[]{:S(2)}) collective-permute-start(f32[3,4,576]{2,1,0:T(4,128)S(1)} %get-tuple-element.93), channel_id=1, source_target_pairs={{4,0},{8,4},{12,8},{16,12},{20,16},{24,20},{28,24},{5,1},{9,5},{13... | collective-permute-start | bytes 82952 | tf_op jit(solution)/shard_map/ppermute | solution.py:391
  384.5 159.9 %collective-permute-start.13 = (bf16[256,1152]{1,0:T(8,128)(2,1)}, bf16[256,1152]{1,0:T(8,128)(2,1)}, u32[]{:S(2)}, u32[]{:S(2)}) collective-permute-start(bf16[256,1152]{1,0:T(8,128)(2,1)} %bitcast.30), channel_id=1, source_target_pairs={{0,3},{1,0},{2,1},{3,2},{4,7},{5,4},{6,5},{7,6},{8,11},{9,8},{10,9... | collective-permute-start | bytes 1769480 | tf_op jit(solution)/shard_map/ppermute | solution.py:397
  386.4 193.9 %collective-permute-start.12 = (bf16[256,1152]{1,0:T(8,128)(2,1)}, bf16[256,1152]{1,0:T(8,128)(2,1)}, u32[]{:S(2)}, u32[]{:S(2)}) collective-permute-start(bf16[256,1152]{1,0:T(8,128)(2,1)} %bitcast.30), channel_id=1, source_target_pairs={{0,2},{1,3},{2,0},{3,1},{4,6},{5,7},{6,4},{7,5},{8,10},{9,11},{10,... | collective-permute-start | bytes 1769480 | tf_op jit(solution)/shard_map/ppermute | solution.py:397
  387.7 193.3 %collective-permute-start.11 = (bf16[256,1152]{1,0:T(8,128)(2,1)}, bf16[256,1152]{1,0:T(8,128)(2,1)}, u32[]{:S(2)}, u32[]{:S(2)}) collective-permute-start(bf16[256,1152]{1,0:T(8,128)(2,1)} %bitcast.30), channel_id=1, source_target_pairs={{0,1},{1,2},{2,3},{3,0},{4,5},{5,6},{6,7},{7,4},{8,9},{9,10},{10,1... | collective-permute-start | bytes 1769480 | tf_op jit(solution)/shard_map/ppermute | solution.py:397
  433.9 79.4 %collective-permute-start.7 = (bf16[256,768]{1,0:T(8,128)(2,1)}, bf16[256,768]{1,0:T(8,128)(2,1)}, u32[]{:S(2)}, u32[]{:S(2)}) collective-permute-start(bf16[256,768]{1,0:T(8,128)(2,1)} %bitcast.246), channel_id=1, source_target_pairs={{0,3},{1,0},{2,1},{3,2},{4,7},{5,4},{6,5},{7,6},{8,11},{9,8},{10,9... | collective-permute-start | bytes 1179656 | tf_op jit(solution)/shard_map/ppermute | solution.py:407
  442.6 72.9 %collective-permute-start.10 = (bf16[256,768]{1,0:T(8,128)(2,1)}, bf16[256,768]{1,0:T(8,128)(2,1)}, u32[]{:S(2)}, u32[]{:S(2)}) collective-permute-start(bf16[256,768]{1,0:T(8,128)(2,1)} %bitcast.242), channel_id=1, source_target_pairs={{0,3},{1,0},{2,1},{3,2},{4,7},{5,4},{6,5},{7,6},{8,11},{9,8},{10,9... | collective-permute-start | bytes 1179656 | tf_op jit(solution)/shard_map/ppermute | solution.py:407
  465.9 49.6 %copy-start.20 = (f32[128,1152]{1,0:T(8,128)S(1)}, f32[128,1152]{1,0:T(8,128)}, u32[]{:S(2)}) copy-start(f32[128,1152]{1,0:T(8,128)} %get-tuple-element.72) | copy-start | bytes 1769476
  513.3 26.3 %collective-permute-start.9 = (bf16[256,768]{1,0:T(8,128)(2,1)}, bf16[256,768]{1,0:T(8,128)(2,1)S(1)}, u32[]{:S(2)}, u32[]{:S(2)}) collective-permute-start(bf16[256,768]{1,0:T(8,128)(2,1)} %bitcast.287), channel_id=1, source_target_pairs={{0,2},{1,3},{2,0},{3,1},{4,6},{5,7},{6,4},{7,5},{8,10},{9,11},{10,... | collective-permute-start | bytes 1179656 | tf_op jit(solution)/shard_map/ppermute | solution.py:407
  515.5 28.3 %collective-permute-start.8 = (bf16[256,768]{1,0:T(8,128)(2,1)}, bf16[256,768]{1,0:T(8,128)(2,1)S(1)}, u32[]{:S(2)}, u32[]{:S(2)}) collective-permute-start(bf16[256,768]{1,0:T(8,128)(2,1)} %bitcast.286), channel_id=1, source_target_pairs={{0,1},{1,2},{2,3},{3,0},{4,5},{5,6},{6,7},{7,4},{8,9},{9,10},{10,1... | collective-permute-start | bytes 1179656 | tf_op jit(solution)/shard_map/ppermute | solution.py:407
  539.7 52.8 %collective-permute-start.4 = (bf16[256,1152]{1,0:T(8,128)(2,1)S(1)}, bf16[256,1152]{1,0:T(8,128)(2,1)S(1)}, u32[]{:S(2)}, u32[]{:S(2)}) collective-permute-start(bf16[256,1152]{1,0:T(8,128)(2,1)S(1)} %bitcast.258), channel_id=1, source_target_pairs={{0,3},{1,0},{2,1},{3,2},{4,7},{5,4},{6,5},{7,6},{8,11},{9,8},{10,9... | collective-permute-start | bytes 1769480 | tf_op jit(solution)/shard_map/ppermute | solution.py:397
  543.8 48.7 %collective-permute-start.3 = (bf16[256,1152]{1,0:T(8,128)(2,1)S(1)}, bf16[256,1152]{1,0:T(8,128)(2,1)}, u32[]{:S(2)}, u32[]{:S(2)}) collective-permute-start(bf16[256,1152]{1,0:T(8,128)(2,1)S(1)} %bitcast.259), channel_id=1, source_target_pairs={{0,2},{1,3},{2,0},{3,1},{4,6},{5,7},{6,4},{7,5},{8,10},{9,11},{10,... | collective-permute-start | bytes 1769480 | tf_op jit(solution)/shard_map/ppermute | solution.py:397
  544.4 48.1 %collective-permute-start.2 = (bf16[256,1152]{1,0:T(8,128)(2,1)S(1)}, bf16[256,1152]{1,0:T(8,128)(2,1)}, u32[]{:S(2)}, u32[]{:S(2)}) collective-permute-start(bf16[256,1152]{1,0:T(8,128)(2,1)S(1)} %bitcast.260), channel_id=1, source_target_pairs={{0,1},{1,2},{2,3},{3,0},{4,5},{5,6},{6,7},{7,4},{8,9},{9,10},{10,1... | collective-permute-start | bytes 1769480 | tf_op jit(solution)/shard_map/ppermute | solution.py:397
  580.3 12.1 %collective-permute-start.6 = (bf16[256,768]{1,0:T(8,128)(2,1)}, bf16[256,768]{1,0:T(8,128)(2,1)S(1)}, u32[]{:S(2)}, u32[]{:S(2)}) collective-permute-start(bf16[256,768]{1,0:T(8,128)(2,1)} %bitcast.284), channel_id=1, source_target_pairs={{0,2},{1,3},{2,0},{3,1},{4,6},{5,7},{6,4},{7,5},{8,10},{9,11},{10,... | collective-permute-start | bytes 1179656 | tf_op jit(solution)/shard_map/ppermute | solution.py:407
  581.0 11.5 %collective-permute-start.5 = (bf16[256,768]{1,0:T(8,128)(2,1)}, bf16[256,768]{1,0:T(8,128)(2,1)S(1)}, u32[]{:S(2)}, u32[]{:S(2)}) collective-permute-start(bf16[256,768]{1,0:T(8,128)(2,1)} %bitcast.283), channel_id=1, source_target_pairs={{0,1},{1,2},{2,3},{3,0},{4,5},{5,6},{6,7},{7,4},{8,9},{9,10},{10,1... | collective-permute-start | bytes 1179656 | tf_op jit(solution)/shard_map/ppermute | solution.py:407
  (104 other events, 907.1 us)
Sparse Core Ops, SparseCore 0:
  379.2 158.7 all-reduce.10
where the time goes:
time: 625 us; the launch traced here: 615 us
  Pallas kernels  308 us (49%)
  blocking collectives  81.2 us (13%)
  local copies, waits for them, and re-layouts  69.2 us (11%)
  matrix products  64.4 us (10%)
  other arithmetic  50.3 us (8%)
  starting transfers between devices  19.4 us (3%)
  between operations  17.5 us (3%)
    pallas_call x11, Pallas kernels, exchange(): pl.pallas_call(functools.partial(exchange_kernel, axis, count, gather), o...  182 us
    pallas_call x4, Pallas kernels, scan_call(): pl.pallas_call(kernel, grid=(pl.cdiv(width, LANES),), in_specs=[whole(a.s...  95.4 us
    psum x1, blocking collectives, local(): lax.psum((grad_gain_one, grad_gain_two, grad_router, loss_part), ('seq',...  45.5 us
    psum x1, blocking collectives, local(): lax.psum((grad_conv_w, grad_conv_b, grad_dt_bias, grad_a_log, grad_skip),...  35.7 us
    pallas_call x2, Pallas kernels, carried(): pl.pallas_call(functools.partial(carry_kernel, axis, count, back), out_sh...  30.7 us
    dot_general x8, matrix products, dot_nt(): lax.dot_general(a, b, (((1,), (1,)), ((), ())), preferred_element_type=f32)  22.6 us
    dot_general x10, matrix products, dot_tn(): lax.dot_general(a, b, (((0,), (0,)), ((), ())), preferred_element_type=f32)  21.5 us
    dot_general x12, matrix products, dot(): return jnp.dot(a, b, preferred_element_type=f32)  20.2 us
  transfers between devices with their start and end apart: 15, of which 2 were waited for; matrix products, arithmetic and copies ran while one was open for 14% of the time, Pallas kernels for 11%

commit v1 on v0

--- a/solution.py
+++ b/solution.py
@@ -1,4 +1,5 @@
 import functools
+import math
 
 import jax
 import jax.numpy as jnp
@@ -17,47 +18,174 @@
 MIB = 1024 * 1024
 
 
-def exchange_kernel(axis, count, gather, x_ref, o_ref, own_sem, send_sem, recv_sem):
+def greet(axes):
+    barrier = pltpu.get_barrier_semaphore()
+    told = 0
+    for axis, count in axes:
+        me = lax.axis_index(axis)
+        for k in range(1, count):
+            pl.semaphore_signal(
+                barrier, inc=1, device_id={axis: lax.rem(me + k, count)}, device_id_type=MESH
+            )
+        told += count - 1
+    return told
+
+
+def sems_of(item):
+    count = item[2]
+    return [pltpu.SemaphoreType.DMA] + [pltpu.SemaphoreType.DMA((count - 1,))] * 2
+
+
+def begin(item, x_ref, o_ref, own_sem, send_sem, recv_sem):
+    mode, axis, count = item
     me = lax.axis_index(axis)
+
+    def remote(source, row, slot, to):
+        return pltpu.make_async_remote_copy(
+            src_ref=source,
+            dst_ref=o_ref.at[row],
+            send_sem=send_sem.at[slot],
+            recv_sem=recv_sem.at[slot],
+            device_id={axis: to},
+            device_id_type=MESH,
+        )
+
+    own = pltpu.make_async_copy(x_ref.at[me] if mode == "scatter" else x_ref, o_ref.at[me], own_sem)
+    copies, later = [], []
+    if mode == "relay":
+        beside = me + 1 - 2 * lax.rem(me, 2)
+        for k in range(1, count // 2):
+            first = remote(x_ref, me, k - 1, lax.rem(me + 2 * k, count))
+            row = lax.rem(me + count - 2 * k, count)
+            later.append((first, remote(o_ref.at[row], row, count // 2 - 1 + k, beside)))
+        copies.append(remote(x_ref, me, count // 2 - 1, beside))
+    else:
+        for k in range(1, count):
+            to = lax.rem(me + k, count)
+            copies.append(remote(x_ref.at[to] if mode == "scatter" else x_ref, me, k - 1, to))
+    for copy in [first for first, _ in later] + copies:
+        copy.start()
+    own.start()
+    return own, copies, later
+
+
+def finish(under_way):
+    for _, _, later in under_way:
+        for first, second in later:
+            first.wait_recv()
+            second.start()
+    for own, copies, later in under_way:
+        own.wait()
+        for copy in copies:
+            copy.wait()
+        for first, second in later:
+            first.wait_send()
+            second.wait()
+
+
+def items_of(exchanges):
+    return [(mode, axis, lax.axis_size(axis)) for _, mode, axis in exchanges]
+
+
+def axes_of(items):
+    return sorted({(axis, count) for _, axis, count in items})
+
+
+def landed(x, item):
+    shape = x.shape if item[0] == "scatter" else (item[2],) + x.shape
+    return jax.ShapeDtypeStruct(shape, x.dtype)
+
+
+def exchange_kernel(items, *refs):
+    number = len(items)
+    sems = refs[2 * number :]
+    pl.semaphore_wait(pltpu.get_barrier_semaphore(), greet(axes_of(items)))
+    finish(
+        [
+            begin(item, refs[i], refs[number + i], *sems[3 * i : 3 * i + 3])
+            for i, item in enumerate(items)
+        ]
+    )
+
+
+def exchange(number, *exchanges):
+    items = items_of(exchanges)
+    return pl.pallas_call(
+        functools.partial(exchange_kernel, items),
+        out_shape=[landed(x, item) for (x, _, _), item in zip(exchanges, items)],
+        in_specs=[pl.BlockSpec(memory_space=pl.ANY)] * len(items),
+        out_specs=[pl.BlockSpec(memory_space=pl.ANY)] * len(items),
+        scratch_shapes=[sem for item in items for sem in sems_of(item)],
+        compiler_params=pltpu.CompilerParams(
+            collective_id=number, has_side_effects=True, vmem_limit_bytes=16 * MIB
+        ),
+    )(*[x for x, _, _ in exchanges])
+
+
+def greet_near(axis, count):
     barrier = pltpu.get_barrier_semaphore()
-    for k in range(1, count):
+    me = lax.axis_index(axis)
+    beside = me + 1 - 2 * lax.rem(me, 2)
+    pl.semaphore_signal(barrier, inc=1, device_id={axis: beside}, device_id_type=MESH)
+    for k in range(1, count // 2):
         pl.semaphore_signal(
-            barrier, inc=1, device_id={axis: lax.rem(me + k, count)}, device_id_type=MESH
+            barrier, inc=1, device_id={axis: lax.rem(me + 2 * k, count)}, device_id_type=MESH
         )
-    own = pltpu.make_async_copy(x_ref if gather else x_ref.at[me], o_ref.at[me], own_sem)
-    own.start()
-    pl.semaphore_wait(barrier, count - 1)
+    pl.semaphore_wait(barrier, count // 2)
+
+
+def sum_kernel(axis, count, x_ref, o_ref, beside_in, pair, far_in, send_sem, recv_sem):
+    me = lax.axis_index(axis)
+    beside = me + 1 - 2 * lax.rem(me, 2)
+    greet_near(axis, count)
+    near = pltpu.make_async_remote_copy(
+        src_ref=x_ref,
+        dst_ref=beside_in,
+        send_sem=send_sem.at[0],
+        recv_sem=recv_sem.at[0],
+        device_id={axis: beside},
+        device_id_type=MESH,
+    )
+    near.start()
+    near.wait_recv()
+    pair[...] = (x_ref[...].astype(f32) + beside_in[...].astype(f32)).astype(bf16)
     copies = []
-    for k in range(1, count):
-        to = lax.rem(me + k, count)
+    for k in range(1, count // 2):
         copies.append(
             pltpu.make_async_remote_copy(
-                src_ref=x_ref if gather else x_ref.at[to],
-                dst_ref=o_ref.at[me],
-                send_sem=send_sem.at[k - 1],
-                recv_sem=recv_sem.at[k - 1],
-                device_id={axis: to},
+                src_ref=pair,
+                dst_ref=far_in.at[k - 1],
+                send_sem=send_sem.at[k],
+                recv_sem=recv_sem.at[k],
+                device_id={axis: lax.rem(me + 2 * k, count)},
                 device_id_type=MESH,
             )
         )
         copies[-1].start()
-    own.wait()
     for copy in copies:
-        copy.wait()
-
-
-def exchange(x, axis, gather, number):
+        copy.wait_recv()
+    total = pair[...].astype(f32)
+    for k in range(count // 2 - 1):
+        total = total + far_in[k].astype(f32)
+    o_ref[...] = total
+    near.wait_send()
+    for copy in copies:
+        copy.wait_send()
+
+
+def summed_over(x, axis, number):
     count = lax.axis_size(axis)
-    shape = (count,) + x.shape if gather else x.shape
     return pl.pallas_call(
-        functools.partial(exchange_kernel, axis, count, gather),
-        out_shape=jax.ShapeDtypeStruct(shape, x.dtype),
-        in_specs=[pl.BlockSpec(memory_space=pl.ANY)],
-        out_specs=pl.BlockSpec(memory_space=pl.ANY),
+        functools.partial(sum_kernel, axis, count),
+        out_shape=jax.ShapeDtypeStruct(x.shape, f32),
+        in_specs=[pl.BlockSpec(memory_space=pltpu.VMEM)],
+        out_specs=pl.BlockSpec(memory_space=pltpu.VMEM),
         scratch_shapes=[
-            pltpu.SemaphoreType.DMA,
-            pltpu.SemaphoreType.DMA((count - 1,)),
-            pltpu.SemaphoreType.DMA((count - 1,)),
+            pltpu.VMEM(x.shape, bf16),
+            pltpu.VMEM(x.shape, bf16),
+            pltpu.VMEM((count // 2 - 1,) + x.shape, bf16),
+            pltpu.SemaphoreType.DMA((count // 2,)),
+            pltpu.SemaphoreType.DMA((count // 2,)),
         ],
         compiler_params=pltpu.CompilerParams(
             collective_id=number, has_side_effects=True, vmem_limit_bytes=16 * MIB
@@ -65,12 +193,104 @@
     )(x)
 
 
+def share_kernel(axis, count, items, *refs):
+    number = len(items)
+    x_ref, xs = refs[0], refs[1 : 1 + number]
+    o_ref, outs = refs[1 + number], refs[2 + number : 2 + 2 * number]
+    near_in, pairs, far_in, near_send, near_recv, far_send, far_recv = refs[2 + 2 * number : 9 + 2 * number]
+    sems = refs[9 + 2 * number :]
+    me = lax.axis_index(axis)
+    half = count // 2
+    side, place = lax.rem(me, 2), me // 2
+    beside = me + 1 - 2 * side
+    if items:
+        pl.semaphore_wait(
+            pltpu.get_barrier_semaphore(), greet(sorted(set(axes_of(items)) | {(axis, count)}))
+        )
+    else:
+        greet_near(axis, count)
+    near = []
+    for k in range(half):
+        to = lax.rem(place + k + 1, half)
+        near.append(
+            pltpu.make_async_remote_copy(
+                src_ref=x_ref.at[2 * to + 1 - side],
+                dst_ref=near_in.at[k],
+                send_sem=near_send.at[k],
+                recv_sem=near_recv.at[k],
+                device_id={axis: beside},
+                device_id_type=MESH,
+            )
+        )
+        near[-1].start()
+    under_way = [
+        begin(item, xs[i], outs[i], *sems[3 * i : 3 * i + 3]) for i, item in enumerate(items)
+    ]
+    far = []
+    for k in range(half - 1):
+        to = 2 * lax.rem(place + k + 1, half) + side
+        near[k].wait_recv()
+        pairs[k] = (x_ref[to].astype(f32) + near_in[k].astype(f32)).astype(bf16)
+        far.append(
+            pltpu.make_async_remote_copy(
+                src_ref=pairs.at[k],
+                dst_ref=far_in.at[k],
+                send_sem=far_send.at[k],
+                recv_sem=far_recv.at[k],
+                device_id={axis: to},
+                device_id_type=MESH,
+            )
+        )
+        far[-1].start()
+    near[half - 1].wait_recv()
+    total = x_ref[me].astype(f32) + near_in[half - 1].astype(f32)
+    for k, copy in enumerate(far):
+        copy.wait_recv()
+        total = total + far_in[k].astype(f32)
+    o_ref[...] = total
+    for copy in near + far:
+        copy.wait_send()
+    finish(under_way)
+
+
+def share_of(x, axis, number, *exchanges):
+    count = lax.axis_size(axis)
+    items = items_of(exchanges)
+    part = x.shape[1:]
+    anywhere = [pl.BlockSpec(memory_space=pl.ANY)] * len(items)
+    return pl.pallas_call(
+        functools.partial(share_kernel, axis, count, items),
+        out_shape=[jax.ShapeDtypeStruct(part, f32)]
+        + [landed(x, item) for (x, _, _), item in zip(exchanges, items)],
+        in_specs=[pl.BlockSpec(memory_space=pltpu.VMEM)] + anywhere,
+        out_specs=[pl.BlockSpec(memory_space=pltpu.VMEM)] + anywhere,
+        scratch_shapes=[
+            pltpu.VMEM((count // 2,) + part, bf16),
+            pltpu.VMEM((count // 2 - 1,) + part, bf16),
+            pltpu.VMEM((count // 2 - 1,) + part, bf16),
+            pltpu.SemaphoreType.DMA((count // 2,)),
+            pltpu.SemaphoreType.DMA((count // 2,)),
+            pltpu.SemaphoreType.DMA((count // 2 - 1,)),
+            pltpu.SemaphoreType.DMA((count // 2 - 1,)),
+        ]
+        + [sem for item in items for sem in sems_of(item)],
+        compiler_params=pltpu.CompilerParams(
+            collective_id=number, has_side_effects=True, vmem_limit_bytes=24 * MIB
+        ),
+    )(x, *[x for x, _, _ in exchanges])
+
+
 def turned(value):
     return pltpu.roll(value, value.shape[0] // 2, 0)
 
 
-def carry_kernel(axis, count, back, local_ref, sums_ref, rate_ref, o_ref, send, got, send_sum, got_sum, total, enter,
-                 send_sem, recv_sem, send_sum_sem, recv_sum_sem):
+def carry_kernel(axis, count, back, items, *refs):
+    number = len(items)
+    local_ref, sums_ref, rate_ref = refs[:3]
+    xs, o_ref, outs = refs[3 : 3 + number], refs[3 + number], refs[4 + number : 4 + 2 * number]
+    send, got, send_sum, got_sum, total, enter = refs[4 + 2 * number : 10 + 2 * number]
+    send_sem, recv_sem, send_sum_sem, recv_sum_sem = refs[10 + 2 * number : 14 + 2 * number]
+    sems = refs[14 + 2 * number :]
     me = lax.axis_index(axis)
     states, rows, width = local_ref.shape
     half = rows // 2
@@ -81,7 +301,7 @@
         span *= 2
     sign = -1 if back else 1
     barrier = pltpu.get_barrier_semaphore()
-    greeted = 0
+    greeted = greet(axes_of(items))
     for span in spans:
         for by in (span, -span):
             there = me + by
@@ -109,12 +329,14 @@
         return (high, low) if back else (low, high)
 
     for j in range(states // 2):
-        begin, end = both(j)
-        total[j] = jnp.exp2(packed_rate(j) * sums_last) * begin + end
+        opening, closing = both(j)
+        total[j] = jnp.exp2(packed_rate(j) * sums_last) * opening + closing
         enter[j] = jnp.zeros((rows, width), f32)
 
     pl.semaphore_wait(barrier, greeted)
-
+    under_way = [
+        begin(item, xs[i], outs[i], *sems[3 * i : 3 * i + 3]) for i, item in enumerate(items)
+    ]
     sums_total = sums_both
     sums_enter = jnp.zeros((rows, width), f32)
     for turn, span in enumerate(spans):
@@ -171,23 +393,27 @@
                 copy.wait_send()
 
     for j in range(states // 2):
-        begin, _ = both(j)
+        opening, _ = both(j)
         outer = enter[j]
-        inner = jnp.exp2(packed_rate(j) * sums_first) * outer + begin
+        inner = jnp.exp2(packed_rate(j) * sums_first) * outer + opening
         low, high = (inner, outer) if back else (outer, inner)
         o_ref[2 * j] = jnp.where(upper, turned(high), low)
         o_ref[2 * j + 1] = jnp.where(upper, high, turned(low))
-
-
-def carried(local, sums, rate, axis, back, number):
+    finish(under_way)
+
+
+def carried(local, sums, rate, axis, back, number, *exchanges):
     count = lax.axis_size(axis)
     states, rows, width = local.shape
     turns = max(1, (count - 1).bit_length())
+    items = items_of(exchanges)
+    anywhere = [pl.BlockSpec(memory_space=pl.ANY)] * len(items)
     return pl.pallas_call(
-        functools.partial(carry_kernel, axis, count, back),
-        out_shape=jax.ShapeDtypeStruct(local.shape, f32),
-        in_specs=[pl.BlockSpec(memory_space=pltpu.VMEM)] * 3,
-        out_specs=pl.BlockSpec(memory_space=pltpu.VMEM),
+        functools.partial(carry_kernel, axis, count, back, items),
+        out_shape=[jax.ShapeDtypeStruct(local.shape, f32)]
+        + [landed(x, item) for (x, _, _), item in zip(exchanges, items)],
+        in_specs=[pl.BlockSpec(memory_space=pltpu.VMEM)] * 3 + anywhere,
+        out_specs=[pl.BlockSpec(memory_space=pltpu.VMEM)] + anywhere,
         scratch_shapes=[
             pltpu.VMEM((turns, states // 2 * rows, width), bf16),
             pltpu.VMEM((turns, states // 2 * rows, width), bf16),
@@ -199,23 +425,21 @@
             pltpu.SemaphoreType.DMA((turns,)),
             pltpu.SemaphoreType.DMA((turns,)),
             pltpu.SemaphoreType.DMA((turns,)),
-        ],
+        ]
+        + [sem for item in items for sem in sems_of(item)],
         compiler_params=pltpu.CompilerParams(
             collective_id=number, has_side_effects=True, vmem_limit_bytes=24 * MIB
         ),
-    )(local, sums, rate)
+    )(local, sums, rate, *[x for x, _, _ in exchanges])
 
 
 def spread(mapped_ref, first, wide_ref):
-    steps, count, rows, lanes = wide_ref.shape
-
-    def one(p, _):
-        values = mapped_ref[p]
-        for n in range(count):
-            wide_ref[p, n] = jnp.broadcast_to(values[:, first + n : first + n + 1], (rows, lanes))
-        return 0
-
-    lax.fori_loop(0, steps, one, 0)
+    count, steps, rows, lanes = wide_ref.shape
+    column = lax.broadcasted_iota(jnp.int32, (mapped_ref.shape[1], lanes), 0)
+    values = mapped_ref[...]
+    for n in range(count):
+        pick = (column == first + n).astype(bf16)
+        wide_ref[n] = jnp.dot(values, pick, preferred_element_type=f32).reshape(steps, rows, lanes)
 
 
 def rows_of(rate_ref, n, rows):
@@ -223,7 +447,7 @@
 
 
 def totals_kernel(rank, delta_ref, drive_ref, mapped_ref, rate_ref, last_ref, sums_ref, wide):
-    steps, count, rows, lanes = wide.shape
+    count, steps, rows, lanes = wide.shape
 
     @pl.when(pl.program_id(0) == 0)
     def _():
@@ -236,7 +460,7 @@
         states, sums = held
         step, drive = delta_ref[p], drive_ref[p]
         states = tuple(
-            jnp.exp2(step * rates[n]) * states[n] + drive * wide[p, n] for n in range(count)
+            jnp.exp2(step * rates[n]) * states[n] + drive * wide[n, p] for n in range(count)
         )
         return states, sums + step
 
@@ -247,7 +471,7 @@
 
 
 def states_kernel(rank, delta_ref, drive_ref, mapped_ref, rate_ref, enter_ref, y_ref, state_ref, wide_in, wide_read):
-    steps, count, rows, lanes = wide_in.shape
+    count, steps, rows, lanes = wide_in.shape
 
     @pl.when(pl.program_id(0) == 0)
     def _():
@@ -259,9 +483,9 @@
     def one(p, states):
         step, drive = delta_ref[p], drive_ref[p]
         states = tuple(
-            jnp.exp2(step * rates[n]) * states[n] + drive * wide_in[p, n] for n in range(count)
+            jnp.exp2(step * rates[n]) * states[n] + drive * wide_in[n, p] for n in range(count)
         )
-        terms = [states[n] * wide_read[p, n] for n in range(count)]
+        terms = [states[n] * wide_read[n, p] for n in range(count)]
         while len(terms) > 1:
             terms = [a + b for a, b in zip(terms[::2], terms[1::2])]
         y_ref[p] = terms[0]
@@ -273,7 +497,7 @@
 
 
 def back_totals_kernel(rank, delta_ref, grad_y_ref, mapped_ref, rate_ref, last_ref, wide):
-    steps, count, rows, lanes = wide.shape
+    count, steps, rows, lanes = wide.shape
 
     @pl.when(pl.program_id(0) == 0)
     def _():
@@ -286,7 +510,7 @@
         p = steps - 1 - turn
         step, grad_y = delta_ref[p], grad_y_ref[p]
         return tuple(
-            jnp.exp2(step * rates[n]) * (held[n] + grad_y * wide[p, n]) for n in range(count)
+            jnp.exp2(step * rates[n]) * (held[n] + grad_y * wide[n, p]) for n in range(count)
         )
 
     held = lax.fori_loop(0, steps, one, (zero,) * count)
@@ -296,7 +520,7 @@
 
 def back_kernel(rank, width, delta_ref, drive_ref, grad_y_ref, mapped_ref, rate_ref, first_ref, state_ref, enter_ref,
                 input_ref, decay_ref, log_ref, maps_ref, wide_in, wide_read, sum_in, sum_read):
-    steps, count, rows, lanes = wide_in.shape
+    count, steps, rows, lanes = wide_in.shape
     place = pl.program_id(0)
 
     @pl.when(place == 0)
@@ -319,14 +543,14 @@
         to_decay = jnp.zeros((rows, lanes), f32)
         new = []
         for n in range(count):
-            grad = grad_y * wide_read[p, n] + carry[n]
+            grad = grad_y * wide_read[n, p] + carry[n]
             passed = jnp.exp2(step * rates[n]) * grad
             new.append(passed)
             prior = jnp.where(opening, first_ref[n], state_ref[before, n])
             grad_decay = passed * prior
             to_decay = to_decay + grad_decay * rates[n]
             log_ref[n] += grad_decay * step
-            to_input = to_input + grad * wide_in[p, n]
+            to_input = to_input + grad * wide_in[n, p]
             part_in = jnp.where(held, grad * drive, 0.0)
             part_read = jnp.where(held, grad_y * state_ref[p, n], 0.0)
             sum_in[p, n] = jnp.where(fresh, 0.0, sum_in[p, n]) + part_in
@@ -391,21 +615,25 @@
     return lax.ppermute(x, axis, pairs)
 
 
-def turns_of(x, axis):
-    count = lax.axis_size(axis)
-    return [
-        lax.ppermute(x, axis, [(i, (i + k) % count) for i in range(count)]) for k in range(1, count)
-    ]
-
-
-def turned_parts(x, axis):
-    count = lax.axis_size(axis)
-    me = lax.axis_index(axis)
-    parts = [lax.dynamic_index_in_dim(x, me, 0, False)]
-    for k in range(1, count):
-        mine = lax.dynamic_index_in_dim(x, lax.rem(me + k, count), 0, False)
-        parts.append(lax.ppermute(mine, axis, [(i, (i + k) % count) for i in range(count)]))
-    return parts
+def packed_size(arrays, rows):
+    total = -(-sum(a.size for a in arrays) // LANES)
+    return -(-total // rows) * rows
+
+
+def packed_rows(arrays, rows):
+    total = packed_size(arrays, rows)
+    joined = jnp.concatenate([a.reshape(-1) for a in arrays])
+    return jnp.pad(joined, (0, total * LANES - joined.size)).reshape(total, LANES)
+
+
+def unpacked_rows(packed, shapes):
+    packed = packed.reshape(-1)
+    arrays, at = [], 0
+    for shape in shapes:
+        size = math.prod(shape)
+        arrays.append(packed[at : at + size].reshape(shape))
+        at += size
+    return arrays
 
 
 def silu_slope(values):
@@ -510,9 +738,9 @@
     act = pre_act * jax.nn.sigmoid(pre_act)
     act_low = act.astype(bf16).reshape(steps * lines, inner)
     mapped_part = dot(act_low, xproj_weight).astype(bf16)
-    mapped = jnp.sum(exchange(mapped_part, "chan", True, 1).astype(f32), axis=0)
+    mapped = summed_over(mapped_part, "chan", 1)
     dt_low = mapped[:, :rank].astype(bf16)
-    mapped_laid = mapped.reshape(steps, lines, rank + 2 * states)
+    mapped_low = mapped.astype(bf16)
     dt_pre = (dot(dt_low, dt_weight) + dt_bias).reshape(steps, lines, inner)
     delta = jax.nn.softplus(dt_pre)
     rate = -jnp.exp(a_log).T
@@ -520,37 +748,35 @@
     step_size = jnp.where(keep[..., None], delta, cut)
     drive = delta * act
 
-    flat = steps * lines * states * inner
-    wide_shape = (steps, states, lines, LANES)
+    work = steps * lines * states * inner
+    wide_shape = (states, steps, lines, LANES)
     last, sums = scan_call(
         functools.partial(totals_kernel, rank),
-        [(step_size, False), (drive, False), (mapped_laid, True), (rate_two, False)],
+        [(step_size, False), (drive, False), (mapped_low, True), (rate_two, False)],
         [((states, lines, inner), False), ((lines, inner), False)],
         [wide_shape],
-        pl.CostEstimate(flops=5 * flat, bytes_accessed=8 * steps * lines * inner, transcendentals=flat),
-    )
-    enter = carried(last, sums, rate_two, "seq", False, 2)
+        pl.CostEstimate(flops=5 * work, bytes_accessed=8 * steps * lines * inner, transcendentals=work),
+    )
+    (enter,) = carried(last, sums, rate_two, "seq", False, 2)
     y_scan, state = scan_call(
         functools.partial(states_kernel, rank),
         [
             (step_size, False),
             (drive, False),
-            (mapped_laid, True),
+            (mapped_low, True),
             (rate_two, False),
             (enter, False),
         ],
         [((steps, lines, inner), False), ((steps, states, lines, inner), False)],
         [wide_shape] * 2,
-        pl.CostEstimate(flops=7 * flat, bytes_accessed=4 * flat, transcendentals=flat),
+        pl.CostEstimate(flops=7 * work, bytes_accessed=4 * work, transcendentals=work),
     )
     y_full = y_scan + skip_weight * act
     silu_z = gate_z * jax.nn.sigmoid(gate_z)
     gated = (y_full * silu_z).astype(bf16)
     gated_rows = gated.reshape(steps * lines, inner)
     out_part = dot(unlaid(gated).reshape(seqs * group, inner), out_weight).astype(bf16)
-    mixed = jnp.sum(
-        exchange(out_part.reshape(n_chan, owned, width), "chan", False, 3).astype(f32), axis=0
-    )
+    (mixed,) = share_of(out_part.reshape(n_chan, owned, width), "chan", 3)
 
     def own(x):
         rows = x.reshape((seqs * group,) + x.shape[2:])
@@ -579,25 +805,30 @@
     hit_send = hit.reshape(owned, experts * slots)
     hit_back = jnp.repeat(hit, shards, axis=1).reshape(owned, n_seq * slots)
 
-    def to_slabs(rows, number):
+    def to_slabs(rows):
         packed = dot_tn(hit_send, rows).astype(bf16).reshape(experts, slots, width)
-        came = exchange(jnp.repeat(packed, shards, axis=0), "seq", False, number)
-        return came.reshape(n_seq * slots, width)
-
-    def from_slabs(rows, number):
-        came = exchange(rows.reshape(n_seq, slots, width), "seq", False, number)
-        return dot(hit_back, came.reshape(n_seq * slots, width))
+        return jnp.repeat(packed, shards, axis=0), "scatter", "seq"
+
+    def to_rows(x):
+        return x.reshape(n_seq, slots, width), "scatter", "seq"
+
+    def by_units(x):
+        return x.reshape(n_seq * slots, n_chan, units).transpose(1, 0, 2), "scatter", "chan"
+
+    def flat(x):
+        return x.reshape(-1, x.shape[-1])
 
     first_slab, second_slab = expert_in[0], expert_out[0]
     units = first_slab.shape[1] // n_chan
-    arrived = to_slabs(normed_two, 4)
+    arrived = flat(exchange(4, to_slabs(normed_two))[0])
     pre_hidden = dot(arrived, first_slab)
     cdf = 0.5 * (1.0 + lax.erf(pre_hidden * 0.7071067811865476))
     hidden_low = (pre_hidden * cdf).astype(bf16)
     density = jnp.exp(-0.5 * pre_hidden * pre_hidden) * 0.3989422804014327
     slope = cdf + pre_hidden * density
     result = dot(hidden_low, second_slab).astype(bf16)
-    expert_total = from_slabs(result, 5)
+    result_rows, rows_all = exchange(5, to_rows(result), (arrived, "relay", "chan"))
+    expert_total = dot(hit_back, flat(result_rows))
     layer = hidden_one + gate_value * expert_total
     layer_low = layer.astype(bf16)
 
@@ -613,20 +844,12 @@
     grad_layer = 2.0 / total_true * loss_mask * error
     grad_gate = jnp.sum(grad_layer * expert_total, axis=-1, keepdims=True)
     grad_result = (gate_value * grad_layer).astype(bf16)
-    grad_rows = to_slabs(grad_result, 6)
+    grad_rows, hidden_all = exchange(6, to_slabs(grad_result), by_units(hidden_low))
+    grad_rows = flat(grad_rows)
     grad_pre = (dot_nt(grad_rows, second_slab) * slope).astype(bf16)
     grad_slab_rows = dot_nt(grad_pre, first_slab).astype(bf16)
-    grad_expert = from_slabs(grad_slab_rows, 7)
-
-    def by_units(x):
-        return x.reshape(n_seq * slots, n_chan, units).transpose(1, 0, 2)
-
-    rows_all = jnp.concatenate([arrived] + turns_of(arrived, "chan"), axis=0)
-    hidden_all = jnp.concatenate(turned_parts(by_units(hidden_low), "chan"), axis=0)
-    grad_rows_all = jnp.concatenate([grad_rows] + turns_of(grad_rows, "chan"), axis=0)
-    grad_pre_all = jnp.concatenate(turned_parts(by_units(grad_pre), "chan"), axis=0)
-    grad_first = dot_tn(rows_all, grad_pre_all)
-    grad_second = dot_tn(hidden_all, grad_rows_all)
+    grad_expert, grad_rows_all = exchange(7, to_rows(grad_slab_rows), (grad_rows, "relay", "chan"))
+    grad_expert = dot(hit_back, flat(grad_expert))
 
     grad_logit = grad_gate * gate_value * (chosen_rows - probs)
     grad_router = dot_tn(normed_two, grad_logit.astype(bf16))
@@ -634,7 +857,11 @@
     grad_gain_two = jnp.sum(grad_normed_two * unit_two, axis=0)
     grad_hidden_one = grad_layer + norm_back(grad_normed_two, unit_two, inverse_two, gain_two)
 
-    grad_mixed = exchange(grad_hidden_one.astype(bf16), "chan", True, 8)
+    shared = packed_rows([grad_gain_two, grad_router, loss_part], 8)
+    grad_mixed, shared = exchange(
+        8, (grad_hidden_one.astype(bf16), "relay", "chan"), (shared, "gather", "chan")
+    )
+    shared = jnp.sum(shared, axis=0)
     grad_mixed = laid(grad_mixed.reshape(seqs, group, width)).reshape(steps * lines, width)
     grad_out_w = dot_tn(gated_rows, grad_mixed)
     grad_gated = dot_nt(grad_mixed, out_weight).reshape(steps, lines, inner)
@@ -642,22 +869,27 @@
     grad_z = (grad_gated * y_full * silu_slope(gate_z)).astype(bf16)
     grad_z_rows = grad_z.reshape(steps * lines, inner)
     grad_in_gate = dot_tn(normed_one, grad_z_rows)
+    summed_out, summed_gate = lax.psum((grad_out_w.astype(bf16), grad_in_gate.astype(bf16)), "seq")
     grad_skip = jnp.sum(grad_y * act, axis=(0, 1))
     (back_last,) = scan_call(
         functools.partial(back_totals_kernel, rank),
-        [(step_size, False), (grad_y, False), (mapped_laid, True), (rate_two, False)],
+        [(step_size, False), (grad_y, False), (mapped_low, True), (rate_two, False)],
         [((states, lines, inner), False)],
         [wide_shape],
-        pl.CostEstimate(flops=5 * flat, bytes_accessed=8 * steps * lines * inner, transcendentals=flat),
-    )
-    back_enter = carried(back_last, sums, rate_two, "seq", True, 9)
+        pl.CostEstimate(flops=5 * work, bytes_accessed=8 * steps * lines * inner, transcendentals=work),
+    )
+    back_enter, grad_pre_all = carried(
+        back_last, sums, rate_two, "seq", True, 9, by_units(grad_pre)
+    )
+    grad_first = dot_tn(flat(rows_all), flat(grad_pre_all))
+    grad_second = dot_tn(flat(hidden_all), flat(grad_rows_all))
     state_input, from_decay, log_sums, maps = scan_call(
         functools.partial(back_kernel, rank, inner),
         [
             (step_size, False),
             (drive, False),
             (grad_y, False),
-            (mapped_laid, True),
+            (mapped_low, True),
             (rate_two, False),
             (enter, False),
             (state, False),
@@ -669,8 +901,8 @@
             ((states, lines, inner), False),
             ((2, steps, 8, states * lines), True),
         ],
-        [wide_shape] * 4,
-        pl.CostEstimate(flops=17 * flat, bytes_accessed=4 * flat, transcendentals=flat),
+        [wide_shape] * 2 + [(steps, states, lines, LANES)] * 2,
+        pl.CostEstimate(flops=17 * work, bytes_accessed=4 * work, transcendentals=work),
     )
     grad_a_log = (jnp.sum(log_sums, axis=1) * rate).T
     grad_maps = maps[:, :, 0].reshape(2, steps, states, lines).transpose(1, 3, 0, 2)
@@ -681,8 +913,8 @@
     grad_dt_low = grad_dt_pre.astype(bf16).reshape(steps * lines, inner)
     grad_dt_w = dot_tn(dt_low, grad_dt_low)
     low_part = jnp.concatenate([dot_nt(grad_dt_low, dt_weight), grad_maps], axis=1).astype(bf16)
-    grad_mapped = jnp.sum(exchange(low_part, "chan", True, 10).astype(f32), axis=0).astype(bf16)
-    grad_xproj = dot_tn(act_low, grad_mapped)
+    grad_mapped = summed_over(low_part, "chan", 10).astype(bf16)
+    grad_xproj = dot_tn(grad_mapped, act_low)
     grad_act = (
         grad_y * skip_weight
         + state_input * delta
@@ -714,37 +946,65 @@
         return unlaid(x).reshape(seqs * group, inner)
 
     normed_part = dot_nt(natural(grad_conv_low), conv_w_in) + dot_nt(natural(grad_z), gate_w_in)
+    unit_all = tokens.reshape(seqs * group, width).astype(f32)
+    unit_all = unit_all * lax.rsqrt(jnp.mean(unit_all * unit_all, axis=-1, keepdims=True) + epsilon)
+    grad_gain_one = packed_rows([jnp.sum(normed_part * unit_all, axis=0)], 8)
     normed_part = normed_part.astype(bf16).reshape(n_chan, owned, width)
-    grad_normed_one = jnp.sum(exchange(normed_part, "chan", False, 11).astype(f32), axis=0)
-    grad_gain_one = jnp.sum(grad_normed_one * unit_one, axis=0)
+    large = jnp.concatenate([grad_in_conv, grad_xproj, grad_dt_w], axis=0).astype(bf16)
+    large_rows = large.shape[0]
+    each = -(-large_rows // (16 * n_seq)) * 16
+    large = jnp.pad(large, ((0, each * n_seq - large_rows), (0, 0))).reshape(n_seq, each, inner)
+    small = [grad_conv_w, grad_conv_b, grad_dt_bias, grad_a_log, grad_skip]
+    small_flat = jnp.concatenate([packed_rows(small, 1), shared], axis=0)
+    small_rows = small_flat.shape[0]
+    each_small = -(-small_rows // (8 * n_seq)) * 8
+    small_flat = jnp.pad(small_flat, ((0, each_small * n_seq - small_rows), (0, 0)))
+    small_flat = small_flat.reshape(n_seq, each_small, LANES)
+    grad_normed_one, large, small_flat, grad_gain_one = share_of(
+        normed_part,
+        "chan",
+        11,
+        (large, "scatter", "seq"),
+        (small_flat, "scatter", "seq"),
+        (grad_gain_one, "gather", "chan"),
+    )
+    large = jnp.sum(large.astype(f32), axis=0).astype(bf16)
+    small_flat = jnp.sum(small_flat, axis=0)
+    grad_gain_one = jnp.sum(grad_gain_one, axis=0)
     grad_own = grad_hidden_one + norm_back(grad_normed_one, unit_one, inverse_one, gain_one)
-    grad_tokens = exchange(grad_own.astype(bf16), "chan", True, 12)
-    layer_out = exchange(layer_low, "chan", True, 13)
-
-    summed_out, summed_gate = lax.psum((grad_out_w.astype(bf16), grad_in_gate.astype(bf16)), "seq")
-    summed_conv, summed_xproj, summed_dt = lax.psum(
-        (grad_in_conv.astype(bf16), grad_xproj.astype(bf16), grad_dt_w.astype(bf16)), "seq"
-    )
-    small = lax.psum(
-        (grad_conv_w, grad_conv_b, grad_dt_bias, grad_a_log, grad_skip), "seq"
-    )
-    tiny = lax.psum((grad_gain_one, grad_gain_two, grad_router, loss_part), ("seq", "chan"))
+    grad_tokens, layer_out, large, small_flat, grad_gain_one = exchange(
+        12,
+        (grad_own.astype(bf16), "relay", "chan"),
+        (layer_low, "relay", "chan"),
+        (large, "gather", "seq"),
+        (small_flat, "gather", "seq"),
+        (grad_gain_one, "gather", "seq"),
+    )
+    (grad_gain_one,) = unpacked_rows(jnp.sum(grad_gain_one, axis=0), [(width,)])
+    large = flat(large).astype(f32)
+    summed_conv, summed_xproj, summed_dt, _ = jnp.split(
+        large, [width, width + grad_xproj.shape[0], large_rows]
+    )
+    small_flat = flat(small_flat)
+    mid = packed_size(small, 1)
+    small = unpacked_rows(small_flat[:mid], [a.shape for a in small])
+    tiny = unpacked_rows(small_flat[mid:small_rows], [(width,), grad_router.shape, ()])
     return (
         layer_out.reshape(seqs, group, width),
-        tiny[3],
+        tiny[2],
         grad_tokens.reshape(seqs, group, width).astype(f32),
-        tiny[0],
-        jnp.stack([summed_conv.astype(f32), summed_gate.astype(f32)], axis=1),
+        grad_gain_one,
+        jnp.stack([summed_conv, summed_gate.astype(f32)], axis=1),
         small[0],
         small[1],
-        summed_xproj.astype(f32),
-        summed_dt.astype(f32),
+        summed_xproj.T,
+        summed_dt,
         small[2],
         small[3],
         small[4],
         summed_out.astype(f32),
+        tiny[0],
         tiny[1],
-        tiny[2],
         grad_first[None],
         grad_second[None],
     )

time: 625 us -> 571 us (0.914)
  blocking collectives: 81.2 us -> 0 us
  Pallas kernels: 308 us -> 339 us
  starting transfers between devices: 19.4 us -> 6.18 us
  matrix products: 64.4 us -> 73.1 us
  local copies, waits for them, and re-layouts: 69.2 us -> 76.8 us
    psum x2 -> x0, blocking collectives: 81.2 us -> none  [the longest x1 45.5 us: local(): lax.psum((grad_gain_one, grad_gain_two, grad_router, loss_part), ('seq',...]
    pallas_call x13 -> x12, Pallas kernels: 212 us -> 274 us  [the longest x6 166 us: exchange(): pl.pallas_call(functools.partial(exchange_kernel, items), out_shape=[land...]
    pallas_call x4, Pallas kernels: 95.4 us -> 65.4 us  [scan_call(): pl.pallas_call(kernel, grid=(pl.cdiv(width, LANES),), in_specs=[whole(a.s...]
    ppermute x12 -> x0, starting transfers between devices: 13.1 us -> none  [the longest x6 7.9 us: turns_of(): lax.ppermute(x, axis, [(i, (i + k) % count) for i in range(count)])]
    dot_general x12, matrix products: 20.2 us -> 28.7 us  [dot(): return jnp.dot(a, b, preferred_element_type=f32)]
    another operation x3, local copies, waits for them, and re-layouts: 9.73 us -> 1.7 us
    unnamed x235 -> x241, local copies, waits for them, and re-layouts: 17.3 us -> 23.9 us
  transfers between devices with their start and end apart: 15 -> 3, of which waited for: 2 -> 0; matrix products, arithmetic and copies ran while one was open for 14% -> 16% of each run, Pallas kernels for 11% -> 23%
where the time goes in v1:
time: 571 us; the launch traced here: 564 us
  Pallas kernels  339 us (59%)
  local copies, waits for them, and re-layouts  76.8 us (13%)
  matrix products  73.1 us (13%)
  other arithmetic  51.1 us (9%)
  between operations  17.6 us (3%)
  starting transfers between devices  6.18 us (1%)
    pallas_call x6, Pallas kernels, exchange(): pl.pallas_call(functools.partial(exchange_kernel, items), out_shape=[land...  166 us
    pallas_call x4, Pallas kernels, scan_call(): pl.pallas_call(kernel, grid=(pl.cdiv(width, LANES),), in_specs=[whole(a.s...  65.4 us
    pallas_call x2, Pallas kernels, share_of(): pl.pallas_call(functools.partial(share_kernel, axis, count, items), out_s...  63.6 us
    pallas_call x2, Pallas kernels, carried(): pl.pallas_call(functools.partial(carry_kernel, axis, count, back, items),...  29.6 us
    dot_general x12, matrix products, dot(): return jnp.dot(a, b, preferred_element_type=f32)  28.7 us
    unnamed x241, local copies, waits for them, and re-layouts  23.9 us
    dot_general x8, matrix products, dot_nt(): lax.dot_general(a, b, (((1,), (1,)), ((), ())), preferred_element_type=f32)  22.8 us
    dot_general x10, matrix products, dot_tn(): lax.dot_general(a, b, (((0,), (0,)), ((), ())), preferred_element_type=f32)  21.6 us
  transfers between devices with their start and end apart: 3, of which 0 were waited for; matrix products, arithmetic and copies ran while one was open for 16% of the time, Pallas kernels for 23%

profile of v1, /device:TPU:0, one launch (start us, length us, event | category | flops | bytes accessed | tf_op | source)
XLA Modules:
  0.0 564.2 jit_solution(2308171253091965644)
XLA Ops:
  8.9 4.9 collective-permute-start
  55.1 7.2 %shard_map.314 = f32[512,104]{1,0:T(8,128)S(1)} custom-call(bf16[512,104]{1,0:T(8,128)(2,1)S(1)} %copy.194.x_ref), custom_call_target="tpu_custom_call" | custom-call | tf_op jit(solution)/shard_map/pallas_call | solution.py:178
  70.4 8.9 %shard_map.315 = (f32[16,8,576]{2,1,0:T(8,128)}, f32[8,576]{1,0:T(8,128)}) custom-call(f32[64,8,576]{2,1,0:T(8,128)} %get-tuple-element.193.delta_ref, f32[64,8,576]{2,1,0:T(8,128)} %get-tuple-element.192.drive_ref, bf16[512,104]{1,0:T(8,128)(2,1)} %copy-done.44, f32[16,576]{1,0:T(8,128)} %multiply_bitcast_fusion.rate_ref.refs_2_), custom_call_target="tpu_custom_call" | custom-call | flops 23592960 | bytes 2359296 | tf_op jit(solution)/shard_map/pallas_call | solution.py:588
  81.1 10.5 %shard_map.316.enter_ref.first_ref = f32[16,8,576]{2,1,0:T(8,128)S(1)} custom-call(f32[16,8,576]{2,1,0:T(8,128)S(1)} %copy-done.12, f32[8,576]{1,0:T(8,128)S(1)} %copy-done.15, f32[16,576]{1,0:T(8,128)S(1)} %copy-done.7), custom_call_target="tpu_custom_call" | custom-call | tf_op jit(solution)/shard_map/pallas_call | solution.py:411
  92.3 14.6 %shard_map.317 = (f32[64,8,576]{2,1,0:T(8,128)}, f32[64,16,8,576]{3,2,1,0:T(8,128)}) custom-call(f32[64,8,576]{2,1,0:T(8,128)} %get-tuple-element.193.delta_ref, f32[64,8,576]{2,1,0:T(8,128)} %get-tuple-element.192.drive_ref, bf16[512,104]{1,0:T(8,128)(2,1)} %copy-done.44, f32[16,576]{1,0:T(8,128)} %multiply_bitcast_fusion.rate_ref.refs_2_, ...), custom_call_target="tpu_custom_call" | custom-call | flops 33030144 | bytes 18874368 | tf_op jit(solution)/shard_map/pallas_call | solution.py:588
  113.0 9.3 %shard_map.318 = f32[128,1152]{1,0:T(8,128)S(1)} custom-call(bf16[4,128,1152]{2,1,0:T(8,128)(2,1)S(1)} %bitcast.272), custom_call_target="tpu_custom_call" | custom-call | tf_op jit(solution)/shard_map/pallas_call | solution.py:261
  125.9 19.1 %shard_map.319 = bf16[8,32,1152]{2,1,0:T(8,128)(2,1)S(1)} custom-call(bf16[8,32,1152]{2,1,0:T(8,128)(2,1)S(1)} %bitcast.269), custom_call_target="tpu_custom_call" | custom-call | tf_op jit(solution)/shard_map/pallas_call | solution.py:113
  145.0 7.1 %multiply_convert_fusion = (bf16[256,3072]{1,0:T(8,128)(2,1)S(1)}, f32[256,3072]{1,0:T(8,128)}) fusion(bf16[256,1152]{1,0:T(8,128)(2,1)S(1)} %bitcast.266, bf16[1,1152,3072]{2,1,0:T(8,128)(2,1)} %param.36), kind=kOutput, calls=%fused_computation.22 | convolution fusion | flops 1815871488 | bytes 12386304 | tf_op jit(solution)/shard_map/dot_general | solution.py:601
  153.7 6.0 %fusion.24 = bf16[256,1152]{1,0:T(8,128)(2,1)} fusion(bf16[256,3072]{1,0:T(8,128)(2,1)S(1)} %get-tuple-element.212, bf16[1,3072,1152]{2,1,0:T(8,128)(2,1)} %param.37), kind=kOutput, calls=%fused_computation.30 | convolution fusion | flops 1812234240 | bytes 9240576 | tf_op jit(solution)/shard_map/dot_general | solution.py:601
  162.5 22.3 %shard_map.320 = (bf16[8,32,1152]{2,1,0:T(8,128)(2,1)S(1)}, bf16[4,256,1152]{2,1,0:T(8,128)(2,1)S(1)}) custom-call(bf16[8,32,1152]{2,1,0:T(8,128)(2,1)S(1)} %bitcast.276, bf16[256,1152]{1,0:T(8,128)(2,1)S(1)} %bitcast.267), custom_call_target="tpu_custom_call" | custom-call | tf_op jit(solution)/shard_map/pallas_call | solution.py:113
  188.5 20.0 %shard_map.321 = (bf16[8,32,1152]{2,1,0:T(8,128)(2,1)S(1)}, bf16[4,256,768]{2,1,0:T(8,128)(2,1)S(1)}) custom-call(bf16[8,32,1152]{2,1,0:T(8,128)(2,1)S(1)} %bitcast.268, bf16[4,256,768]{2,1,0:T(8,128)(2,1)S(1)} %bitcast.264), custom_call_target="tpu_custom_call" | custom-call | tf_op jit(solution)/shard_map/pallas_call | solution.py:113
  209.6 5.8 %fusion.11 = bf16[256,3072]{1,0:T(8,128)(2,1)S(1)} fusion(bf16[256,1152]{1,0:T(8,128)(2,1)S(1)} %bitcast.273, bf16[1,3072,1152]{2,1,0:T(8,128)(2,1)} %param.37, f32[256,3072]{1,0:T(8,128)S(1)} %copy-done.115), kind=kOutput, calls=%fused_computation.12 | convolution fusion | flops 1819803648 | bytes 12386304 | tf_op jit(solution)/shard_map/dot_general | solution.py:605
  226.8 19.1 %shard_map.322 = (bf16[8,32,1152]{2,1,0:T(8,128)(2,1)S(1)}, bf16[4,256,1152]{2,1,0:T(8,128)(2,1)S(1)}) custom-call(bf16[8,32,1152]{2,1,0:T(8,128)(2,1)S(1)} %bitcast.275, bf16[256,1152]{1,0:T(8,128)(2,1)S(1)} %bitcast.274), custom_call_target="tpu_custom_call" | custom-call | tf_op jit(solution)/shard_map/pallas_call | solution.py:113
  249.5 11.2 %shard_map.323 = (bf16[4,128,1152]{2,1,0:T(8,128)(2,1)S(1)}, f32[4,88,128]{2,1,0:T(8,128)S(1)}) custom-call(bf16[128,1152]{1,0:T(8,128)(2,1)S(1)} %get-tuple-element.182.refs_0_, f32[88,128]{1,0:T(8,128)S(1)} %fusion.116.refs_1_), custom_call_target="tpu_custom_call" | custom-call | tf_op jit(solution)/shard_map/pallas_call | solution.py:113
  265.7 5.8 %multiply_reduce_fusion.3 = (f32[576]{0:T(1024)}, f32[64,8,576]{2,1,0:T(8,128)}, bf16[64,8,576]{2,1,0:T(8,128)(2,1)}) fusion(f32[64,8,576]{2,1,0:T(8,128)} %fusion.59, f32[64,8,576]{2,1,0:T(8,128)} %get-tuple-element.211, f32[64,8,576]{2,1,0:T(8,128)} %get-tuple-element.46, f32[576]{0:T(1024)S(1)} %copy-done.114, bf16[64,8,1152]{2,1,0:T(8,128)(2,1)} %dot_general.110, ...), kind=kOutput, calls=%fused_computation.81 | convolution fusion | flops 684195264 | bytes 7819776 | tf_op jit(solution)/shard_map/dot_general | solution.py:605
  271.5 8.6 %shard_map.324.refs_0_ = f32[16,8,576]{2,1,0:T(8,128)} custom-call(f32[64,8,576]{2,1,0:T(8,128)} %get-tuple-element.193.delta_ref, f32[64,8,576]{2,1,0:T(8,128)} %get-tuple-element.179.grad_y_ref, bf16[512,104]{1,0:T(8,128)(2,1)} %copy-done.44, f32[16,576]{1,0:T(8,128)} %multiply_bitcast_fusion.rate_ref.refs_2_), custom_call_target="tpu_custom_call" | custom-call | flops 23592960 | bytes 2359296 | tf_op jit(solution)/shard_map/pallas_call | solution.py:588
  281.1 19.1 %shard_map.325 = (f32[16,8,576]{2,1,0:T(8,128)S(1)}, bf16[4,256,768]{2,1,0:T(8,128)(2,1)S(1)}) custom-call(f32[16,8,576]{2,1,0:T(8,128)S(1)} %copy-done.13, f32[8,576]{1,0:T(8,128)S(1)} %copy-done.16, f32[16,576]{1,0:T(8,128)S(1)} %copy-done.8, bf16[4,256,768]{2,1,0:T(8,128)(2,1)S(1)} %bitcast.265), custom_call_target="tpu_custom_call" | custom-call | tf_op jit(solution)/shard_map/pallas_call | solution.py:411
  300.9 33.2 %shard_map.326 = (f32[64,8,576]{2,1,0:T(8,128)}, f32[64,8,576]{2,1,0:T(8,128)}, f32[16,8,576]{2,1,0:T(8,128)}, f32[2,64,8,128]{3,2,1,0:T(8,128)}) custom-call(f32[64,8,576]{2,1,0:T(8,128)} %get-tuple-element.193.delta_ref, f32[64,8,576]{2,1,0:T(8,128)} %get-tuple-element.192.drive_ref, f32[64,8,576]{2,1,0:T(8,128)} %get-tuple-element.179.grad_y_ref, ...), custom_call_target="tpu_custom_call" | custom-call | flops 80216064 | bytes 18874368 | tf_op jit(solution)/shard_map/pallas_call | solution.py:588
  340.2 7.4 %shard_map.327 = f32[512,104]{1,0:T(8,128)S(1)} custom-call(bf16[512,104]{1,0:T(8,128)(2,1)S(1)} %pad_maximum_fusion.2.x_ref), custom_call_target="tpu_custom_call" | custom-call | tf_op jit(solution)/shard_map/pallas_call | solution.py:178
  347.6 4.4 fusion.30
  368.0 5.4 convolution_bitcast_fusion.1
  373.4 4.0 convolution_bitcast_fusion
  400.8 54.3 %shard_map.328 = (f32[128,1152]{1,0:T(8,128)S(1)}, bf16[8,176,576]{2,1,0:T(8,128)(2,1)S(1)}, f32[8,24,128]{2,1,0:T(8,128)S(1)}, f32[4,16,128]{2,1,0:T(8,128)S(1)}) custom-call(bf16[4,128,1152]{2,1,0:T(8,128)(2,1)S(1)} %bitcast.270, bf16[8,176,576]{2,1,0:T(8,128)(2,1)S(1)} %bitcast.263, f32[8,24,128]{2,1,0:T(8,128)S(1)} %bitcast.277, ...), custom_call_target="tpu_custom_call" | custom-call | tf_op jit(solution)/shard_map/pallas_call | solution.py:261
  458.2 74.6 %shard_map.329 = (bf16[4,128,1152]{2,1,0:T(8,128)(2,1)S(1)}, bf16[4,128,1152]{2,1,0:T(8,128)(2,1)S(1)}, bf16[8,176,576]{2,1,0:T(8,128)(2,1)S(1)}, f32[8,24,128]{2,1,0:T(8,128)S(1)}, f32[8,16,128]{2,1,0:T(8,128)S(1)}) custom-call(bf16[128,1152]{1,0:T(8,128)(2,1)S(1)} %fusion.85.refs_0_, bf16[128,1152]{1,0:T(8,128)(2,1)S(1)} %get-tuple-element.176.refs_1_, ...), custom_call_target="tpu_custom_call" | custom-call | tf_op jit(solution)/shard_map/pallas_call | solution.py:113
  (418 shorter events, 163.9 us)
Async XLA Ops:
  7.2 104.7 %copy-start = (bf16[576,1152]{1,0:T(8,128)(2,1)S(1)}, bf16[576,1152]{1,0:T(8,128)(2,1)}, u32[]{:S(2)}) copy-start(bf16[576,1152]{1,0:T(8,128)(2,1)} %param.33) | copy-start | bytes 3981316
  7.2 541.5 %all-reduce.13.cloned.1.call-start = ((), (), s32[]{:S(2)}) async-start(), calls=%async_computation | async-start | bytes 5308416 | tf_op jit(solution)/shard_map/psum | solution.py:872
  8.9 40.2 %collective-permute-start = (bf16[4,3,1152]{2,1,0:T(4,128)(2,1)}, bf16[4,3,1152]{2,1,0:T(4,128)(2,1)S(1)}, u32[]{:S(2)}, u32[]{:S(2)}) collective-permute-start(bf16[4,3,1152]{2,1,0:T(4,128)(2,1)} %slice.158), channel_id=1, source_target_pairs={{0,4},{4,8},{8,12},{12,16},{16,20},{20,24},{24,28},{1,5},{5,9},{9,... | collective-permute-start | bytes 82952 | tf_op jit(solution)/shard_map/ppermute | solution.py:615
  42.7 23.7 %copy-start.48 = (f32[64,8]{1,0:T(8,128)}, f32[64,8]{1,0:T(8,128)S(1)}, u32[]{:S(2)}) copy-start(f32[64,8]{1,0:T(8,128)S(1)} %copy.193) | copy-start | bytes 6148
  43.9 22.6 %copy-start.81 = (f32[576]{0:T(1024)}, f32[576]{0:T(1024)S(1)}, u32[]{:S(2)}) copy-start(f32[576]{0:T(1024)S(1)} %convert_element_type.363) | copy-start | bytes 6916
  44.7 21.8 %copy-start.50 = (f32[64,8]{1,0:T(8,128)}, f32[64,8]{1,0:T(8,128)S(1)}, u32[]{:S(2)}) copy-start(f32[64,8]{1,0:T(8,128)S(1)} %copy.192) | copy-start | bytes 6148
  45.5 21.0 %copy-start.52 = (f32[64,8]{1,0:T(8,128)}, f32[64,8]{1,0:T(8,128)S(1)}, u32[]{:S(2)}) copy-start(f32[64,8]{1,0:T(8,128)S(1)} %copy.191) | copy-start | bytes 6148
  49.1 76.4 %copy-start.70 = (pred[128,256]{0,1:T(32,128)(4,1)}, pred[128,256]{0,1:T(32,128)(4,1)S(1)}, u32[]{:S(2)}) copy-start(pred[128,256]{0,1:T(32,128)(4,1)S(1)} %fusion.98) | copy-start | bytes 98308
  124.9 99.4 %copy-start.86 = (f32[128]{0:T(128)}, f32[128]{0:T(128)S(1)}, u32[]{:S(2)}) copy-start(f32[128]{0:T(128)S(1)} %get-tuple-element.214) | copy-start | bytes 1540
  125.0 27.1 %copy-start.90 = (f32[128]{0:T(128)}, f32[128]{0:T(128)S(1)}, u32[]{:S(2)}) copy-start(f32[128]{0:T(128)S(1)} %fusion.134) | copy-start | bytes 1540
  159.7 25.1 %copy-start.84 = (f32[128,8]{0,1:T(8,128)S(1)}, f32[128,8]{0,1:T(8,128)}, u32[]{:S(2)}) copy-start(f32[128,8]{0,1:T(8,128)} %convolution_add_fusion.3) | copy-start | bytes 12292
  162.5 22.3 %copy-start.31 = (f32[128,1152]{1,0:T(8,128)S(1)}, f32[128,1152]{1,0:T(8,128)}, u32[]{:S(2)}) copy-start(f32[128,1152]{1,0:T(8,128)} %copy-done.30) | copy-start | bytes 1769476
  186.8 22.8 %copy-start.115 = (f32[256,3072]{1,0:T(8,128)S(1)}, f32[256,3072]{1,0:T(8,128)}, u32[]{:S(2)}) copy-start(f32[256,3072]{1,0:T(8,128)} %get-tuple-element.213) | copy-start | bytes 9437188
  188.5 28.1 %slice-start = ((s8[7077888]{0:T(1024)(128)(4,1)}), s8[4194304]{0:T(1024)(128)(4,1)S(1)}, s32[]{:S(2)}) async-start(s8[7077888]{0:T(1024)(128)(4,1)} %bitcast.304), calls=%async_computation.1 | async-start | bytes 8388608
  224.4 21.5 %copy-start.89 = (pred[128,8]{0,1:T(8,128)(4,1)S(1)}, pred[128,8]{0,1:T(8,128)(4,1)}, u32[]{:S(2)}) copy-start(pred[128,8]{0,1:T(8,128)(4,1)} %iota_compare_fusion.4) | copy-start | bytes 3076
  300.9 33.3 %copy-start.19 = (bf16[4,256,768]{2,1,0:T(8,128)(2,1)}, bf16[4,256,768]{2,1,0:T(8,128)(2,1)S(1)}, u32[]{:S(2)}) copy-start(bf16[4,256,768]{2,1,0:T(8,128)(2,1)S(1)} %get-tuple-element.68) | copy-start | bytes 4718596
  300.9 33.3 %copy-start.21 = (bf16[67,8,576]{2,1,0:T(8,128)(2,1)S(1)}, bf16[67,8,576]{2,1,0:T(8,128)(2,1)}, u32[]{:S(2)}) copy-start(bf16[67,8,576]{2,1,0:T(8,128)(2,1)} %copy-done.20) | copy-start | bytes 1852420
  300.9 33.3 %copy-start.26 = (bf16[512,576]{1,0:T(8,128)(2,1)S(1)}, bf16[512,576]{1,0:T(8,128)(2,1)}, u32[]{:S(2)}) copy-start(bf16[512,576]{1,0:T(8,128)(2,1)} %copy-done.25) | copy-start | bytes 1769476
  300.9 33.3 %copy-start.34 = (f32[512,576]{1,0:T(8,128)S(1)}, f32[512,576]{1,0:T(8,128)}, u32[]{:S(2)}) copy-start(f32[512,576]{1,0:T(8,128)} %copy.195) | copy-start | bytes 3538948
  300.9 33.3 %copy-start.49 = (f32[64,8]{1,0:T(8,128)S(1)}, f32[64,8]{1,0:T(8,128)}, u32[]{:S(2)}) copy-start(f32[64,8]{1,0:T(8,128)} %copy-done.48) | copy-start | bytes 6148
  300.9 33.3 %copy-start.51 = (f32[64,8]{1,0:T(8,128)S(1)}, f32[64,8]{1,0:T(8,128)}, u32[]{:S(2)}) copy-start(f32[64,8]{1,0:T(8,128)} %copy-done.50) | copy-start | bytes 6148
  300.9 33.3 %copy-start.53 = (f32[64,8]{1,0:T(8,128)S(1)}, f32[64,8]{1,0:T(8,128)}, u32[]{:S(2)}) copy-start(f32[64,8]{1,0:T(8,128)} %copy-done.52) | copy-start | bytes 6148
  300.9 33.3 %copy-start.82 = (f32[576]{0:T(1024)S(1)}, f32[576]{0:T(1024)}, u32[]{:S(2)}) copy-start(f32[576]{0:T(1024)} %copy-done.81) | copy-start | bytes 6916
  357.1 27.3 %collective-permute-start.1 = (f32[3,4,576]{2,1,0:T(4,128)}, f32[3,4,576]{2,1,0:T(4,128)}, u32[]{:S(2)}, u32[]{:S(2)}) collective-permute-start(f32[3,4,576]{2,1,0:T(4,128)} %get-tuple-element.198), channel_id=1, source_target_pairs={{4,0},{8,4},{12,8},{16,12},{20,16},{24,20},{28,24},{5,1},{9,5},{13... | collective-permute-start | bytes 82952 | tf_op jit(solution)/shard_map/ppermute | solution.py:615
  (97 other events, 451.6 us)
Sparse Core Ops, SparseCore 0:
  366.4 169.1 all-reduce.12

commit v2 on v1

v2 whole, which is shorter than its diff:
```python
import functools
import math

import jax
import jax.numpy as jnp
from jax import lax
from jax.experimental import pallas as pl
from jax.experimental.pallas import tpu as pltpu
from jax.sharding import PartitionSpec as P

epsilon = 1e-05
log2e = 1.4426950408889634
cut = 1e30
MESH = pl.DeviceIdType.MESH
f32 = jnp.float32
bf16 = jnp.bfloat16
LANES = 128
MIB = 1024 * 1024


def greet(axes):
    barrier = pltpu.get_barrier_semaphore()
    told = 0
    for axis, count in axes:
        me = lax.axis_index(axis)
        for k in range(1, count):
            pl.semaphore_signal(
                barrier, inc=1, device_id={axis: lax.rem(me + k, count)}, device_id_type=MESH
            )
        told += count - 1
    return told


def sems_of(item):
    count = item[2]
    return [pltpu.SemaphoreType.DMA] + [pltpu.SemaphoreType.DMA((count - 1,))] * 2


def flipped(i, mask):
    bit = 1
    while bit <= mask:
        if mask & bit:
            i = i + bit - 2 * bit * lax.rem(i // bit, 2)
        bit *= 2
    return i


def begin(item, x_ref, o_ref, own_sem, send_sem, recv_sem):
    mode, axis, count = item
    me = lax.axis_index(axis)

    def remote(source, row, slot, to):
        return pltpu.make_async_remote_copy(
            src_ref=source,
            dst_ref=o_ref.at[row],
            send_sem=send_sem.at[slot],
            recv_sem=recv_sem.at[slot],
            device_id={axis: to},
            device_id_type=MESH,
        )

    own = pltpu.make_async_copy(x_ref.at[me] if mode == "scatter" else x_ref, o_ref.at[me], own_sem)
    copies, later = [], []
    if mode in ("gather", "scatter"):
        for mask in range(count - 1, 0, -1):
            to = flipped(me, mask)
            copies.append(remote(x_ref.at[to] if mode == "scatter" else x_ref, me, mask - 1, to))
    else:
        groups = count // mode
        side, place = lax.rem(me, mode), me // mode
        mates = [place * mode + lax.rem(side + j, mode) for j in range(1, mode)]
        slot = groups - 1
        for mate in mates:
            copies.append(remote(x_ref, me, slot, mate))
            slot += 1
        for mask in range(groups - 1, 0, -1):
            row = flipped(place, mask) * mode + side
            first = remote(x_ref, me, mask - 1, row)
            passed = []
            for mate in mates:
                passed.append(remote(o_ref.at[row], row, slot, mate))
                slot += 1
            later.append((first, passed))
    for copy in [first for first, _ in later] + copies:
        copy.start()
    own.start()
    return own, copies, later


def finish(under_way):
    for _, _, later in under_way:
        for first, passed in later:
            first.wait_recv()
            for second in passed:
                second.start()
    for own, copies, later in under_way:
        own.wait()
        for copy in copies:
            copy.wait()
        for first, passed in later:
            first.wait_send()
            for second in passed:
                second.wait()


def items_of(exchanges):
    return [(mode, axis, lax.axis_size(axis)) for _, mode, axis in exchanges]


def axes_of(items):
    return sorted({(axis, count) for _, axis, count in items})


def landed(x, item):
    shape = x.shape if item[0] == "scatter" else (item[2],) + x.shape
    return jax.ShapeDtypeStruct(shape, x.dtype)


def exchange_kernel(items, *refs):
    number = len(items)
    sems = refs[2 * number :]
    pl.semaphore_wait(pltpu.get_barrier_semaphore(), greet(axes_of(items)))
    finish(
        [
            begin(item, refs[i], refs[number + i], *sems[3 * i : 3 * i + 3])
            for i, item in enumerate(items)
        ]
    )


def exchange(number, *exchanges):
    items = items_of(exchanges)
    return pl.pallas_call(
        functools.partial(exchange_kernel, items),
        out_shape=[landed(x, item) for (x, _, _), item in zip(exchanges, items)],
        in_specs=[pl.BlockSpec(memory_space=pl.ANY)] * len(items),
        out_specs=[pl.BlockSpec(memory_space=pl.ANY)] * len(items),
        scratch_shapes=[sem for item in items for sem in sems_of(item)],
        compiler_params=pltpu.CompilerParams(
            collective_id=number, has_side_effects=True, vmem_limit_bytes=16 * MIB
        ),
    )(*[x for x, _, _ in exchanges])


def greet_near(axis, count):
    barrier = pltpu.get_barrier_semaphore()
    me = lax.axis_index(axis)
    beside = me + 1 - 2 * lax.rem(me, 2)
    pl.semaphore_signal(barrier, inc=1, device_id={axis: beside}, device_id_type=MESH)
    for k in range(1, count // 2):
        pl.semaphore_signal(
            barrier, inc=1, device_id={axis: lax.rem(me + 2 * k, count)}, device_id_type=MESH
        )
    pl.semaphore_wait(barrier, count // 2)


def sum_kernel(axis, count, x_ref, o_ref, beside_in, pair, far_in, send_sem, recv_sem):
    me = lax.axis_index(axis)
    beside = me + 1 - 2 * lax.rem(me, 2)
    greet_near(axis, count)
    near = pltpu.make_async_remote_copy(
        src_ref=x_ref,
        dst_ref=beside_in,
        send_sem=send_sem.at[0],
        recv_sem=recv_sem.at[0],
        device_id={axis: beside},
        device_id_type=MESH,
    )
    near.start()
    near.wait_recv()
    pair[...] = (x_ref[...].astype(f32) + beside_in[...].astype(f32)).astype(bf16)
    copies = []
    for k in range(1, count // 2):
        copies.append(
            pltpu.make_async_remote_copy(
                src_ref=pair,
                dst_ref=far_in.at[k - 1],
                send_sem=send_sem.at[k],
                recv_sem=recv_sem.at[k],
                device_id={axis: lax.rem(me + 2 * k, count)},
                device_id_type=MESH,
            )
        )
        copies[-1].start()
    for copy in copies:
        copy.wait_recv()
    total = pair[...].astype(f32)
    for k in range(count // 2 - 1):
        total = total + far_in[k].astype(f32)
    o_ref[...] = total
    near.wait_send()
    for copy in copies:
        copy.wait_send()


def summed_over(x, axis, number):
    count = lax.axis_size(axis)
    return pl.pallas_call(
        functools.partial(sum_kernel, axis, count),
        out_shape=jax.ShapeDtypeStruct(x.shape, f32),
        in_specs=[pl.BlockSpec(memory_space=pltpu.VMEM)],
        out_specs=pl.BlockSpec(memory_space=pltpu.VMEM),
        scratch_shapes=[
            pltpu.VMEM(x.shape, bf16),
            pltpu.VMEM(x.shape, bf16),
            pltpu.VMEM((count // 2 - 1,) + x.shape, bf16),
            pltpu.SemaphoreType.DMA((count // 2,)),
            pltpu.SemaphoreType.DMA((count // 2,)),
        ],
        compiler_params=pltpu.CompilerParams(
            collective_id=number, has_side_effects=True, vmem_limit_bytes=16 * MIB
        ),
    )(x)


class Share:
    def __init__(self, axis, count, size, x_ref, near_in, pairs, far_in, near_send, near_recv, far_send, far_recv):
        self.groups, self.size, self.x = count // size, size, x_ref
        self.near_in, self.pairs, self.far_in = near_in, pairs, far_in
        me = lax.axis_index(axis)
        side, place = lax.rem(me, size), me // size
        self.rows, self.near, self.far = [], [], []
        for k in range(self.groups):
            group = flipped(place, self.groups - 1 - k)
            self.rows.append(group * size + side)
            self.near.append(
                [
                    pltpu.make_async_remote_copy(
                        src_ref=x_ref.at[group * size + lax.rem(side + j, size)],
                        dst_ref=near_in.at[k, j - 1],
                        send_sem=near_send.at[k, j - 1],
                        recv_sem=near_recv.at[k, j - 1],
                        device_id={axis: place * size + lax.rem(side + j, size)},
                        device_id_type=MESH,
                    )
                    for j in range(1, size)
                ]
            )
            if k < self.groups - 1:
                self.far.append(
                    pltpu.make_async_remote_copy(
                        src_ref=pairs.at[k],
                        dst_ref=far_in.at[k],
                        send_sem=far_send.at[k],
                        recv_sem=far_recv.at[k],
                        device_id={axis: self.rows[k]},
                        device_id_type=MESH,
                    )
                )

    def begin(self):
        for copies in self.near:
            for copy in copies:
                copy.start()

    def near_sum(self, k):
        total = self.x[self.rows[k]].astype(f32)
        for j, copy in enumerate(self.near[k]):
            copy.wait_recv()
            total = total + self.near_in[k, j].astype(f32)
        return total

    def pass_on(self):
        for k, copy in enumerate(self.far):
            self.pairs[k] = self.near_sum(k).astype(bf16)
            copy.start()

    def total(self):
        total = self.near_sum(self.groups - 1)
        for k, copy in enumerate(self.far):
            copy.wait_recv()
            total = total + self.far_in[k].astype(f32)
        return total

    def close(self):
        for copy in [copy for copies in self.near for copy in copies] + self.far:
            copy.wait_send()


def share_kernel(shares, items, *refs):
    many, number = len(shares), len(items)
    at = 0

    def take(k):
        nonlocal at
        at += k
        return refs[at - k : at]

    xs, riders, outs, rider_outs = take(many), take(number), take(many), take(number)
    tasks = [Share(axis, count, size, x, *take(7)) for (axis, count, size), x in zip(shares, xs)]
    axes = set(axes_of(items)) | {(axis, count) for axis, count, _ in shares}
    pl.semaphore_wait(pltpu.get_barrier_semaphore(), greet(sorted(axes)))
    for task in tasks:
        task.begin()
    under_way = [begin(item, riders[i], rider_outs[i], *take(3)) for i, item in enumerate(items)]
    for task in tasks:
        task.pass_on()
    for task, out in zip(tasks, outs):
        out[...] = task.total().astype(out.dtype)
    for task in tasks:
        task.close()
    finish(under_way)


def share_of(number, shares, *exchanges):
    items = items_of(exchanges)
    anywhere = [pl.BlockSpec(memory_space=pl.ANY)] * len(items)
    held = [pl.BlockSpec(memory_space=pltpu.VMEM)] * len(shares)
    scratch = []
    for x, axis, size, _ in shares:
        groups = lax.axis_size(axis) // size
        part = x.shape[1:]
        scratch += [
            pltpu.VMEM((groups, size - 1) + part, bf16),
            pltpu.VMEM((groups - 1,) + part, bf16),
            pltpu.VMEM((groups - 1,) + part, bf16),
            pltpu.SemaphoreType.DMA((groups, size - 1)),
            pltpu.SemaphoreType.DMA((groups, size - 1)),
            pltpu.SemaphoreType.DMA((groups - 1,)),
            pltpu.SemaphoreType.DMA((groups - 1,)),
        ]
    return pl.pallas_call(
        functools.partial(
            share_kernel, [(axis, lax.axis_size(axis), size) for _, axis, size, _ in shares], items
        ),
        out_shape=[jax.ShapeDtypeStruct(x.shape[1:], kind) for x, _, _, kind in shares]
        + [landed(x, item) for (x, _, _), item in zip(exchanges, items)],
        in_specs=held + anywhere,
        out_specs=held + anywhere,
        scratch_shapes=scratch + [sem for item in items for sem in sems_of(item)],
        compiler_params=pltpu.CompilerParams(
            collective_id=number, has_side_effects=True, vmem_limit_bytes=32 * MIB
        ),
    )(*[share[0] for share in shares], *[x for x, _, _ in exchanges])


def turned(value):
    return pltpu.roll(value, value.shape[0] // 2, 0)


def carry_kernel(axis, count, back, items, *refs):
    number = len(items)
    local_ref, sums_ref, rate_ref = refs[:3]
    xs, o_ref, outs = refs[3 : 3 + number], refs[3 + number], refs[4 + number : 4 + 2 * number]
    send, got, send_sum, got_sum, total, enter = refs[4 + 2 * number : 10 + 2 * number]
    send_sem, recv_sem, send_sum_sem, recv_sum_sem = refs[10 + 2 * number : 14 + 2 * number]
    sems = refs[14 + 2 * number :]
    me = lax.axis_index(axis)
    states, rows, width = local_ref.shape
    half = rows // 2
    spans = []
    span = 1
    while span < count:
        spans.append(span)
        span *= 2
    sign = -1 if back else 1
    barrier = pltpu.get_barrier_semaphore()
    greeted = greet(axes_of(items))
    for span in spans:
        for by in (span, -span):
            there = me + by
            greeted = greeted + jnp.where((there >= 0) & (there < count), 1, 0)

            @pl.when((there >= 0) & (there < count))
            def _():
                pl.semaphore_signal(barrier, inc=1, device_id={axis: there}, device_id_type=MESH)

    upper = lax.broadcasted_iota(jnp.int32, (rows, width), 0) >= half
    first = upper if back else jnp.logical_not(upper)
    sums = sums_ref[...]
    sums_turned = turned(sums)
    sums_both = sums + sums_turned
    sums_first = jnp.where(first, sums, sums_turned)
    sums_last = jnp.where(first, sums_turned, sums)

    def packed_rate(j):
        return jnp.where(upper, rate_ref[pl.ds(2 * j + 1, 1), :], rate_ref[pl.ds(2 * j, 1), :])

    def both(j):
        even, odd = local_ref[2 * j], local_ref[2 * j + 1]
        low = jnp.where(upper, turned(odd), even)
        high = jnp.where(upper, odd, turned(even))
        return (high, low) if back else (low, high)

    for j in range(states // 2):
        opening, closing = both(j)
        total[j] = jnp.exp2(packed_rate(j) * sums_last) * opening + closing
        enter[j] = jnp.zeros((rows, width), f32)

    pl.semaphore_wait(barrier, greeted)
    under_way = [
        begin(item, xs[i], outs[i], *sems[3 * i : 3 * i + 3]) for i, item in enumerate(items)
    ]
    sums_total = sums_both
    sums_enter = jnp.zeros((rows, width), f32)
    for turn, span in enumerate(spans):
        to = me + sign * span
        origin = me - sign * span
        sends = (to >= 0) & (to < count)
        takes = (origin >= 0) & (origin < count)
        for j in range(0, states // 2, 2):
            send[turn, pl.ds(j * rows, 2 * rows), :] = jnp.concatenate([total[j], total[j + 1]], axis=0).astype(bf16)
        send_sum[turn] = sums_total
        copies = [
            pltpu.make_async_remote_copy(
                src_ref=source.at[turn],
                dst_ref=target.at[turn],
                send_sem=ssem.at[turn],
                recv_sem=rsem.at[turn],
                device_id={axis: to},
                device_id_type=MESH,
            )
            for source, target, ssem, rsem in (
                (send, got, send_sem, recv_sem),
                (send_sum, got_sum, send_sum_sem, recv_sum_sem),
            )
        ]

        @pl.when(sends)
        def _():
            for copy in copies:
                copy.start()

        @pl.when(jnp.logical_not(takes))
        def _():
            got[turn] = jnp.zeros(got.shape[1:], bf16)
            got_sum[turn] = jnp.zeros(got_sum.shape[1:], f32)

        @pl.when(takes)
        def _():
            for copy in copies:
                copy.wait_recv()

        for j in range(0, states // 2, 2):
            pair = got[turn, pl.ds(j * rows, 2 * rows), :].astype(f32)
            for i in (j, j + 1):
                came = pair[(i - j) * rows : (i - j + 1) * rows]
                rate = packed_rate(i)
                enter[i] = jnp.exp2(rate * sums_enter) * came + enter[i]
                total[i] = jnp.exp2(rate * sums_total) * came + total[i]
        sums_enter = sums_enter + got_sum[turn]
        sums_total = sums_total + got_sum[turn]

        @pl.when(sends)
        def _():
            for copy in copies:
                copy.wait_send()

    for j in range(states // 2):
        opening, _ = both(j)
        outer = enter[j]
        inner = jnp.exp2(packed_rate(j) * sums_first) * outer + opening
        low, high = (inner, outer) if back else (outer, inner)
        o_ref[2 * j] = jnp.where(upper, turned(high), low)
        o_ref[2 * j + 1] = jnp.where(upper, high, turned(low))
    finish(under_way)


def carried(local, sums, rate, axis, back, number, *exchanges):
    count = lax.axis_size(axis)
    states, rows, width = local.shape
    turns = max(1, (count - 1).bit_length())
    items = items_of(exchanges)
    anywhere = [pl.BlockSpec(memory_space=pl.ANY)] * len(items)
    return pl.pallas_call(
        functools.partial(carry_kernel, axis, count, back, items),
        out_shape=[jax.ShapeDtypeStruct(local.shape, f32)]
        + [landed(x, item) for (x, _, _), item in zip(exchanges, items)],
        in_specs=[pl.BlockSpec(memory_space=pltpu.VMEM)] * 3 + anywhere,
        out_specs=[pl.BlockSpec(memory_space=pltpu.VMEM)] + anywhere,
        scratch_shapes=[
            pltpu.VMEM((turns, states // 2 * rows, width), bf16),
            pltpu.VMEM((turns, states // 2 * rows, width), bf16),
            pltpu.VMEM((turns, rows, width), f32),
            pltpu.VMEM((turns, rows, width), f32),
            pltpu.VMEM((states // 2, rows, width), f32),
            pltpu.VMEM((states // 2, rows, width), f32),
            pltpu.SemaphoreType.DMA((turns,)),
            pltpu.SemaphoreType.DMA((turns,)),
            pltpu.SemaphoreType.DMA((turns,)),
            pltpu.SemaphoreType.DMA((turns,)),
        ]
        + [sem for item in items for sem in sems_of(item)],
        compiler_params=pltpu.CompilerParams(
            collective_id=number, has_side_effects=True, vmem_limit_bytes=24 * MIB
        ),
    )(local, sums, rate, *[x for x, _, _ in exchanges])


def spread(mapped_ref, first, wide_ref):
    count, steps, rows, lanes = wide_ref.shape
    column = lax.broadcasted_iota(jnp.int32, (mapped_ref.shape[1], lanes), 0)
    values = mapped_ref[...]
    for n in range(count):
        pick = (column == first + n).astype(bf16)
        wide_ref[n] = jnp.dot(values, pick, preferred_element_type=f32).reshape(steps, rows, lanes)


def rows_of(rate_ref, n, rows):
    return jnp.broadcast_to(rate_ref[n : n + 1, :], (rows, rate_ref.shape[1]))


def perm_of(steps, lines, seqs):
    rows = steps * lines
    laid = lax.broadcasted_iota(jnp.int32, (rows, rows), 0)
    natural = lax.broadcasted_iota(jnp.int32, (rows, rows), 1)
    line = laid % lines
    wanted = (line % seqs) * (rows // seqs) + (line // seqs) * steps + laid // lines
    return (natural == wanted).astype(bf16)


def unit_of(rows):
    return rows * lax.rsqrt(jnp.mean(rows * rows, axis=-1, keepdims=True) + epsilon)


def softplus(x):
    return jnp.maximum(x, 0.0) + jnp.log1p(jnp.exp(-jnp.abs(x)))


def sigmoid(x):
    return 1.0 / (1.0 + jnp.exp(-x))


def silu_slope(values, sigma):
    return sigma * (1.0 + values * (1.0 - sigma))


def dot(a, b):
    return jnp.dot(a, b, preferred_element_type=f32)


def dot_nt(a, b):
    return lax.dot_general(a, b, (((1,), (1,)), ((), ())), preferred_element_type=f32)


def dot_tn(a, b):
    return lax.dot_general(a, b, (((0,), (0,)), ((), ())), preferred_element_type=f32)


def front_kernel(seq_count, chan_count, tokens_ref, gain_ref, w_ref, taps_ref, bias_ref, xproj_ref, valid_ref,
                 normed_ref, ext_ref, pre_ref, gate_ref, mapped_ref,
                 halo, part, beside_in, pair, far_in, halo_send, halo_recv, send_sem, recv_sem):
    seqs, group, width = tokens_ref.shape
    steps, lines, full = pre_ref.shape
    taps, inner = taps_ref.shape[0], w_ref.shape[1]
    rim, rows, tail = taps - 1, steps * lines, halo.shape[1]
    here, me = lax.axis_index("seq"), lax.axis_index("chan")
    beside = me + 1 - 2 * lax.rem(me, 2)
    barrier = pltpu.get_barrier_semaphore()
    told = chan_count // 2
    for by in (1, -1):
        there = here + by
        near = (there >= 0) & (there < seq_count)
        told = told + jnp.where(near, 1, 0)

        @pl.when(near)
        def _():
            pl.semaphore_signal(barrier, inc=1, device_id={"seq": there}, device_id_type=MESH)

    pl.semaphore_signal(barrier, inc=1, device_id={"chan": beside}, device_id_type=MESH)
    for k in range(1, chan_count // 2):
        to = lax.rem(me + 2 * k, chan_count)
        pl.semaphore_signal(barrier, inc=1, device_id={"chan": to}, device_id_type=MESH)
    pl.semaphore_wait(barrier, told)
    ends = pltpu.make_async_remote_copy(
        src_ref=tokens_ref.at[:, pl.ds(group - tail, tail), :],
        dst_ref=halo,
        send_sem=halo_send,
        recv_sem=halo_recv,
        device_id={"seq": here + 1},
        device_id_type=MESH,
    )

    @pl.when(here + 1 < seq_count)
    def _():
        ends.start()

    def normed_of(rows_low):
        return (unit_of(rows_low.astype(f32)) * gain_ref[...]).astype(bf16)

    perm = perm_of(steps, lines, seqs)
    normed = dot(perm, normed_of(tokens_ref[...].reshape(rows, width))).astype(bf16)
    normed_ref[...] = normed
    conv_in = dot_nt(normed, w_ref[0]).astype(bf16).astype(f32)
    ext_ref[pl.ds(rim, steps), :, pl.ds(0, inner)] = conv_in.reshape(steps, lines, inner)
    gate_ref[:, :, pl.ds(0, inner)] = dot_nt(normed, w_ref[1]).reshape(steps, lines, inner)
    if full > inner:
        ext_ref[:, :, pl.ds(inner, full - inner)] = jnp.zeros((steps + rim, lines, full - inner), f32)
        gate_ref[:, :, pl.ds(inner, full - inner)] = jnp.zeros((steps, lines, full - inner), f32)

    @pl.when(here == 0)
    def _():
        halo[...] = jnp.zeros(halo.shape, bf16)

    @pl.when(here > 0)
    def _():
        ends.wait_recv()

    prior = dot_nt(normed_of(halo[...].reshape(seqs * tail, width)), w_ref[0]).astype(bf16)
    to = lax.broadcasted_iota(jnp.int32, (rim * lines, seqs * tail), 0)
    origin = lax.broadcasted_iota(jnp.int32, (rim * lines, seqs * tail), 1)
    pick = (to % lines < seqs) & (origin == (to % lines) * tail + tail - rim + to // lines)
    prior = dot(pick.astype(bf16), prior).reshape(rim, lines, inner)
    upper = lax.broadcasted_iota(jnp.int32, (lines, inner), 0) >= seqs
    for j in range(rim):
        own = turned(ext_ref[steps + j, :, pl.ds(0, inner)])
        ext_ref[j, :, pl.ds(0, inner)] = jnp.where(upper, own, prior[j])
    pre = jnp.broadcast_to(bias_ref[...], (steps, lines, full))
    for k in range(taps):
        pre = pre + taps_ref[k : k + 1, :] * ext_ref[pl.ds(k, steps)] * valid_ref[:, :, k : k + 1]
    pre_ref[...] = pre
    act_low = (pre * sigmoid(pre)).astype(bf16).reshape(rows, full)
    part[...] = dot_nt(act_low, xproj_ref[...]).astype(bf16)
    near = pltpu.make_async_remote_copy(
        src_ref=part,
        dst_ref=beside_in,
        send_sem=send_sem.at[0],
        recv_sem=recv_sem.at[0],
        device_id={"chan": beside},
        device_id_type=MESH,
    )
    near.start()
    near.wait_recv()
    pair[...] = (part[...].astype(f32) + beside_in[...].astype(f32)).astype(bf16)
    copies = []
    for k in range(1, chan_count // 2):
        copies.append(
            pltpu.make_async_remote_copy(
                src_ref=pair,
                dst_ref=far_in.at[k - 1],
                send_sem=send_sem.at[k],
                recv_sem=recv_sem.at[k],
                device_id={"chan": lax.rem(me + 2 * k, chan_count)},
                device_id_type=MESH,
            )
        )
        copies[-1].start()
    for copy in copies:
        copy.wait_recv()
    total = pair[...].astype(f32)
    for k in range(chan_count // 2 - 1):
        total = total + far_in[k].astype(f32)
    mapped_ref[...] = total.astype(bf16)
    near.wait_send()
    for copy in copies:
        copy.wait_send()

    @pl.when(here + 1 < seq_count)
    def _():
        ends.wait_send()


def front(tokens, gain, w_in, taps, bias, xproj, valid, full, number):
    seqs, group, width = tokens.shape
    steps, lines = valid.shape[:2]
    count, rows, maps = lax.axis_size("chan"), steps * lines, xproj.shape[0]
    tail = min(16, group)
    return pl.pallas_call(
        functools.partial(front_kernel, lax.axis_size("seq"), count),
        out_shape=[
            jax.ShapeDtypeStruct((rows, width), bf16),
            jax.ShapeDtypeStruct((steps + taps.shape[0] - 1, lines, full), f32),
            jax.ShapeDtypeStruct((steps, lines, full), f32),
            jax.ShapeDtypeStruct((steps, lines, full), f32),
            jax.ShapeDtypeStruct((rows, maps), bf16),
        ],
        in_specs=[pl.BlockSpec(memory_space=pltpu.VMEM)] * 7,
        out_specs=[pl.BlockSpec(memory_space=pltpu.VMEM)] * 5,
        scratch_shapes=[
            pltpu.VMEM((seqs, tail, width), bf16),
            pltpu.VMEM((rows, maps), bf16),
            pltpu.VMEM((rows, maps), bf16),
            pltpu.VMEM((rows, maps), bf16),
            pltpu.VMEM((count // 2 - 1, rows, maps), bf16),
            pltpu.SemaphoreType.DMA,
            pltpu.SemaphoreType.DMA,
            pltpu.SemaphoreType.DMA((count // 2,)),
            pltpu.SemaphoreType.DMA((count // 2,)),
        ],
        compiler_params=pltpu.CompilerParams(
            collective_id=number, has_side_effects=True, vmem_limit_bytes=48 * MIB
        ),
    )(tokens, gain, w_in, taps, bias, xproj, valid)


def totals_kernel(rank, taps, pre_ref, mapped_ref, dtw_ref, bias_ref, valid_ref, rate_ref,
                  dt_ref, step_ref, drive_ref, last_ref, sums_ref, wide):
    count, steps, rows, lanes = wide.shape

    @pl.when(pl.program_id(0) == 0)
    def _():
        spread(mapped_ref, rank, wide)

    dt_pre = (dot(mapped_ref[...], dtw_ref[...]) + bias_ref[...]).reshape(steps, rows, lanes)
    delta = softplus(dt_pre)
    pre = pre_ref[...]
    dt_ref[...] = dt_pre
    step_ref[...] = jnp.where(valid_ref[:, :, taps : taps + 1] > 0.5, delta, cut)
    drive_ref[...] = delta * pre * sigmoid(pre)
    rates = [rows_of(rate_ref, n, rows) for n in range(count)]
    zero = jnp.zeros((rows, lanes), f32)

    def one(p, held):
        states, sums = held
        step, drive = step_ref[p], drive_ref[p]
        states = tuple(
            jnp.exp2(step * rates[n]) * states[n] + drive * wide[n, p] for n in range(count)
        )
        return states, sums + step

    states, sums = lax.fori_loop(0, steps, one, ((zero,) * count, zero), unroll=2)
    for n in range(count):
        last_ref[n] = states[n]
    sums_ref[...] = sums


def states_kernel(rank, seqs, step_ref, drive_ref, mapped_ref, rate_ref, enter_ref, pre_ref, gate_ref, skip_ref, out_w_ref,
                  y_ref, gated_ref, state_ref, out_ref, wide_in, wide_read, total):
    count, steps, rows, lanes = wide_in.shape
    place = pl.program_id(0)

    @pl.when(place == 0)
    def _():
        spread(mapped_ref, rank, wide_in)
        spread(mapped_ref, rank + count, wide_read)
        total[...] = jnp.zeros_like(total)

    rates = [rows_of(rate_ref, n, rows) for n in range(count)]

    def one(p, states):
        step, drive = step_ref[p], drive_ref[p]
        states = tuple(
            jnp.exp2(step * rates[n]) * states[n] + drive * wide_in[n, p] for n in range(count)
        )
        terms = [states[n] * wide_read[n, p] for n in range(count)]
        while len(terms) > 1:
            terms = [a + b for a, b in zip(terms[::2], terms[1::2])]
        y_ref[p] = terms[0]
        for n in range(count):
            state_ref[p, n] = states[n]
        return states

    lax.fori_loop(0, steps, one, tuple(enter_ref[n] for n in range(count)), unroll=2)
    pre, gate = pre_ref[...], gate_ref[...]
    y_full = y_ref[...] + skip_ref[...] * (pre * sigmoid(pre))
    y_ref[...] = y_full
    gated = (y_full * (gate * sigmoid(gate))).astype(bf16).reshape(steps * rows, lanes)
    gated_ref[...] = gated
    total[...] += dot(gated, out_w_ref[...])

    @pl.when(place == pl.num_programs(0) - 1)
    def _():
        perm = perm_of(steps, rows, seqs)
        out_ref[...] = dot_tn(perm, total[...].astype(bf16)).astype(bf16)


def back_totals_kernel(rank, seqs, step_ref, mapped_ref, rate_ref, mixed_ref, normed_ref, out_w_ref, gate_ref, y_ref, gated_ref,
                       pre_ref, grad_y_ref, grad_z_ref, grad_out_ref, grad_gate_ref, skip_ref, last_ref,
                       wide, mixed):
    count, steps, rows, lanes = wide.shape

    @pl.when(pl.program_id(0) == 0)
    def _():
        spread(mapped_ref, rank + count, wide)
        mixed[...] = dot(perm_of(steps, rows, seqs), mixed_ref[...]).astype(bf16)

    grad_gated = dot_nt(mixed[...], out_w_ref[...]).reshape(steps, rows, lanes)
    gate, pre = gate_ref[...], pre_ref[...]
    sigma = sigmoid(gate)
    grad_y = grad_gated * (gate * sigma)
    grad_y_ref[...] = grad_y
    grad_z = (grad_gated * y_ref[...] * silu_slope(gate, sigma)).astype(bf16)
    grad_z = grad_z.reshape(steps * rows, lanes)
    grad_z_ref[...] = grad_z
    skip_ref[...] = jnp.sum(grad_y * (pre * sigmoid(pre)), axis=0)
    grad_out_ref[...] = dot_tn(gated_ref[...], mixed[...]).astype(bf16)
    grad_gate_ref[...] = dot_tn(grad_z, normed_ref[...]).astype(bf16)
    rates = [rows_of(rate_ref, n, rows) for n in range(count)]
    zero = jnp.zeros((rows, lanes), f32)

    def one(turn, held):
        p = steps - 1 - turn
        step, grad_y = step_ref[p], grad_y_ref[p]
        return tuple(
            jnp.exp2(step * rates[n]) * (held[n] + grad_y * wide[n, p]) for n in range(count)
        )

    held = lax.fori_loop(0, steps, one, (zero,) * count, unroll=2)
    for n in range(count):
        last_ref[n] = held[n]


def back_kernel(rank, step_ref, drive_ref, grad_y_ref, mapped_ref, rate_ref, first_ref, state_ref, enter_ref, dt_ref, pre_ref,
                dtw_ref, side_ref, log_ref, bias_ref, grad_dtw_ref, low_ref,
                wide_in, wide_read, sum_in, sum_read, to_input, to_decay, total):
    count, steps, rows, lanes = wide_in.shape
    place = pl.program_id(0)

    @pl.when(place == 0)
    def _():
        spread(mapped_ref, rank, wide_in)
        spread(mapped_ref, rank + count, wide_read)
        sum_in[...] = jnp.zeros_like(sum_in)
        sum_read[...] = jnp.zeros_like(sum_read)
        total[...] = jnp.zeros_like(total)

    rates = [rows_of(rate_ref, n, rows) for n in range(count)]
    for n in range(count):
        log_ref[n] = jnp.zeros((rows, lanes), f32)

    def step_back(p, carry, prior_of):
        step, drive, grad_y = step_ref[p], drive_ref[p], grad_y_ref[p]
        inputs = jnp.zeros((rows, lanes), f32)
        decays = jnp.zeros((rows, lanes), f32)
        new = []
        for n in range(count):
            grad = grad_y * wide_read[n, p] + carry[n]
            passed = jnp.exp2(step * rates[n]) * grad
            new.append(passed)
            grad_decay = passed * prior_of(n)
            decays = decays + grad_decay * rates[n]
            log_ref[n] += grad_decay * step
            inputs = inputs + grad * wide_in[n, p]
            sum_in[n, p] += grad * drive
            sum_read[n, p] += grad_y * state_ref[p, n]
        to_input[p] = inputs
        to_decay[p] = decays
        return tuple(new)

    def one(turn, carry):
        p = steps - 1 - turn
        return step_back(p, carry, lambda n: state_ref[p - 1, n])

    carry = lax.fori_loop(0, steps - 1, one, tuple(enter_ref[n] for n in range(count)))
    step_back(0, carry, lambda n: first_ref[n])
    dt_pre, pre = dt_ref[...], pre_ref[...]
    inputs = to_input[...]
    side_ref[...] = inputs * softplus(dt_pre)
    grad_delta = to_decay[...] * (1.0 / log2e) + inputs * (pre * sigmoid(pre))
    grad_dt = grad_delta * sigmoid(dt_pre)
    bias_ref[...] = jnp.sum(grad_dt, axis=0)
    grad_dt = grad_dt.astype(bf16).reshape(steps * rows, lanes)
    grad_dtw_ref[...] = dot_tn(mapped_ref[...], grad_dt)
    total[...] += dot_nt(grad_dt, dtw_ref[...])

    @pl.when(place == pl.num_programs(0) - 1)
    def _():
        column = lax.broadcasted_iota(jnp.int32, (lanes, total.shape[1]), 1)
        sums = total[...]
        for which, source in enumerate((sum_in, sum_read)):
            for n in range(count):
                pick = (column == rank + which * count + n).astype(bf16)
                sums = sums + dot(source[n].reshape(steps * rows, lanes).astype(bf16), pick)
        low_ref[...] = sums.astype(bf16)


def conv_back_kernel(taps, grad_mapped_ref, grad_y_ref, side_ref, pre_ref, ext_ref, skip_ref, xproj_ref, taps_ref, valid_ref,
                     grad_ref, rim_ref, grad_xproj_ref, sums_ref, ext_grad):
    steps, rows, lanes = pre_ref.shape
    rim = taps - 1
    pre = pre_ref[...]
    sigma = sigmoid(pre)
    grad_act = dot(grad_mapped_ref[...], xproj_ref[...]).reshape(steps, rows, lanes)
    grad_act = grad_act + grad_y_ref[...] * skip_ref[...] + side_ref[...]
    grad_pre = grad_act * silu_slope(pre, sigma)
    act_low = (pre * sigma).astype(bf16).reshape(steps * rows, lanes)
    grad_xproj_ref[...] = dot_tn(grad_mapped_ref[...], act_low)
    ext_grad[...] = jnp.zeros_like(ext_grad)
    for k in range(taps):
        masked = grad_pre * valid_ref[:, :, k : k + 1]
        sums_ref[k] = jnp.sum(masked * ext_ref[pl.ds(k, steps)], axis=0)
        ext_grad[pl.ds(k, steps)] += masked * taps_ref[k : k + 1, :]
    sums_ref[taps] = jnp.sum(grad_pre, axis=0)
    upper = lax.broadcasted_iota(jnp.int32, (rows, lanes), 0) >= rows // 2
    for j in range(rim):
        edge = ext_grad[j]
        rim_ref[j] = edge
        ext_grad[steps + j] += jnp.where(upper, 0.0, turned(edge))
    grad_ref[...] = ext_grad[pl.ds(rim, steps)]


def ends_kernel(count, tokens_ref, grad_ref, rim_ref, grad_z_ref, normed_ref, w_ref, grad_conv_ref, part_ref, gain_ref,
                came, send_sem, recv_sem):
    steps, lines, full = grad_ref.shape
    seqs, group, width = tokens_ref.shape
    rows, inner, rim = steps * lines, w_ref.shape[1], rim_ref.shape[0]
    here = lax.axis_index("seq")
    barrier = pltpu.get_barrier_semaphore()
    told = 0
    for by in (1, -1):
        there = here + by
        near = (there >= 0) & (there < count)
        told = told + jnp.where(near, 1, 0)

        @pl.when(near)
        def _():
            pl.semaphore_signal(barrier, inc=1, device_id={"seq": there}, device_id_type=MESH)

    pl.semaphore_wait(barrier, told)
    edge = pltpu.make_async_remote_copy(
        src_ref=rim_ref,
        dst_ref=came,
        send_sem=send_sem,
        recv_sem=recv_sem,
        device_id={"seq": here - 1},
        device_id_type=MESH,
    )

    @pl.when(here > 0)
    def _():
        edge.start()

    unit = unit_of(tokens_ref[...].reshape(rows, width).astype(f32))
    by_gate = dot(grad_z_ref[:, pl.ds(0, inner)], w_ref[1])

    @pl.when(here == count - 1)
    def _():
        came[...] = jnp.zeros(came.shape, f32)

    @pl.when(here < count - 1)
    def _():
        edge.wait_recv()

    upper = lax.broadcasted_iota(jnp.int32, (lines, full), 0) >= lines // 2
    last = [
        (grad_ref[steps - rim + j] + jnp.where(upper, turned(came[j]), 0.0))[None] for j in range(rim)
    ]
    grad = jnp.concatenate([grad_ref[pl.ds(0, steps - rim)]] + last, axis=0)
    grad = grad.reshape(rows, full).astype(bf16)
    grad_conv_ref[...] = dot_tn(grad, normed_ref[...]).astype(bf16)
    part = (dot(grad[:, :inner], w_ref[0]) + by_gate).astype(bf16)
    part = dot_tn(perm_of(steps, lines, seqs), part)
    part_ref[...] = part.astype(bf16)
    gain_ref[...] = jnp.sum(part * unit, axis=0, keepdims=True)

    @pl.when(here > 0)
    def _():
        edge.wait_send()


def ends(tokens, grad, rim, grad_z, normed, w_in, number):
    steps, lines, full = grad.shape
    rows, width = normed.shape
    return pl.pallas_call(
        functools.partial(ends_kernel, lax.axis_size("seq")),
        out_shape=[
            jax.ShapeDtypeStruct((full, width), bf16),
            jax.ShapeDtypeStruct((rows, width), bf16),
            jax.ShapeDtypeStruct((1, width), f32),
        ],
        in_specs=[pl.BlockSpec(memory_space=pltpu.VMEM)] * 6,
        out_specs=[pl.BlockSpec(memory_space=pltpu.VMEM)] * 3,
        scratch_shapes=[
            pltpu.VMEM(rim.shape, f32),
            pltpu.SemaphoreType.DMA,
            pltpu.SemaphoreType.DMA,
        ],
        compiler_params=pltpu.CompilerParams(
            collective_id=number, has_side_effects=True, vmem_limit_bytes=48 * MIB
        ),
    )(tokens, grad, rim, grad_z, normed, w_in)


def block_of(shape, kind):
    if kind == "tile":
        return pl.BlockSpec(shape[:-1] + (LANES,), lambda i: (0,) * (len(shape) - 1) + (i,))
    if kind == "rows":
        return pl.BlockSpec((LANES,) + shape[1:], lambda i: (i,) + (0,) * (len(shape) - 1))
    return pl.BlockSpec(shape, lambda i: (0,) * len(shape))


def by_tiles(kernel, full, ins, outs, scratch):
    return pl.pallas_call(
        kernel,
        grid=(full // LANES,),
        in_specs=[block_of(a.shape, kind) for a, kind in ins],
        out_specs=[block_of(shape, kind) for shape, _, kind in outs],
        out_shape=[jax.ShapeDtypeStruct(shape, dtype) for shape, dtype, _ in outs],
        scratch_shapes=[pltpu.VMEM(shape, dtype) for shape, dtype in scratch],
        compiler_params=pltpu.CompilerParams(vmem_limit_bytes=58 * MIB),
        cost_estimate=pl.CostEstimate(flops=1000, bytes_accessed=1000, transcendentals=0),
    )(*[a for a, _ in ins])


def packed_size(arrays, rows):
    total = -(-sum(a.size for a in arrays) // LANES)
    return -(-total // rows) * rows


def packed_rows(arrays, rows):
    total = packed_size(arrays, rows)
    joined = jnp.concatenate([a.reshape(-1) for a in arrays])
    return jnp.pad(joined, (0, total * LANES - joined.size)).reshape(total, LANES)


def unpacked_rows(packed, shapes):
    packed = packed.reshape(-1)
    arrays, at = [], 0
    for shape in shapes:
        size = math.prod(shape)
        arrays.append(packed[at : at + size].reshape(shape))
        at += size
    return arrays


def norm_back(grad_normed, unit_rows, inverse, weight_gain):
    scaled = grad_normed * weight_gain
    return inverse * (scaled - unit_rows * jnp.mean(scaled * unit_rows, axis=-1, keepdims=True))


def local(
    tokens,
    teacher,
    true_lengths,
    doc_lengths,
    routes,
    norm1_gain,
    in_weight,
    conv_weight,
    conv_bias,
    xproj_weight,
    dt_weight,
    dt_bias,
    a_log,
    skip_weight,
    out_weight,
    norm2_gain,
    router_weight,
    expert_in,
    expert_out,
):
    seqs, group, width = tokens.shape
    inner = in_weight.shape[2]
    rank = dt_weight.shape[0]
    states = a_log.shape[1]
    experts = router_weight.shape[1]
    n_seq = lax.axis_size("seq")
    n_chan = lax.axis_size("chan")
    shards = n_seq // experts
    most = group // 4
    taps = conv_weight.shape[0]
    rim = taps - 1
    lines = 8
    chunks = lines // seqs
    steps = group // chunks
    owned = seqs * group // n_chan
    part = min(group, owned)
    most = min(most, part)
    parts = owned // part
    place = lax.axis_index("chan")
    first_pos = lax.axis_index("seq") * group

    full = -(-inner // LANES) * LANES
    rows = steps * lines
    maps = rank + 2 * states

    def padded(x):
        return jnp.pad(x, ((0, 0),) * (x.ndim - 1) + ((0, full - inner),))

    at = (
        first_pos
        + jnp.arange(steps, dtype=jnp.int32)[:, None]
        + (jnp.arange(lines, dtype=jnp.int32) // seqs * steps)[None, :]
    )
    stops = []
    for k in range(doc_lengths.shape[1] - 1):
        stops.append(doc_lengths[:, k] + (stops[-1] if stops else 0))
    stops = [jnp.tile(stop, chunks)[None, :] for stop in stops]

    def doc_at(pos):
        return sum((pos >= stop).astype(jnp.int32) for stop in stops)

    doc_ids = doc_at(at)
    keep = (doc_ids == doc_at(at - 1)) & (at > 0)
    valid = [doc_at(at - rim + k) == doc_ids for k in range(taps)] + [keep]
    valid = jnp.stack(valid + [keep] * (lines - taps - 1), axis=-1).astype(f32)

    w_in = in_weight.transpose(1, 2, 0)
    router_rows = router_weight.T
    gain_one = norm1_gain.astype(f32)
    taps_full = padded(conv_weight.astype(f32))
    xproj_rows = padded(xproj_weight.T)
    dt_rows = jnp.pad(padded(dt_weight), ((0, maps - rank), (0, 0)))
    skip_row = padded(skip_weight[None])
    out_rows = jnp.pad(out_weight, ((0, full - inner), (0, 0)))
    rate = -jnp.exp(a_log.T)
    rate_two = padded(rate * log2e)
    normed_one, extended, pre_act, gate_z, mapped = front(
        tokens,
        gain_one[None],
        w_in,
        taps_full,
        padded(conv_bias.astype(f32)[None]),
        xproj_rows,
        valid,
        full,
        1,
    )
    act_shape, state_shape, wide_shape = (steps, lines, full), (states, lines, full), (states, steps, lines, LANES)
    dt_pre, step_size, drive, last, sums = by_tiles(
        functools.partial(totals_kernel, rank, taps),
        full,
        [
            (pre_act, "tile"),
            (mapped, "whole"),
            (dt_rows, "tile"),
            (padded(dt_bias[None]), "tile"),
            (valid, "whole"),
            (rate_two, "tile"),
        ],
        [
            (act_shape, f32, "tile"),
            (act_shape, f32, "tile"),
            (act_shape, f32, "tile"),
            (state_shape, f32, "tile"),
            ((lines, full), f32, "tile"),
        ],
        [(wide_shape, f32)],
    )
    (enter,) = carried(last, sums, rate_two, "seq", False, 2)
    y_full, gated, state, out_part = by_tiles(
        functools.partial(states_kernel, rank, seqs),
        full,
        [
            (step_size, "tile"),
            (drive, "tile"),
            (mapped, "whole"),
            (rate_two, "tile"),
            (enter, "tile"),
            (pre_act, "tile"),
            (gate_z, "tile"),
            (skip_row, "tile"),
            (out_rows, "rows"),
        ],
        [
            (act_shape, f32, "tile"),
            ((rows, full), bf16, "tile"),
            ((steps, states, lines, full), f32, "tile"),
            ((rows, width), bf16, "whole"),
        ],
        [(wide_shape, f32)] * 2 + [((rows, width), f32)],
    )
    (mixed,) = share_of(3, [(out_part.reshape(n_chan, owned, width), "chan", 2, f32)])

    def own(x):
        return lax.dynamic_slice_in_dim(x.reshape((rows,) + x.shape[2:]), place * owned, owned, 0)

    tokens_own = own(tokens).astype(f32)
    inverse_one = lax.rsqrt(jnp.mean(tokens_own * tokens_own, axis=-1, keepdims=True) + epsilon)
    unit_one = tokens_own * inverse_one
    hidden_one = tokens_own + mixed
    inverse_two = lax.rsqrt(jnp.mean(hidden_one * hidden_one, axis=-1, keepdims=True) + epsilon)
    unit_two = hidden_one * inverse_two
    gain_two = norm2_gain.astype(f32)
    normed_two = (unit_two * gain_two).astype(bf16)
    probs = jax.nn.softmax(dot_nt(normed_two, router_rows), axis=-1)
    routes_own = own(routes)
    chosen = routes_own[..., None] == jnp.arange(experts, dtype=jnp.int32)
    chosen_rows = chosen.astype(f32)
    gate_value = jnp.sum(probs * chosen_rows, axis=-1, keepdims=True)
    row = jnp.arange(owned, dtype=jnp.int32)
    earlier = (row[None, :] < row[:, None]) & (row[None, :] // part == row[:, None] // part)
    rank_in = dot(earlier.astype(bf16), chosen.astype(bf16))
    slots = parts * most
    wanted = rank_in + (row // part * most).astype(f32)[:, None]
    hit = (wanted[..., None] == jnp.arange(slots, dtype=f32)) & chosen[..., None]
    hit = hit.astype(bf16)
    hit_send = hit.reshape(owned, experts * slots)
    hit_back = jnp.repeat(hit, shards, axis=1).reshape(owned, n_seq * slots)

    def to_slabs(x):
        packed = dot_tn(hit_send, x).astype(bf16).reshape(experts, slots, width)
        return jnp.repeat(packed, shards, axis=0), "scatter", "seq"

    def to_rows(x):
        return x.reshape(n_seq, slots, width), "scatter", "seq"

    def by_units(x):
        return x.reshape(n_seq * slots, n_chan, units).transpose(1, 0, 2), "scatter", "chan"

    def flat(x):
        return x.reshape(-1, x.shape[-1])

    first_slab, second_slab = expert_in[0], expert_out[0]
    units = first_slab.shape[1] // n_chan
    arrived = flat(exchange(4, to_slabs(normed_two))[0])
    pre_hidden = dot(arrived, first_slab)
    cdf = 0.5 * (1.0 + lax.erf(pre_hidden * 0.7071067811865476))
    hidden_low = (pre_hidden * cdf).astype(bf16)
    density = jnp.exp(-0.5 * pre_hidden * pre_hidden) * 0.3989422804014327
    slope = cdf + pre_hidden * density
    result = dot(hidden_low, second_slab).astype(bf16)
    result_rows, rows_all = exchange(5, to_rows(result), (arrived, 2, "chan"))
    expert_total = dot(hit_back, flat(result_rows))
    layer = hidden_one + gate_value * expert_total
    layer_low = layer.astype(bf16)

    flat_row = place * owned + row
    seq_of = flat_row // group
    lengths_own = sum(
        jnp.where(seq_of == s, true_lengths[s], 0) for s in range(seqs)
    )
    total_true = jnp.sum(true_lengths).astype(f32)
    loss_mask = (first_pos + flat_row % group < lengths_own).astype(f32)[:, None]
    error = layer - own(teacher).astype(f32)
    loss_part = jnp.sum(loss_mask * error * error) / total_true
    grad_layer = 2.0 / total_true * loss_mask * error
    grad_gate = jnp.sum(grad_layer * expert_total, axis=-1, keepdims=True)
    grad_result = (gate_value * grad_layer).astype(bf16)
    grad_rows, hidden_all = exchange(6, to_slabs(grad_result), by_units(hidden_low))
    grad_rows = flat(grad_rows)
    grad_pre = (dot_nt(grad_rows, second_slab) * slope).astype(bf16)
    grad_slab_rows = dot_nt(grad_pre, first_slab).astype(bf16)
    grad_expert, grad_rows_all = exchange(7, to_rows(grad_slab_rows), (grad_rows, 2, "chan"))
    grad_expert = dot(hit_back, flat(grad_expert))

    grad_logit = grad_gate * gate_value * (chosen_rows - probs)
    grad_router = dot_tn(grad_logit.astype(bf16), normed_two)
    grad_normed_two = grad_expert + dot(grad_logit.astype(bf16), router_rows)
    grad_gain_two = jnp.sum(grad_normed_two * unit_two, axis=0)
    grad_hidden_one = grad_layer + norm_back(grad_normed_two, unit_two, inverse_two, gain_two)

    shared = packed_rows([grad_gain_two, grad_router, loss_part], 8)
    grad_mixed, shared = exchange(
        8, (grad_hidden_one.astype(bf16), 2, "chan"), (shared, "gather", "chan")
    )
    shared = jnp.sum(shared, axis=0)
    grad_y, grad_z, grad_out_w, grad_in_gate, skip_sums, back_last = by_tiles(
        functools.partial(back_totals_kernel, rank, seqs),
        full,
        [
            (step_size, "tile"),
            (mapped, "whole"),
            (rate_two, "tile"),
            (grad_mixed.reshape(rows, width), "whole"),
            (normed_one, "whole"),
            (out_rows, "rows"),
            (gate_z, "tile"),
            (y_full, "tile"),
            (gated, "tile"),
            (pre_act, "tile"),
        ],
        [
            (act_shape, f32, "tile"),
            ((rows, full), bf16, "tile"),
            ((full, width), bf16, "rows"),
            ((full, width), bf16, "rows"),
            ((lines, full), f32, "tile"),
            (state_shape, f32, "tile"),
        ],
        [(wide_shape, f32), ((rows, width), bf16)],
    )
    summed_out, summed_gate = lax.psum((grad_out_w, grad_in_gate), "seq")
    (back_enter,) = carried(back_last, sums, rate_two, "seq", True, 9)
    side, log_sums, bias_sums, grad_dt_w, low_part = by_tiles(
        functools.partial(back_kernel, rank),
        full,
        [
            (step_size, "tile"),
            (drive, "tile"),
            (grad_y, "tile"),
            (mapped, "whole"),
            (rate_two, "tile"),
            (enter, "tile"),
            (state, "tile"),
            (back_enter, "tile"),
            (dt_pre, "tile"),
            (pre_act, "tile"),
            (dt_rows, "tile"),
        ],
        [
            (act_shape, f32, "tile"),
            (state_shape, f32, "tile"),
            ((lines, full), f32, "tile"),
            ((maps, full), f32, "tile"),
            ((rows, maps), bf16, "whole"),
        ],
        [(wide_shape, f32)] * 4 + [((steps, lines, LANES), f32)] * 2 + [((rows, maps), f32)],
    )
    grad_mapped = summed_over(low_part, "chan", 10).astype(bf16)
    grad_conv_in, rims, grad_xproj, conv_sums = by_tiles(
        functools.partial(conv_back_kernel, taps),
        full,
        [
            (grad_mapped, "whole"),
            (grad_y, "tile"),
            (side, "tile"),
            (pre_act, "tile"),
            (extended, "tile"),
            (skip_row, "tile"),
            (xproj_rows, "tile"),
            (taps_full, "tile"),
            (valid, "whole"),
        ],
        [
            (act_shape, f32, "tile"),
            ((rim, lines, full), f32, "tile"),
            ((maps, full), f32, "tile"),
            ((taps + 1, lines, full), f32, "tile"),
        ],
        [((steps + rim, lines, LANES), f32)],
    )
    grad_in_conv, normed_part, grad_gain_one = ends(
        tokens, grad_conv_in, rims, grad_z, normed_one, w_in, 14
    )
    normed_part = normed_part.reshape(n_chan, owned, width)
    sums_all = jnp.concatenate([conv_sums, bias_sums[None], skip_sums[None], log_sums], axis=0)
    sums_all = jnp.sum(sums_all, axis=1)

    def cut_rows(x, unit):
        each = -(-x.shape[0] // (unit * n_seq)) * unit
        return jnp.pad(x, ((0, each * n_seq - x.shape[0]), (0, 0))).reshape(n_seq, each, -1)

    large = cut_rows(grad_in_conv, 16)
    middle = cut_rows(jnp.concatenate([grad_xproj, grad_dt_w[:rank]], axis=0).astype(bf16), 16)
    across = n_chan // 2
    grad_normed_one, large, middle, sums_all, shared, grad_gain_one, grad_pre_all = share_of(
        11,
        [
            (normed_part, "chan", 2, f32),
            (large, "seq", across, bf16),
            (middle, "seq", across, bf16),
        ],
        (cut_rows(sums_all, 8), "scatter", "seq"),
        (cut_rows(shared, 8), "scatter", "seq"),
        (grad_gain_one, "gather", "chan"),
        by_units(grad_pre),
    )
    sums_all = jnp.sum(sums_all, axis=0)
    shared = jnp.sum(shared, axis=0)
    grad_gain_one = jnp.sum(grad_gain_one, axis=0)
    grad_own = grad_hidden_one + norm_back(grad_normed_one, unit_one, inverse_one, gain_one)
    large, grad_tokens, layer_out, middle, sums_all, shared, grad_gain_one = exchange(
        12,
        (large, across, "seq"),
        (grad_own.astype(bf16), 2, "chan"),
        (layer_low, 2, "chan"),
        (middle, across, "seq"),
        (sums_all, "gather", "seq"),
        (shared, "gather", "seq"),
        (grad_gain_one, "gather", "seq"),
    )
    grad_first = dot_tn(flat(rows_all), flat(grad_pre_all))
    grad_second = dot_tn(flat(hidden_all), flat(grad_rows_all))
    grad_gain_one = jnp.sum(grad_gain_one, axis=(0, 1))
    summed_in = jnp.stack([flat(large)[:inner], summed_gate[:inner]]).astype(f32)
    middle = flat(middle)[:, :inner].astype(f32)
    small = flat(sums_all)[:, :inner]
    tiny = unpacked_rows(flat(shared), [(width,), grad_router.shape, ()])
    return (
        layer_out.reshape(seqs, group, width),
        tiny[2],
        grad_tokens.reshape(seqs, group, width).astype(f32),
        grad_gain_one,
        summed_in.transpose(2, 0, 1),
        small[:taps],
        small[taps],
        middle[:maps].T,
        middle[maps : maps + rank],
        small[taps + 1],
        (small[taps + 3 : taps + 3 + states] * rate).T,
        small[taps + 2],
        summed_out[:inner].astype(f32),
        tiny[0],
        tiny[1].T,
        grad_first[None],
        grad_second[None],
    )


def solution(mesh):
    placed = (
        P(None, "seq", None),
        P(None, "seq", None),
        P(),
        P(),
        P(None, "seq"),
        P(),
        P(None, None, "chan"),
        P(None, "chan"),
        P("chan"),
        P("chan", None),
        P(None, "chan"),
        P("chan"),
        P("chan", None),
        P("chan"),
        P("chan", None),
        P(),
        P(),
        P("seq", None, None),
        P("seq", None, None),
    )
    return jax.shard_map(
        local,
        mesh=mesh,
        in_specs=placed,
        out_specs=(
            P(None, "seq", None),
            P(),
            P(None, "seq", None),
            P(),
            P(None, None, "chan"),
            P(None, "chan"),
            P("chan"),
            P("chan", None),
            P(None, "chan"),
            P("chan"),
            P("chan", None),
            P("chan"),
            P("chan", None),
            P(),
            P(),
            P("seq", None, "chan"),
            P("seq", "chan", None),
        ),
        check_vma=False,
    )
```

time: 571 us -> 486 us (0.85)
  matrix products: 73.1 us -> 36.3 us
  other arithmetic: 51.1 us -> 24.9 us
  local copies, waits for them, and re-layouts: 76.8 us -> 54.2 us
  Pallas kernels: 339 us -> 347 us
  starting transfers between devices: 6.18 us -> 0.04 us
    pallas_call x6 -> x9, Pallas kernels: 129 us -> 172 us  [the longest x5 79 us: by_tiles(): pl.pallas_call(kernel, grid=(full // LANES,), in_specs=[block_of(a.shape,...]
    pallas_call x6, Pallas kernels: 166 us -> 128 us  [exchange(): pl.pallas_call(functools.partial(exchange_kernel, items), out_shape=[land...]
    dot_general x8 -> x3, matrix products: 22.8 us -> 8.06 us  [dot_nt(): lax.dot_general(a, b, (((1,), (1,)), ((), ())), preferred_element_type=f32)]
    dot_general x12 -> x6, matrix products: 28.7 us -> 16.6 us  [dot(): return jnp.dot(a, b, preferred_element_type=f32)]
    pallas_call x2, Pallas kernels: 29.6 us -> 40.5 us  [carried(): pl.pallas_call(functools.partial(carry_kernel, axis, count, back, items),...]
    mul x9 -> x1, other arithmetic: 10.9 us -> 0.79 us  [local(): rate_two = padded(rate * log2e)]
    dot_general x10 -> x5, matrix products: 21.6 us -> 11.6 us  [dot_tn(): lax.dot_general(a, b, (((0,), (0,)), ((), ())), preferred_element_type=f32)]
    convert_element_type x10 -> x0, local copies, waits for them, and re-layouts: 9.9 us -> none  [the longest x2 6.6 us: normed_of(): full = rows.astype(f32)]
  transfers between devices with their start and end apart: 3 -> 1, of which waited for: 0 -> 0; matrix products, arithmetic and copies ran while one was open for 16% -> 7% of each run, Pallas kernels for 23% -> 36%
where the time goes in v2:
time: 486 us; the launch traced here: 479 us
  Pallas kernels  347 us (71%)
  local copies, waits for them, and re-layouts  54.2 us (11%)
  matrix products  36.3 us (7%)
  other arithmetic  24.9 us (5%)
  between operations  16.6 us (3%)
    pallas_call x6, Pallas kernels, exchange(): pl.pallas_call(functools.partial(exchange_kernel, items), out_shape=[land...  128 us
    pallas_call x5, Pallas kernels, by_tiles(): pl.pallas_call(kernel, grid=(full // LANES,), in_specs=[block_of(a.shape,...  79 us
    pallas_call x2, Pallas kernels, share_of(): pl.pallas_call(functools.partial(share_kernel, [(axis, lax.axis_size(axis...  66.2 us
    pallas_call x2, Pallas kernels, carried(): pl.pallas_call(functools.partial(carry_kernel, axis, count, back, items),...  40.5 us
    unnamed x141, local copies, waits for them, and re-layouts  25.6 us
    dot_general x6, matrix products, dot(): return jnp.dot(a, b, preferred_element_type=f32)  16.6 us
    pallas_call x1, Pallas kernels, front(): pl.pallas_call(functools.partial(front_kernel, lax.axis_size('seq'), coun...  16.6 us
    dot_general x5, matrix products, dot_tn(): lax.dot_general(a, b, (((0,), (0,)), ((), ())), preferred_element_type=f32)  11.6 us
  transfers between devices with their start and end apart: 1, of which 0 were waited for; matrix products, arithmetic and copies ran while one was open for 7% of the time, Pallas kernels for 36%

profile of v2, /device:TPU:0, one launch (start us, length us, event | category | flops | bytes accessed | tf_op | source)
XLA Modules:
  0.0 478.6 jit_solution(11214980620897481831)
XLA Ops:
  17.4 16.6 %shard_map.314 = (bf16[512,1152]{1,0:T(8,128)(2,1)S(1)}, f32[67,8,640]{2,1,0:T(8,128)}, f32[64,8,640]{2,1,0:T(8,128)S(1)}, f32[64,8,640]{2,1,0:T(8,128)S(1)}, bf16[512,104]{1,0:T(8,128)(2,1)S(1)}) custom-call(bf16[4,128,1152]{2,1,0:T(8,128)(2,1)S(1)} %copy-done.3, f32[1,1152]{1,0:T(1,128)S(1)} %broadcast_in_dim.35.gain_ref, bf16[2,576,1152]{2,1,0:T(8,128)(2,1)} %bitcast.131, ...), custom_call_target="tpu_custom_call" | custom-call | tf_op jit(solution)/shard_map/pallas_call | solution.py:658
  37.8 9.6 %shard_map.315 = (f32[64,8,640]{2,1,0:T(8,128)}, f32[64,8,640]{2,1,0:T(8,128)}, f32[64,8,640]{2,1,0:T(8,128)}, f32[16,8,640]{2,1,0:T(8,128)}, f32[8,640]{1,0:T(8,128)}) custom-call(f32[64,8,640]{2,1,0:T(8,128)} %copy-done.2, bf16[512,104]{1,0:T(8,128)(2,1)} %copy-done.11, bf16[104,640]{1,0:T(8,128)(2,1)} %pad.80.dtw_ref, f32[1,640]{1,0:T(1,128)} %pad.61.bias_ref, ...), custom_call_target="tpu_custom_call" | custom-call | flops 1000 | bytes 1000 | tf_op jit(solution)/shard_map/pallas_call | solution.py:973
  49.1 11.5 %shard_map.316.enter_ref.first_ref = f32[16,8,640]{2,1,0:T(8,128)S(1)} custom-call(f32[16,8,640]{2,1,0:T(8,128)S(1)} %copy-done.26, f32[8,640]{1,0:T(8,128)S(1)} %copy-done.33, f32[16,640]{1,0:T(8,128)S(1)} %copy-done.12), custom_call_target="tpu_custom_call" | custom-call | tf_op jit(solution)/shard_map/pallas_call | solution.py:465
  61.4 17.2 %shard_map.317 = (f32[64,8,640]{2,1,0:T(8,128)}, bf16[512,640]{1,0:T(8,128)(2,1)}, f32[64,16,8,640]{3,2,1,0:T(8,128)}, bf16[512,1152]{1,0:T(8,128)(2,1)}) custom-call(f32[64,8,640]{2,1,0:T(8,128)} %get-tuple-element.73.step_ref, f32[64,8,640]{2,1,0:T(8,128)} %get-tuple-element.74.drive_ref, bf16[512,104]{1,0:T(8,128)(2,1)} %copy-done.11, ...), custom_call_target="tpu_custom_call" | custom-call | flops 1000 | bytes 1000 | tf_op jit(solution)/shard_map/pallas_call | solution.py:973
  79.8 10.9 %shard_map.318 = f32[128,1152]{1,0:T(8,128)S(1)} custom-call(bf16[4,128,1152]{2,1,0:T(8,128)(2,1)S(1)} %bitcast.116), custom_call_target="tpu_custom_call" | custom-call | tf_op jit(solution)/shard_map/pallas_call | solution.py:322
  94.5 22.3 %shard_map.319 = bf16[8,32,1152]{2,1,0:T(8,128)(2,1)S(1)} custom-call(bf16[8,32,1152]{2,1,0:T(8,128)(2,1)S(1)} %bitcast.112), custom_call_target="tpu_custom_call" | custom-call | tf_op jit(solution)/shard_map/pallas_call | solution.py:133
  116.7 7.5 %multiply_convert_fusion = (bf16[256,3072]{1,0:T(8,128)(2,1)}, f32[256,3072]{1,0:T(8,128)}) fusion(bf16[256,1152]{1,0:T(8,128)(2,1)S(1)} %bitcast.109, bf16[1,1152,3072]{2,1,0:T(8,128)(2,1)} %param.36), kind=kOutput, calls=%fused_computation.18 | convolution fusion | flops 1815871488 | bytes 12386304 | tf_op jit(solution)/shard_map/dot_general | solution.py:529
  126.8 5.7 %fusion.21 = bf16[256,1152]{1,0:T(8,128)(2,1)S(1)} fusion(bf16[256,3072]{1,0:T(8,128)(2,1)} %get-tuple-element.153, bf16[1,3072,1152]{2,1,0:T(8,128)(2,1)} %param.37), kind=kOutput, calls=%fused_computation.21 | convolution fusion | flops 1812234240 | bytes 9240576 | tf_op jit(solution)/shard_map/dot_general | solution.py:529
  132.5 17.8 %shard_map.320 = (bf16[8,32,1152]{2,1,0:T(8,128)(2,1)S(1)}, bf16[4,256,1152]{2,1,0:T(8,128)(2,1)S(1)}) custom-call(bf16[8,32,1152]{2,1,0:T(8,128)(2,1)S(1)} %bitcast.121, bf16[256,1152]{1,0:T(8,128)(2,1)S(1)} %bitcast.110), custom_call_target="tpu_custom_call" | custom-call | tf_op jit(solution)/shard_map/pallas_call | solution.py:133
  161.2 22.3 %shard_map.321 = (bf16[8,32,1152]{2,1,0:T(8,128)(2,1)S(1)}, bf16[4,256,768]{2,1,0:T(8,128)(2,1)S(1)}) custom-call(bf16[8,32,1152]{2,1,0:T(8,128)(2,1)S(1)} %bitcast.111, bf16[4,256,768]{2,1,0:T(8,128)(2,1)S(1)} %bitcast.107), custom_call_target="tpu_custom_call" | custom-call | tf_op jit(solution)/shard_map/pallas_call | solution.py:133
  184.7 5.7 %fusion.11 = bf16[256,3072]{1,0:T(8,128)(2,1)S(1)} fusion(bf16[256,1152]{1,0:T(8,128)(2,1)S(1)} %bitcast.119, bf16[1,3072,1152]{2,1,0:T(8,128)(2,1)} %param.37, f32[256,3072]{1,0:T(8,128)S(1)} %copy-done.67), kind=kOutput, calls=%fused_computation.11 | convolution fusion | flops 1819803648 | bytes 12386304 | tf_op jit(solution)/shard_map/dot_general | solution.py:533
  192.6 17.6 %shard_map.322 = (bf16[8,32,1152]{2,1,0:T(8,128)(2,1)S(1)}, bf16[4,256,1152]{2,1,0:T(8,128)(2,1)S(1)}) custom-call(bf16[8,32,1152]{2,1,0:T(8,128)(2,1)S(1)} %bitcast.122, bf16[256,1152]{1,0:T(8,128)(2,1)S(1)} %bitcast.120), custom_call_target="tpu_custom_call" | custom-call | tf_op jit(solution)/shard_map/pallas_call | solution.py:133
  217.3 11.4 %shard_map.323 = (bf16[4,128,1152]{2,1,0:T(8,128)(2,1)S(1)}, f32[4,88,128]{2,1,0:T(8,128)S(1)}) custom-call(bf16[128,1152]{1,0:T(8,128)(2,1)S(1)} %get-tuple-element.138.refs_0_, f32[88,128]{1,0:T(8,128)S(1)} %fusion.59.refs_1_), custom_call_target="tpu_custom_call" | custom-call | tf_op jit(solution)/shard_map/pallas_call | solution.py:133
  229.7 15.2 %shard_map.324 = (f32[64,8,640]{2,1,0:T(8,128)}, bf16[512,640]{1,0:T(8,128)(2,1)}, bf16[640,1152]{1,0:T(8,128)(2,1)}, bf16[640,1152]{1,0:T(8,128)(2,1)}, f32[8,640]{1,0:T(8,128)}, /*index=5*/f32[16,8,640]{2,1,0:T(8,128)}) custom-call(f32[64,8,640]{2,1,0:T(8,128)} %get-tuple-element.73.step_ref, bf16[512,104]{1,0:T(8,128)(2,1)} %copy-done.11, ...), custom_call_target="tpu_custom_call" | custom-call | flops 1000 | bytes 1000 | tf_op jit(solution)/shard_map/pallas_call | solution.py:973
  248.0 29.0 %shard_map.325.enter_ref = f32[16,8,640]{2,1,0:T(8,128)S(1)} custom-call(f32[16,8,640]{2,1,0:T(8,128)S(1)} %copy-done.25, f32[8,640]{1,0:T(8,128)S(1)} %copy-done.34, f32[16,640]{1,0:T(8,128)S(1)} %copy-done.13), custom_call_target="tpu_custom_call" | custom-call | tf_op jit(solution)/shard_map/pallas_call | solution.py:465
  277.7 30.5 %shard_map.326 = (f32[64,8,640]{2,1,0:T(8,128)}, f32[16,8,640]{2,1,0:T(8,128)}, f32[8,640]{1,0:T(8,128)}, f32[104,640]{1,0:T(8,128)}, bf16[512,104]{1,0:T(8,128)(2,1)}) custom-call(f32[64,8,640]{2,1,0:T(8,128)} %get-tuple-element.73.step_ref, f32[64,8,640]{2,1,0:T(8,128)} %get-tuple-element.74.drive_ref, f32[64,8,640]{2,1,0:T(8,128)} %get-tuple-element.86.grad_y_ref, ...), custom_call_target="tpu_custom_call" | custom-call | flops 1000 | bytes 1000 | tf_op jit(solution)/shard_map/pallas_call | solution.py:973
  309.2 6.5 %shard_map.327 = f32[512,104]{1,0:T(8,128)S(1)} custom-call(bf16[512,104]{1,0:T(8,128)(2,1)S(1)} %copy-done.31), custom_call_target="tpu_custom_call" | custom-call | tf_op jit(solution)/shard_map/pallas_call | solution.py:198
  316.3 6.6 %shard_map.328 = (f32[64,8,640]{2,1,0:T(8,128)}, f32[3,8,640]{2,1,0:T(8,128)}, f32[104,640]{1,0:T(8,128)}, f32[5,8,640]{2,1,0:T(8,128)}) custom-call(bf16[512,104]{1,0:T(8,128)(2,1)} %convert_element_type.277.grad_mapped_ref, f32[64,8,640]{2,1,0:T(8,128)} %get-tuple-element.86.grad_y_ref, f32[64,8,640]{2,1,0:T(8,128)} %get-tuple-element.91.side_ref, ...), custom_call_target="tpu_custom_call" | custom-call | flops 1000 | bytes 1000 | tf_op jit(solution)/shard_map/pallas_call | solution.py:973
  332.0 10.1 %shard_map.329 = (bf16[640,1152]{1,0:T(8,128)(2,1)}, bf16[512,1152]{1,0:T(8,128)(2,1)S(1)}, f32[1,1152]{1,0:T(1,128)S(1)}) custom-call(bf16[4,128,1152]{2,1,0:T(8,128)(2,1)S(1)} %copy-done.3, f32[64,8,640]{2,1,0:T(8,128)S(1)} %copy-done.17, f32[3,8,640]{2,1,0:T(8,128)S(1)} %copy-done.36, bf16[512,640]{1,0:T(8,128)(2,1)S(1)} %copy-done.24, ...), custom_call_target="tpu_custom_call" | custom-call | tf_op jit(solution)/shard_map/pallas_call | solution.py:944
  343.5 55.3 %shard_map.330 = (f32[128,1152]{1,0:T(8,128)S(1)}, bf16[80,1152]{1,0:T(8,128)(2,1)S(1)}, bf16[32,640]{1,0:T(8,128)(2,1)S(1)}, f32[8,8,640]{2,1,0:T(8,128)S(1)}, ...) custom-call(bf16[4,128,1152]{2,1,0:T(8,128)(2,1)S(1)} %bitcast.117, ...), custom_call_target="tpu_custom_call" | custom-call | tf_op jit(solution)/shard_map/pallas_call | solution.py:322
  404.7 36.3 %shard_map.331 = (bf16[8,80,1152]{2,1,0:T(8,128)(2,1)S(1)}, bf16[4,128,1152]{2,1,0:T(8,128)(2,1)S(1)}, bf16[4,128,1152]{2,1,0:T(8,128)(2,1)S(1)}, bf16[8,32,640]...) custom-call(bf16[80,1152]{1,0:T(8,128)(2,1)S(1)} %copy-done.29, ...), custom_call_target="tpu_custom_call" | custom-call | tf_op jit(solution)/shard_map/pallas_call | solution.py:133
  454.7 5.6 %convolution_bitcast_fusion = f32[1,768,1152]{2,1,0:T(8,128)} fusion(bf16[4,256,768]{2,1,0:T(8,128)(2,1)} %copy-done.14, bf16[4,256,1152]{2,1,0:T(8,128)(2,1)S(1)} %copy-done.10), kind=kOutput, calls=%fused_computation.12 | convolution fusion | flops 1811939328 | bytes 7471104 | tf_op jit(solution)/shard_map/dot_general | solution.py:537
  460.3 3.9 convolution_bitcast_fusion.1
  467.8 2.7 convert_bitcast_fusion
  (236 shorter events, 84.4 us)
Async XLA Ops:
  7.2 144.5 %copy-start = (bf16[1152,8]{0,1:T(8,128)(2,1)S(1)}, bf16[1152,8]{0,1:T(8,128)(2,1)}, u32[]{:S(2)}) copy-start(bf16[1152,8]{0,1:T(8,128)(2,1)} %param.35) | copy-start | bytes 55300
  7.2 6.4 %copy-start.58 = (bf16[72,576]{1,0:T(8,128)(2,1)S(1)}, bf16[72,576]{1,0:T(8,128)(2,1)}, u32[]{:S(2)}) copy-start(bf16[72,576]{1,0:T(8,128)(2,1)} %param.29) | copy-start | bytes 248836
  7.2 7.1 %copy-start.65 = (f32[576]{0:T(1024)S(1)}, f32[576]{0:T(1024)}, u32[]{:S(2)}) copy-start(f32[576]{0:T(1024)} %param.30) | copy-start | bytes 6916
  7.2 8.3 %copy-start.55 = (bf16[576,1152]{1,0:T(8,128)(2,1)S(1)}, bf16[576,1152]{1,0:T(8,128)(2,1)}, u32[]{:S(2)}) copy-start(bf16[576,1152]{1,0:T(8,128)(2,1)} %param.33) | copy-start | bytes 3981316
  7.2 457.1 %all-reduce.16.cloned.1.call-start = ((), (), s32[]{:S(2)}) async-start(), calls=%async_computation | async-start | bytes 5898240 | tf_op jit(solution)/shard_map/psum | solution.py:1253
  9.8 7.7 %copy-start.7 = (f32[64,8,8]{2,1,0:T(8,128)}, f32[64,8,8]{2,1,0:T(8,128)S(1)}, u32[]{:S(2)}) copy-start(f32[64,8,8]{2,1,0:T(8,128)S(1)} %convert_element_type.259.valid_ref) | copy-start | bytes 49156
  10.5 7.0 %copy-start.32 = (f32[4,640]{1,0:T(4,128)}, f32[4,640]{1,0:T(4,128)S(1)}, u32[]{:S(2)}) copy-start(f32[4,640]{1,0:T(4,128)S(1)} %pad_convert_fusion.taps_ref) | copy-start | bytes 30724
  13.6 20.4 %copy-start.18 = (bf16[104,640]{1,0:T(8,128)(2,1)}, bf16[104,640]{1,0:T(8,128)(2,1)S(1)}, u32[]{:S(2)}) copy-start(bf16[104,640]{1,0:T(8,128)(2,1)S(1)} %pad.58.xproj_ref) | copy-start | bytes 399364
  37.8 9.6 %copy-start.12 = (f32[16,640]{1,0:T(8,128)S(1)}, f32[16,640]{1,0:T(8,128)}, u32[]{:S(2)}) copy-start(f32[16,640]{1,0:T(8,128)} %pad.62.rate_ref.refs_2_) | copy-start | bytes 122884
  61.4 30.6 %copy-start.64 = (bf16[1152]{0:T(1024)(128)(2,1)S(1)}, bf16[1152]{0:T(1024)(128)(2,1)}, u32[]{:S(2)}) copy-start(bf16[1152]{0:T(1024)(128)(2,1)} %param.34) | copy-start | bytes 6916
  78.6 12.2 %copy-start.62 = (s32[4]{0:T(128)S(1)}, s32[4]{0:T(128)}, u32[]{:S(2)}) copy-start(s32[4]{0:T(128)} %param.21) | copy-start | bytes 52
  94.0 56.2 %copy-start.48 = (bf16[128,1152]{1,0:T(8,128)(2,1)}, bf16[128,1152]{1,0:T(8,128)(2,1)S(1)}, u32[]{:S(2)}) copy-start(bf16[128,1152]{1,0:T(8,128)(2,1)S(1)} %multiply_convert_fusion.2) | copy-start | bytes 884740
  159.5 25.2 %copy-start.67 = (f32[256,3072]{1,0:T(8,128)S(1)}, f32[256,3072]{1,0:T(8,128)}, u32[]{:S(2)}) copy-start(f32[256,3072]{1,0:T(8,128)} %get-tuple-element.154) | copy-start | bytes 9437188
  161.2 29.1 %slice-start = ((s8[7077888]{0:T(1024)(128)(4,1)}), s8[4194304]{0:T(1024)(128)(4,1)S(1)}, s32[]{:S(2)}) async-start(s8[7077888]{0:T(1024)(128)(4,1)} %bitcast.142), calls=%async_computation.1 | async-start | bytes 8388608
  184.7 5.7 %slice-start.1 = ((s8[7077888]{0:T(1024)(128)(4,1)}), s8[2883584]{0:T(1024)(128)(4,1)S(1)}, s32[]{:S(2)}) async-start(s8[7077888]{0:T(1024)(128)(4,1)} %bitcast.142), calls=%async_computation.2 | async-start | bytes 5767168
  190.4 21.3 %copy-start.51 = (f32[128,1152]{1,0:T(8,128)S(1)}, f32[128,1152]{1,0:T(8,128)}, u32[]{:S(2)}) copy-start(f32[128,1152]{1,0:T(8,128)} %get-tuple-element.157) | copy-start | bytes 1769476
  192.6 19.1 %copy-start.47 = (f32[128,1152]{1,0:T(8,128)S(1)}, f32[128,1152]{1,0:T(8,128)}, u32[]{:S(2)}) copy-start(f32[128,1152]{1,0:T(8,128)} %get-tuple-element.137) | copy-start | bytes 1769476
  192.6 21.0 %copy-start.49 = (bf16[128,1152]{1,0:T(8,128)(2,1)S(1)}, bf16[128,1152]{1,0:T(8,128)(2,1)}, u32[]{:S(2)}) copy-start(bf16[128,1152]{1,0:T(8,128)(2,1)} %copy-done.48) | copy-start | bytes 884740
  316.3 6.6 %copy-start.57 = (f32[16,8,640]{2,1,0:T(8,128)S(1)}, f32[16,8,640]{2,1,0:T(8,128)}, u32[]{:S(2)}) copy-start(f32[16,8,640]{2,1,0:T(8,128)} %get-tuple-element.103) | copy-start | bytes 983044
  316.3 6.6 %copy-start.59 = (f32[8,640]{1,0:T(8,128)S(1)}, f32[8,640]{1,0:T(8,128)}, u32[]{:S(2)}) copy-start(f32[8,640]{1,0:T(8,128)} %get-tuple-element.102) | copy-start | bytes 61444
  316.3 6.6 %copy-start.60 = (f32[8,640]{1,0:T(8,128)S(1)}, f32[8,640]{1,0:T(8,128)}, u32[]{:S(2)}) copy-start(f32[8,640]{1,0:T(8,128)} %get-tuple-element.101) | copy-start | bytes 61444
  332.0 10.1 %copy-start.27 = (f32[128,128]{1,0:T(8,128)S(1)}, f32[128,128]{1,0:T(8,128)}, u32[]{:S(2)}) copy-start(f32[128,128]{1,0:T(8,128)} %pad.68) | copy-start | bytes 196612
  343.5 57.8 %copy-start.63 = (f32[128]{0:T(128)S(1)}, f32[128]{0:T(128)}, u32[]{:S(2)}) copy-start(f32[128]{0:T(128)} %get-tuple-element.161) | copy-start | bytes 1540
  442.8 11.9 %copy-start.10 = (bf16[4,256,1152]{2,1,0:T(8,128)(2,1)S(1)}, bf16[4,256,1152]{2,1,0:T(8,128)(2,1)}, u32[]{:S(2)}) copy-start(bf16[4,256,1152]{2,1,0:T(8,128)(2,1)} %copy-done.9) | copy-start | bytes 7077892
  (47 other events, 85.9 us)
Sparse Core Ops, SparseCore 0:
  245.1 154.2 all-reduce.15

commit v3 on v2

--- a/solution.py
+++ b/solution.py
@@ -1,5 +1,4 @@
 import functools
-import math
 
 import jax
 import jax.numpy as jnp
@@ -45,62 +44,94 @@
     return i
 
 
-def begin(item, x_ref, o_ref, own_sem, send_sem, recv_sem):
-    mode, axis, count = item
-    me = lax.axis_index(axis)
-
-    def remote(source, row, slot, to):
-        return pltpu.make_async_remote_copy(
-            src_ref=source,
-            dst_ref=o_ref.at[row],
-            send_sem=send_sem.at[slot],
-            recv_sem=recv_sem.at[slot],
-            device_id={axis: to},
-            device_id_type=MESH,
-        )
-
-    own = pltpu.make_async_copy(x_ref.at[me] if mode == "scatter" else x_ref, o_ref.at[me], own_sem)
-    copies, later = [], []
-    if mode in ("gather", "scatter"):
-        for mask in range(count - 1, 0, -1):
-            to = flipped(me, mask)
-            copies.append(remote(x_ref.at[to] if mode == "scatter" else x_ref, me, mask - 1, to))
-    else:
+def order_of(groups):
+    masks, low, high = [], 1, groups - 1
+    while low <= high:
+        masks += [high] if low == high else [high, low]
+        low, high = low + 1, high - 1
+    return masks
+
+
+class Riders:
+    def __init__(self, items, xs, outs, sems):
+        self.own, self.copies, self.chains = [], [], {}
+        for i, item in enumerate(items):
+            self.add(item, xs[i], outs[i], *sems[3 * i : 3 * i + 3])
+        self.at = {axis: 0 for axis in self.chains}
+
+    def start(self):
+        for copy in self.copies + self.own:
+            copy.start()
+        for chain in self.chains.values():
+            for first, _ in chain[:2]:
+                first.start()
+        return self
+
+    def add(self, item, x_ref, o_ref, own_sem, send_sem, recv_sem):
+        mode, axis, count = item
+        me = lax.axis_index(axis)
+
+        def remote(source, row, slot, to):
+            return pltpu.make_async_remote_copy(
+                src_ref=source,
+                dst_ref=o_ref.at[row],
+                send_sem=send_sem.at[slot],
+                recv_sem=recv_sem.at[slot],
+                device_id={axis: to},
+                device_id_type=MESH,
+            )
+
+        source = x_ref.at[me] if mode == "scatter" else x_ref
+        self.own.append(pltpu.make_async_copy(source, o_ref.at[me], own_sem))
+        if mode in ("gather", "scatter"):
+            for mask in range(count - 1, 0, -1):
+                to = flipped(me, mask)
+                source = x_ref.at[to] if mode == "scatter" else x_ref
+                self.copies.append(remote(source, me, mask - 1, to))
+            return
         groups = count // mode
         side, place = lax.rem(me, mode), me // mode
         mates = [place * mode + lax.rem(side + j, mode) for j in range(1, mode)]
         slot = groups - 1
         for mate in mates:
-            copies.append(remote(x_ref, me, slot, mate))
+            self.copies.append(remote(x_ref, me, slot, mate))
             slot += 1
-        for mask in range(groups - 1, 0, -1):
+        chain = self.chains.setdefault(axis, [])
+        for mask in order_of(groups):
             row = flipped(place, mask) * mode + side
             first = remote(x_ref, me, mask - 1, row)
             passed = []
             for mate in mates:
                 passed.append(remote(o_ref.at[row], row, slot, mate))
                 slot += 1
-            later.append((first, passed))
-    for copy in [first for first, _ in later] + copies:
-        copy.start()
-    own.start()
-    return own, copies, later
-
-
-def finish(under_way):
-    for _, _, later in under_way:
-        for first, passed in later:
+            chain.append((first, passed))
+
+    def left(self):
+        return max([len(chain) - self.at[axis] for axis, chain in self.chains.items()] + [0])
+
+    def step(self):
+        for axis, chain in self.chains.items():
+            i = self.at[axis]
+            if i == len(chain):
+                continue
+            self.at[axis] = i + 1
+            first, passed = chain[i]
             first.wait_recv()
-            for second in passed:
-                second.start()
-    for own, copies, later in under_way:
-        own.wait()
-        for copy in copies:
+            for copy in passed:
+                copy.start()
+            if i + 2 < len(chain):
+                chain[i + 2][0].start()
+
+    def finish(self):
+        while self.left():
+            self.step()
+        for copy in self.own + self.copies:
             copy.wait()
-        for first, passed in later:
-            first.wait_send()
-            for second in passed:
-                second.wait()
+        for chain in self.chains.values():
+            for first, passed in chain:
+                first.wait_send()
+                for copy in passed:
+                    copy.wait()
 
 
 def items_of(exchanges):
@@ -120,12 +151,7 @@
     number = len(items)
     sems = refs[2 * number :]
     pl.semaphore_wait(pltpu.get_barrier_semaphore(), greet(axes_of(items)))
-    finish(
-        [
-            begin(item, refs[i], refs[number + i], *sems[3 * i : 3 * i + 3])
-            for i, item in enumerate(items)
-        ]
-    )
+    Riders(items, refs[:number], refs[number : 2 * number], sems).start().finish()
 
 
 def exchange(number, *exchanges):
@@ -221,7 +247,7 @@
         side, place = lax.rem(me, size), me // size
         self.rows, self.near, self.far = [], [], []
         for k in range(self.groups):
-            group = flipped(place, self.groups - 1 - k)
+            group = flipped(place, (order_of(self.groups) + [0])[k])
             self.rows.append(group * size + side)
             self.near.append(
                 [
@@ -248,25 +274,28 @@
                     )
                 )
 
-    def begin(self):
-        for copies in self.near:
-            for copy in copies:
-                copy.start()
-
-    def near_sum(self, k):
+    def begin(self, k):
+        for copy in self.near[k]:
+            copy.start()
+
+    def near_sum(self, k, wait=True):
         total = self.x[self.rows[k]].astype(f32)
         for j, copy in enumerate(self.near[k]):
-            copy.wait_recv()
+            if wait:
+                copy.wait_recv()
             total = total + self.near_in[k, j].astype(f32)
         return total
 
-    def pass_on(self):
-        for k, copy in enumerate(self.far):
+    def pass_on(self, k):
+        if k < self.groups - 1:
             self.pairs[k] = self.near_sum(k).astype(bf16)
-            copy.start()
+            self.far[k].start()
+        else:
+            for copy in self.near[k]:
+                copy.wait_recv()
 
     def total(self):
-        total = self.near_sum(self.groups - 1)
+        total = self.near_sum(self.groups - 1, False)
         for k, copy in enumerate(self.far):
             copy.wait_recv()
             total = total + self.far_in[k].astype(f32)
@@ -290,16 +319,27 @@
     tasks = [Share(axis, count, size, x, *take(7)) for (axis, count, size), x in zip(shares, xs)]
     axes = set(axes_of(items)) | {(axis, count) for axis, count, _ in shares}
     pl.semaphore_wait(pltpu.get_barrier_semaphore(), greet(sorted(axes)))
-    for task in tasks:
-        task.begin()
-    under_way = [begin(item, riders[i], rider_outs[i], *take(3)) for i, item in enumerate(items)]
-    for task in tasks:
-        task.pass_on()
+    turns = {}
+    for (axis, _, _), task in zip(shares, tasks):
+        turns.setdefault(axis, []).extend((task, k) for k in range(task.groups))
+    for turn in turns.values():
+        for task, k in turn[:2]:
+            task.begin(k)
+    under_way = Riders(items, riders, rider_outs, take(3 * number)).start()
+    for i in range(max(len(turn) for turn in turns.values())):
+        for turn in turns.values():
+            if i < len(turn):
+                task, k = turn[i]
+                task.pass_on(k)
+                if i + 2 < len(turn):
+                    task, k = turn[i + 2]
+                    task.begin(k)
+        under_way.step()
     for task, out in zip(tasks, outs):
         out[...] = task.total().astype(out.dtype)
     for task in tasks:
         task.close()
-    finish(under_way)
+    under_way.finish()
 
 
 def share_of(number, shares, *exchanges):
@@ -308,17 +348,7 @@
     held = [pl.BlockSpec(memory_space=pltpu.VMEM)] * len(shares)
     scratch = []
     for x, axis, size, _ in shares:
-        groups = lax.axis_size(axis) // size
-        part = x.shape[1:]
-        scratch += [
-            pltpu.VMEM((groups, size - 1) + part, bf16),
-            pltpu.VMEM((groups - 1,) + part, bf16),
-            pltpu.VMEM((groups - 1,) + part, bf16),
-            pltpu.SemaphoreType.DMA((groups, size - 1)),
-            pltpu.SemaphoreType.DMA((groups, size - 1)),
-            pltpu.SemaphoreType.DMA((groups - 1,)),
-            pltpu.SemaphoreType.DMA((groups - 1,)),
-        ]
+        scratch += share_scratch(x, axis, size)
     return pl.pallas_call(
         functools.partial(
             share_kernel, [(axis, lax.axis_size(axis), size) for _, axis, size, _ in shares], items
@@ -388,9 +418,7 @@
         enter[j] = jnp.zeros((rows, width), f32)
 
     pl.semaphore_wait(barrier, greeted)
-    under_way = [
-        begin(item, xs[i], outs[i], *sems[3 * i : 3 * i + 3]) for i, item in enumerate(items)
-    ]
+    under_way = Riders(items, xs, outs, sems).start()
     sums_total = sums_both
     sums_enter = jnp.zeros((rows, width), f32)
     for turn, span in enumerate(spans):
@@ -453,7 +481,7 @@
         low, high = (inner, outer) if back else (outer, inner)
         o_ref[2 * j] = jnp.where(upper, turned(high), low)
         o_ref[2 * j + 1] = jnp.where(upper, high, turned(low))
-    finish(under_way)
+    under_way.finish()
 
 
 def carried(local, sums, rate, axis, back, number, *exchanges):
@@ -790,20 +818,57 @@
         last_ref[n] = held[n]
 
 
-def back_kernel(rank, step_ref, drive_ref, grad_y_ref, mapped_ref, rate_ref, first_ref, state_ref, enter_ref, dt_ref, pre_ref,
-                dtw_ref, side_ref, log_ref, bias_ref, grad_dtw_ref, low_ref,
-                wide_in, wide_read, sum_in, sum_read, to_input, to_decay, total):
+def back_kernel(rank, pieces, shares, items, step_ref, drive_ref, grad_y_ref, mapped_ref, rate_ref, first_ref, state_ref, enter_ref, dt_ref,
+                pre_ref, dtw_ref, *refs):
+    many, number = len(shares), len(items)
+    at = 0
+
+    def take(k):
+        nonlocal at
+        at += k
+        return refs[at - k : at]
+
+    xs, riders = take(many), take(number)
+    side_ref, log_ref, bias_ref, grad_dtw_ref, low_ref = take(5)
+    parts, rider_outs = take(many), take(number)
+    wide_in, wide_read, sum_in, sum_read, to_input, to_decay, total = take(7)
     count, steps, rows, lanes = wide_in.shape
-    place = pl.program_id(0)
+    place, tiles = pl.program_id(0), pl.num_programs(0)
+    kept, kept_sem = take(many), take(1)[0]
+    tasks = [Share(*share, held, *take(7)) for share, held in zip(shares, kept)]
+    under_way = Riders(items, riders, rider_outs, take(3 * number))
+    turn = [(task, k) for task in tasks for k in range(task.groups)]
 
     @pl.when(place == 0)
     def _():
+        copies = [
+            pltpu.make_async_copy(x, held, kept_sem.at[i]) for i, (x, held) in enumerate(zip(xs, kept))
+        ]
+        for copy in copies:
+            copy.start()
+        axes = {share[:2] for share in shares} | set(axes_of(items))
+        pl.semaphore_wait(pltpu.get_barrier_semaphore(), greet(sorted(axes)))
+        for copy in copies:
+            copy.wait()
+        for task, k in turn[:2]:
+            task.begin(k)
+        under_way.start()
         spread(mapped_ref, rank, wide_in)
         spread(mapped_ref, rank + count, wide_read)
         sum_in[...] = jnp.zeros_like(sum_in)
         sum_read[...] = jnp.zeros_like(sum_read)
         total[...] = jnp.zeros_like(total)
 
+    each = -(-len(turn) // (pieces - 1))
+    for piece in range(1, pieces):
+
+        @pl.when(place == piece)
+        def _():
+            for i in range((piece - 1) * each, min(piece * each, len(turn))):
+                turn[i][0].pass_on(turn[i][1])
+                if i + 2 < len(turn):
+                    turn[i + 2][0].begin(turn[i + 2][1])
+
     rates = [rows_of(rate_ref, n, rows) for n in range(count)]
     for n in range(count):
         log_ref[n] = jnp.zeros((rows, lanes), f32)
@@ -812,7 +877,7 @@
         step, drive, grad_y = step_ref[p], drive_ref[p], grad_y_ref[p]
         inputs = jnp.zeros((rows, lanes), f32)
         decays = jnp.zeros((rows, lanes), f32)
-        new = []
+        new, grads = [], []
         for n in range(count):
             grad = grad_y * wide_read[n, p] + carry[n]
             passed = jnp.exp2(step * rates[n]) * grad
@@ -821,17 +886,20 @@
             decays = decays + grad_decay * rates[n]
             log_ref[n] += grad_decay * step
             inputs = inputs + grad * wide_in[n, p]
-            sum_in[n, p] += grad * drive
-            sum_read[n, p] += grad_y * state_ref[p, n]
+            grads.append(grad)
         to_input[p] = inputs
         to_decay[p] = decays
+        grads = jnp.concatenate(grads, axis=0).astype(bf16)
+        held_states = state_ref[p].reshape(count * rows, lanes).astype(bf16)
+        sum_in[p] += dot_nt(drive.astype(bf16), grads)
+        sum_read[p] += dot_nt(grad_y.astype(bf16), held_states)
         return tuple(new)
 
     def one(turn, carry):
         p = steps - 1 - turn
         return step_back(p, carry, lambda n: state_ref[p - 1, n])
 
-    carry = lax.fori_loop(0, steps - 1, one, tuple(enter_ref[n] for n in range(count)))
+    carry = lax.fori_loop(0, steps - 1, one, tuple(enter_ref[n] for n in range(count)), unroll=7 if (steps - 1) % 7 == 0 else 1)
     step_back(0, carry, lambda n: first_ref[n])
     dt_pre, pre = dt_ref[...], pre_ref[...]
     inputs = to_input[...]
@@ -843,15 +911,23 @@
     grad_dtw_ref[...] = dot_tn(mapped_ref[...], grad_dt)
     total[...] += dot_nt(grad_dt, dtw_ref[...])
 
-    @pl.when(place == pl.num_programs(0) - 1)
-    def _():
-        column = lax.broadcasted_iota(jnp.int32, (lanes, total.shape[1]), 1)
+    @pl.when(place == tiles - 1)
+    def _():
+        wide = count * rows
+        line = lax.broadcasted_iota(jnp.int32, (steps * rows, wide), 0) % rows
+        lane = lax.broadcasted_iota(jnp.int32, (steps * rows, wide), 1)
+        state = lax.broadcasted_iota(jnp.int32, (wide, total.shape[1]), 0) // rows
+        column = lax.broadcasted_iota(jnp.int32, (wide, total.shape[1]), 1)
         sums = total[...]
         for which, source in enumerate((sum_in, sum_read)):
-            for n in range(count):
-                pick = (column == rank + which * count + n).astype(bf16)
-                sums = sums + dot(source[n].reshape(steps * rows, lanes).astype(bf16), pick)
+            values = jnp.where(lane % rows == line, source[...].reshape(steps * rows, wide), 0.0)
+            pick = (column == rank + which * count + state).astype(bf16)
+            sums = sums + dot(values.astype(bf16), pick)
         low_ref[...] = sums.astype(bf16)
+        for task, part in zip(tasks, parts):
+            part[...] = task.total().astype(bf16)
+            task.close()
+        under_way.finish()
 
 
 def conv_back_kernel(taps, grad_mapped_ref, grad_y_ref, side_ref, pre_ref, ext_ref, skip_ref, xproj_ref, taps_ref, valid_ref,
@@ -879,24 +955,17 @@
     grad_ref[...] = ext_grad[pl.ds(rim, steps)]
 
 
-def ends_kernel(count, tokens_ref, grad_ref, rim_ref, grad_z_ref, normed_ref, w_ref, grad_conv_ref, part_ref, gain_ref,
-                came, send_sem, recv_sem):
+def ends_kernel(count, items, tokens_ref, grad_ref, rim_ref, grad_z_ref, normed_ref, w_ref, *refs):
+    number = len(items)
+    xs, refs = refs[:number], refs[number:]
+    grad_conv_ref, part_ref, gain_ref = refs[:3]
+    outs, (came, send_sem, recv_sem), sems = refs[3 : 3 + number], refs[3 + number : 6 + number], refs[6 + number :]
     steps, lines, full = grad_ref.shape
     seqs, group, width = tokens_ref.shape
     rows, inner, rim = steps * lines, w_ref.shape[1], rim_ref.shape[0]
     here = lax.axis_index("seq")
-    barrier = pltpu.get_barrier_semaphore()
-    told = 0
-    for by in (1, -1):
-        there = here + by
-        near = (there >= 0) & (there < count)
-        told = told + jnp.where(near, 1, 0)
-
-        @pl.when(near)
-        def _():
-            pl.semaphore_signal(barrier, inc=1, device_id={"seq": there}, device_id_type=MESH)
-
-    pl.semaphore_wait(barrier, told)
+    told = greet(sorted({("seq", count)} | set(axes_of(items))))
+    pl.semaphore_wait(pltpu.get_barrier_semaphore(), told)
     edge = pltpu.make_async_remote_copy(
         src_ref=rim_ref,
         dst_ref=came,
@@ -910,6 +979,7 @@
     def _():
         edge.start()
 
+    under_way = Riders(items, xs, outs, sems).start()
     unit = unit_of(tokens_ref[...].reshape(rows, width).astype(f32))
     by_gate = dot(grad_z_ref[:, pl.ds(0, inner)], w_ref[1])
 
@@ -927,38 +997,207 @@
     ]
     grad = jnp.concatenate([grad_ref[pl.ds(0, steps - rim)]] + last, axis=0)
     grad = grad.reshape(rows, full).astype(bf16)
+    under_way.step()
     grad_conv_ref[...] = dot_tn(grad, normed_ref[...]).astype(bf16)
+    under_way.step()
     part = (dot(grad[:, :inner], w_ref[0]) + by_gate).astype(bf16)
     part = dot_tn(perm_of(steps, lines, seqs), part)
     part_ref[...] = part.astype(bf16)
     gain_ref[...] = jnp.sum(part * unit, axis=0, keepdims=True)
+    under_way.finish()
 
     @pl.when(here > 0)
     def _():
         edge.wait_send()
 
 
-def ends(tokens, grad, rim, grad_z, normed, w_in, number):
+def ends(tokens, grad, rim, grad_z, normed, w_in, number, *exchanges):
     steps, lines, full = grad.shape
     rows, width = normed.shape
+    items = items_of(exchanges)
+    anywhere = [pl.BlockSpec(memory_space=pl.ANY)] * len(items)
     return pl.pallas_call(
-        functools.partial(ends_kernel, lax.axis_size("seq")),
+        functools.partial(ends_kernel, lax.axis_size("seq"), items),
         out_shape=[
             jax.ShapeDtypeStruct((full, width), bf16),
             jax.ShapeDtypeStruct((rows, width), bf16),
             jax.ShapeDtypeStruct((1, width), f32),
-        ],
-        in_specs=[pl.BlockSpec(memory_space=pltpu.VMEM)] * 6,
-        out_specs=[pl.BlockSpec(memory_space=pltpu.VMEM)] * 3,
+        ]
+        + [landed(x, item) for (x, _, _), item in zip(exchanges, items)],
+        in_specs=[pl.BlockSpec(memory_space=pltpu.VMEM)] * 6 + anywhere,
+        out_specs=[pl.BlockSpec(memory_space=pltpu.VMEM)] * 3 + anywhere,
         scratch_shapes=[
             pltpu.VMEM(rim.shape, f32),
             pltpu.SemaphoreType.DMA,
             pltpu.SemaphoreType.DMA,
-        ],
+        ]
+        + [sem for item in items for sem in sems_of(item)],
         compiler_params=pltpu.CompilerParams(
             collective_id=number, has_side_effects=True, vmem_limit_bytes=48 * MIB
         ),
-    )(tokens, grad, rim, grad_z, normed, w_in)
+    )(tokens, grad, rim, grad_z, normed, w_in, *[x for x, _, _ in exchanges])
+
+
+def hits_of(routes, experts, part, most, slots):
+    rows = routes.shape[0]
+    chosen = (lax.broadcasted_iota(jnp.int32, (rows, experts), 1) == routes).astype(f32)
+    row = lax.broadcasted_iota(jnp.int32, (rows, rows), 0)
+    other = lax.broadcasted_iota(jnp.int32, (rows, rows), 1)
+    earlier = (other < row) & (row // part == other // part)
+    ranks = jnp.sum(dot(earlier.astype(bf16), chosen.astype(bf16)) * chosen, axis=1, keepdims=True)
+    slot = lax.broadcasted_iota(jnp.int32, (rows, 1), 0) // part * most + ranks.astype(jnp.int32)
+    column = lax.broadcasted_iota(jnp.int32, (rows, experts * slots), 1)
+    return chosen, (column == routes * slots + slot).astype(bf16)
+
+
+def route_kernel(part, most, slots, tokens_ref, mixed_ref, gain_ref, routes_ref, router_ref,
+                 hidden_ref, normed_ref, probs_ref, chosen_ref, hit_ref, packed_ref):
+    hidden = tokens_ref[...].astype(f32) + mixed_ref[...]
+    hidden_ref[...] = hidden
+    normed = (unit_of(hidden) * gain_ref[...]).astype(bf16)
+    normed_ref[...] = normed
+    logits = dot_nt(normed, router_ref[...])
+    raised = jnp.exp(logits - jnp.max(logits, axis=1, keepdims=True))
+    probs_ref[...] = raised / jnp.sum(raised, axis=1, keepdims=True)
+    chosen, hit = hits_of(routes_ref[...], router_ref.shape[0], part, most, slots)
+    chosen_ref[...] = chosen
+    hit_ref[...] = hit
+    packed_ref[...] = dot_tn(hit, normed).astype(bf16)
+
+
+def loss_kernel(group, lengths_ref, came_ref, back_ref, hit_ref, hidden_ref, probs_ref, chosen_ref, teacher_ref,
+                layer_ref, grad_layer_ref, grad_logit_ref, loss_ref, packed_ref):
+    rows, width = hidden_ref.shape
+    seqs = lengths_ref.shape[0]
+    expert = dot(back_ref[...], came_ref[...])
+    probs, chosen = probs_ref[...], chosen_ref[...]
+    gate = jnp.sum(probs * chosen, axis=1, keepdims=True)
+    layer = hidden_ref[...] + gate * expert
+    layer_ref[...] = layer.astype(bf16)
+    flat_row = lax.axis_index("chan") * rows + lax.broadcasted_iota(jnp.int32, (rows, 1), 0)
+    length = jnp.zeros((rows, 1), jnp.int32)
+    total = 0
+    for s in range(seqs):
+        length = jnp.where(flat_row // group == s, lengths_ref[s], length)
+        total = total + lengths_ref[s]
+    scale = 1.0 / jnp.broadcast_to(total, (rows, 1)).astype(f32)
+    at = lax.axis_index("seq") * group + flat_row % group
+    mask = jnp.where(at < length, scale, 0.0)
+    error = layer - teacher_ref[...].astype(f32)
+    scaled = mask * error
+    lost = jnp.sum(scaled * error, axis=0, keepdims=True)
+    loss_ref[...] = jnp.broadcast_to(jnp.sum(lost, axis=1, keepdims=True), (1, width))
+    grad_layer = 2.0 * scaled
+    grad_layer_ref[...] = grad_layer
+    grad_gate = jnp.sum(grad_layer * expert, axis=1, keepdims=True)
+    grad_logit_ref[...] = grad_gate * gate * (chosen - probs)
+    packed_ref[...] = dot_tn(hit_ref[...], (gate * grad_layer).astype(bf16)).astype(bf16)
+
+
+def norm_back_kernel(came_ref, back_ref, grad_logit_ref, router_ref, normed_ref, hidden_ref, grad_layer_ref, gain_ref, loss_ref,
+                     grad_ref, low_ref, shared_ref):
+    experts = router_ref.shape[0]
+    grad_logit = grad_logit_ref[...].astype(bf16)
+    grad_normed = dot(back_ref[...], came_ref[...]) + dot(grad_logit, router_ref[...])
+    hidden = hidden_ref[...]
+    inverse = lax.rsqrt(jnp.mean(hidden * hidden, axis=1, keepdims=True) + epsilon)
+    unit = hidden * inverse
+    shared_ref[...] = jnp.zeros_like(shared_ref)
+    shared_ref[pl.ds(0, experts), :] = dot_tn(grad_logit, normed_ref[...])
+    shared_ref[pl.ds(experts, 1), :] = jnp.sum(grad_normed * unit, axis=0, keepdims=True)
+    shared_ref[pl.ds(experts + 1, 1), :] = loss_ref[...]
+    grad = grad_layer_ref[...] + norm_back(grad_normed, unit, inverse, gain_ref[...])
+    grad_ref[...] = grad
+    low_ref[...] = grad.astype(bf16)
+
+
+def at_once(kernel, ins, outs, scalars=0):
+    spaces = [pltpu.SMEM] * scalars + [pltpu.VMEM] * (len(ins) - scalars)
+    return pl.pallas_call(
+        kernel,
+        in_specs=[pl.BlockSpec(memory_space=space) for space in spaces],
+        out_specs=[pl.BlockSpec(memory_space=pltpu.VMEM)] * len(outs),
+        out_shape=[jax.ShapeDtypeStruct(shape, dtype) for shape, dtype in outs],
+        compiler_params=pltpu.CompilerParams(vmem_limit_bytes=32 * MIB),
+        cost_estimate=pl.CostEstimate(flops=1000, bytes_accessed=1000, transcendentals=0),
+    )(*ins)
+
+
+def expert_kernel(x_ref, first_ref, second_ref, hidden_ref, slope_ref, result_ref, total):
+    place = pl.program_id(0)
+
+    @pl.when(place == 0)
+    def _():
+        total[...] = jnp.zeros_like(total)
+
+    pre = dot(x_ref[...], first_ref[...])
+    cdf = 0.5 * (1.0 + lax.erf(pre * 0.7071067811865476))
+    hidden = (pre * cdf).astype(bf16)
+    hidden_ref[0] = hidden
+    slope = cdf + pre * (jnp.exp(-0.5 * pre * pre) * 0.3989422804014327)
+    slope_ref[...] = slope.astype(bf16)
+    total[...] += dot(hidden, second_ref[...])
+
+    @pl.when(place == pl.num_programs(0) - 1)
+    def _():
+        result_ref[...] = total[...].astype(bf16)
+
+
+def expert_back_kernel(grad_ref, first_ref, second_ref, slope_ref, grad_pre_ref, result_ref, total):
+    place = pl.program_id(0)
+
+    @pl.when(place == 0)
+    def _():
+        total[...] = jnp.zeros_like(total)
+
+    grad = dot_nt(grad_ref[...], second_ref[...]) * slope_ref[...].astype(f32)
+    grad = grad.astype(bf16)
+    grad_pre_ref[0] = grad
+    total[...] += dot_nt(grad, first_ref[...])
+
+    @pl.when(place == pl.num_programs(0) - 1)
+    def _():
+        result_ref[...] = total[...].astype(bf16)
+
+
+def expert(x, first, second, parts, slope=None):
+    rows, width = x.shape
+    units = first.shape[1] // parts
+    tile = next((t for t in (768, 384, 256, 128) if units % t == 0), None)
+    low = jax.ShapeDtypeStruct((rows, width), bf16)
+    if tile is None:
+
+        def split(h):
+            return h.reshape(rows, parts, units).transpose(1, 0, 2)
+
+        if slope is not None:
+            grad = (dot_nt(x, second) * slope.astype(f32)).astype(bf16)
+            return split(grad), dot_nt(grad, first).astype(bf16)
+        pre = dot(x, first)
+        cdf = 0.5 * (1.0 + lax.erf(pre * 0.7071067811865476))
+        hidden = (pre * cdf).astype(bf16)
+        slope = cdf + pre * (jnp.exp(-0.5 * pre * pre) * 0.3989422804014327)
+        return split(hidden), slope.astype(bf16), dot(hidden, second).astype(bf16)
+    each = units // tile
+    columns = pl.BlockSpec((width, tile), lambda i: (0, i))
+    lines = pl.BlockSpec((tile, width), lambda i: (i, 0))
+    everything = pl.BlockSpec((rows, width), lambda i: (0, 0))
+    slopes = pl.BlockSpec((rows, tile), lambda i: (0, i))
+    hiddens = pl.BlockSpec((1, rows, tile), lambda i: (i // each, 0, i % each))
+    hidden_shape = jax.ShapeDtypeStruct((parts, rows, units), bf16)
+    back = slope is not None
+    return pl.pallas_call(
+        expert_back_kernel if back else expert_kernel,
+        grid=(parts * each,),
+        in_specs=[everything, columns, lines] + ([slopes] if back else []),
+        out_specs=[hiddens] + ([] if back else [slopes]) + [everything],
+        out_shape=[hidden_shape]
+        + ([] if back else [jax.ShapeDtypeStruct((rows, first.shape[1]), bf16)])
+        + [low],
+        scratch_shapes=[pltpu.VMEM((rows, width), f32)],
+        compiler_params=pltpu.CompilerParams(vmem_limit_bytes=60 * MIB),
+        cost_estimate=pl.CostEstimate(flops=1000, bytes_accessed=1000, transcendentals=0),
+    )(x, first, second, *([slope] if back else []))
 
 
 def block_of(shape, kind):
@@ -966,41 +1205,36 @@
         return pl.BlockSpec(shape[:-1] + (LANES,), lambda i: (0,) * (len(shape) - 1) + (i,))
     if kind == "rows":
         return pl.BlockSpec((LANES,) + shape[1:], lambda i: (i,) + (0,) * (len(shape) - 1))
+    if kind == "any":
+        return pl.BlockSpec(memory_space=pl.ANY)
     return pl.BlockSpec(shape, lambda i: (0,) * len(shape))
 
 
-def by_tiles(kernel, full, ins, outs, scratch):
+def share_scratch(x, axis, size):
+    groups = lax.axis_size(axis) // size
+    part = x.shape[1:]
+    return [
+        pltpu.VMEM((groups, size - 1) + part, bf16),
+        pltpu.VMEM((groups - 1,) + part, bf16),
+        pltpu.VMEM((groups - 1,) + part, bf16),
+        pltpu.SemaphoreType.DMA((groups, size - 1)),
+        pltpu.SemaphoreType.DMA((groups, size - 1)),
+        pltpu.SemaphoreType.DMA((groups - 1,)),
+        pltpu.SemaphoreType.DMA((groups - 1,)),
+    ]
+
+
+def by_tiles(kernel, full, ins, outs, scratch, more=(), params=None):
     return pl.pallas_call(
         kernel,
         grid=(full // LANES,),
         in_specs=[block_of(a.shape, kind) for a, kind in ins],
         out_specs=[block_of(shape, kind) for shape, _, kind in outs],
         out_shape=[jax.ShapeDtypeStruct(shape, dtype) for shape, dtype, _ in outs],
-        scratch_shapes=[pltpu.VMEM(shape, dtype) for shape, dtype in scratch],
-        compiler_params=pltpu.CompilerParams(vmem_limit_bytes=58 * MIB),
+        scratch_shapes=[pltpu.VMEM(shape, dtype) for shape, dtype in scratch] + list(more),
+        compiler_params=pltpu.CompilerParams(vmem_limit_bytes=58 * MIB, **(params or {})),
         cost_estimate=pl.CostEstimate(flops=1000, bytes_accessed=1000, transcendentals=0),
     )(*[a for a, _ in ins])
-
-
-def packed_size(arrays, rows):
-    total = -(-sum(a.size for a in arrays) // LANES)
-    return -(-total // rows) * rows
-
-
-def packed_rows(arrays, rows):
-    total = packed_size(arrays, rows)
-    joined = jnp.concatenate([a.reshape(-1) for a in arrays])
-    return jnp.pad(joined, (0, total * LANES - joined.size)).reshape(total, LANES)
-
-
-def unpacked_rows(packed, shapes):
-    packed = packed.reshape(-1)
-    arrays, at = [], 0
-    for shape in shapes:
-        size = math.prod(shape)
-        arrays.append(packed[at : at + size].reshape(shape))
-        at += size
-    return arrays
 
 
 def norm_back(grad_normed, unit_rows, inverse, weight_gain):
@@ -1097,7 +1331,7 @@
         1,
     )
     act_shape, state_shape, wide_shape = (steps, lines, full), (states, lines, full), (states, steps, lines, LANES)
-    dt_pre, step_size, drive, last, sums = by_tiles(
+    dt_pre, step_size, drive, own_states, sums = by_tiles(
         functools.partial(totals_kernel, rank, taps),
         full,
         [
@@ -1117,7 +1351,7 @@
         ],
         [(wide_shape, f32)],
     )
-    (enter,) = carried(last, sums, rate_two, "seq", False, 2)
+    (enter,) = carried(own_states, sums, rate_two, "seq", False, 2)
     y_full, gated, state, out_part = by_tiles(
         functools.partial(states_kernel, rank, seqs),
         full,
@@ -1145,86 +1379,83 @@
     def own(x):
         return lax.dynamic_slice_in_dim(x.reshape((rows,) + x.shape[2:]), place * owned, owned, 0)
 
-    tokens_own = own(tokens).astype(f32)
-    inverse_one = lax.rsqrt(jnp.mean(tokens_own * tokens_own, axis=-1, keepdims=True) + epsilon)
-    unit_one = tokens_own * inverse_one
-    hidden_one = tokens_own + mixed
-    inverse_two = lax.rsqrt(jnp.mean(hidden_one * hidden_one, axis=-1, keepdims=True) + epsilon)
-    unit_two = hidden_one * inverse_two
-    gain_two = norm2_gain.astype(f32)
-    normed_two = (unit_two * gain_two).astype(bf16)
-    probs = jax.nn.softmax(dot_nt(normed_two, router_rows), axis=-1)
-    routes_own = own(routes)
-    chosen = routes_own[..., None] == jnp.arange(experts, dtype=jnp.int32)
-    chosen_rows = chosen.astype(f32)
-    gate_value = jnp.sum(probs * chosen_rows, axis=-1, keepdims=True)
-    row = jnp.arange(owned, dtype=jnp.int32)
-    earlier = (row[None, :] < row[:, None]) & (row[None, :] // part == row[:, None] // part)
-    rank_in = dot(earlier.astype(bf16), chosen.astype(bf16))
     slots = parts * most
-    wanted = rank_in + (row // part * most).astype(f32)[:, None]
-    hit = (wanted[..., None] == jnp.arange(slots, dtype=f32)) & chosen[..., None]
-    hit = hit.astype(bf16)
-    hit_send = hit.reshape(owned, experts * slots)
-    hit_back = jnp.repeat(hit, shards, axis=1).reshape(owned, n_seq * slots)
+    tokens_own, gain_two = own(tokens), norm2_gain.astype(f32)[None]
+    line, low = (owned, width), ((owned, width), bf16)
+    hidden_one, normed_two, probs, chosen, hit, packed = at_once(
+        functools.partial(route_kernel, part, most, slots),
+        [tokens_own, mixed, gain_two, own(routes)[:, None], router_rows],
+        [
+            (line, f32),
+            low,
+            ((owned, experts), f32),
+            ((owned, experts), f32),
+            ((owned, experts * slots), bf16),
+            ((experts * slots, width), bf16),
+        ],
+    )
+    hit_back = hit
+    if shards > 1:
+        hit_back = hit.reshape(owned, experts, slots)
+        hit_back = jnp.repeat(hit_back, shards, axis=1).reshape(owned, n_seq * slots)
 
     def to_slabs(x):
-        packed = dot_tn(hit_send, x).astype(bf16).reshape(experts, slots, width)
-        return jnp.repeat(packed, shards, axis=0), "scatter", "seq"
+        x = x.reshape(experts, slots, width)
+        return x if shards == 1 else jnp.repeat(x, shards, axis=0), "scatter", "seq"
 
     def to_rows(x):
         return x.reshape(n_seq, slots, width), "scatter", "seq"
 
-    def by_units(x):
-        return x.reshape(n_seq * slots, n_chan, units).transpose(1, 0, 2), "scatter", "chan"
-
     def flat(x):
         return x.reshape(-1, x.shape[-1])
 
     first_slab, second_slab = expert_in[0], expert_out[0]
-    units = first_slab.shape[1] // n_chan
-    arrived = flat(exchange(4, to_slabs(normed_two))[0])
-    pre_hidden = dot(arrived, first_slab)
-    cdf = 0.5 * (1.0 + lax.erf(pre_hidden * 0.7071067811865476))
-    hidden_low = (pre_hidden * cdf).astype(bf16)
-    density = jnp.exp(-0.5 * pre_hidden * pre_hidden) * 0.3989422804014327
-    slope = cdf + pre_hidden * density
-    result = dot(hidden_low, second_slab).astype(bf16)
+    arrived = flat(exchange(4, to_slabs(packed))[0])
+    hidden, slope, result = expert(arrived, first_slab, second_slab, n_chan)
     result_rows, rows_all = exchange(5, to_rows(result), (arrived, 2, "chan"))
-    expert_total = dot(hit_back, flat(result_rows))
-    layer = hidden_one + gate_value * expert_total
-    layer_low = layer.astype(bf16)
-
-    flat_row = place * owned + row
-    seq_of = flat_row // group
-    lengths_own = sum(
-        jnp.where(seq_of == s, true_lengths[s], 0) for s in range(seqs)
-    )
-    total_true = jnp.sum(true_lengths).astype(f32)
-    loss_mask = (first_pos + flat_row % group < lengths_own).astype(f32)[:, None]
-    error = layer - own(teacher).astype(f32)
-    loss_part = jnp.sum(loss_mask * error * error) / total_true
-    grad_layer = 2.0 / total_true * loss_mask * error
-    grad_gate = jnp.sum(grad_layer * expert_total, axis=-1, keepdims=True)
-    grad_result = (gate_value * grad_layer).astype(bf16)
-    grad_rows, hidden_all = exchange(6, to_slabs(grad_result), by_units(hidden_low))
+    layer_low, grad_layer, grad_logit, loss_row, packed = at_once(
+        functools.partial(loss_kernel, group),
+        [
+            true_lengths,
+            flat(result_rows),
+            hit_back,
+            hit,
+            hidden_one,
+            probs,
+            chosen,
+            own(teacher),
+        ],
+        [
+            low,
+            (line, f32),
+            ((owned, experts), f32),
+            ((1, width), f32),
+            ((experts * slots, width), bf16),
+        ],
+        scalars=1,
+    )
+    grad_rows, hidden_all = exchange(6, to_slabs(packed), (hidden, "scatter", "chan"))
     grad_rows = flat(grad_rows)
-    grad_pre = (dot_nt(grad_rows, second_slab) * slope).astype(bf16)
-    grad_slab_rows = dot_nt(grad_pre, first_slab).astype(bf16)
+    grad_pre, grad_slab_rows = expert(grad_rows, first_slab, second_slab, n_chan, slope)
     grad_expert, grad_rows_all = exchange(7, to_rows(grad_slab_rows), (grad_rows, 2, "chan"))
-    grad_expert = dot(hit_back, flat(grad_expert))
-
-    grad_logit = grad_gate * gate_value * (chosen_rows - probs)
-    grad_router = dot_tn(grad_logit.astype(bf16), normed_two)
-    grad_normed_two = grad_expert + dot(grad_logit.astype(bf16), router_rows)
-    grad_gain_two = jnp.sum(grad_normed_two * unit_two, axis=0)
-    grad_hidden_one = grad_layer + norm_back(grad_normed_two, unit_two, inverse_two, gain_two)
-
-    shared = packed_rows([grad_gain_two, grad_router, loss_part], 8)
-    grad_mixed, shared = exchange(
-        8, (grad_hidden_one.astype(bf16), 2, "chan"), (shared, "gather", "chan")
-    )
-    shared = jnp.sum(shared, axis=0)
+    shared_rows = -(-(experts + 2) // 8) * 8
+    grad_hidden_one, grad_low, shared = at_once(
+        norm_back_kernel,
+        [
+            flat(grad_expert),
+            hit_back,
+            grad_logit,
+            router_rows,
+            normed_two,
+            hidden_one,
+            grad_layer,
+            gain_two,
+            loss_row,
+        ],
+        [(line, f32), low, ((shared_rows, width), f32)],
+    )
+
+    (grad_mixed,) = exchange(8, (grad_low, 2, "chan"))
     grad_y, grad_z, grad_out_w, grad_in_gate, skip_sums, back_last = by_tiles(
         functools.partial(back_totals_kernel, rank, seqs),
         full,
@@ -1250,10 +1481,21 @@
         ],
         [(wide_shape, f32), ((rows, width), bf16)],
     )
-    summed_out, summed_gate = lax.psum((grad_out_w, grad_in_gate), "seq")
-    (back_enter,) = carried(back_last, sums, rate_two, "seq", True, 9)
-    side, log_sums, bias_sums, grad_dt_w, low_part = by_tiles(
-        functools.partial(back_kernel, rank),
+    back_enter, shared = carried(
+        back_last, sums, rate_two, "seq", True, 9, (shared, "gather", "chan")
+    )
+    shared = jnp.sum(shared, axis=0).reshape(-1, LANES)
+    def cut_rows(x, unit):
+        each = -(-x.shape[0] // (unit * n_seq)) * unit
+        return jnp.pad(x, ((0, each * n_seq - x.shape[0]), (0, 0))).reshape(n_seq, each, -1)
+
+    across = n_chan // 2
+    by_out, by_gate = cut_rows(grad_out_w, 16), cut_rows(grad_in_gate, 16)
+    rider = (grad_pre, "scatter", "chan")
+    side, log_sums, bias_sums, grad_dt_w, low_part, by_out, by_gate, grad_pre_all = by_tiles(
+        functools.partial(
+            back_kernel, rank, full // LANES, [("seq", n_seq, across)] * 2, items_of([rider])
+        ),
         full,
         [
             (step_size, "tile"),
@@ -1267,6 +1509,9 @@
             (dt_pre, "tile"),
             (pre_act, "tile"),
             (dt_rows, "tile"),
+            (by_out, "any"),
+            (by_gate, "any"),
+            (grad_pre, "any"),
         ],
         [
             (act_shape, f32, "tile"),
@@ -1274,8 +1519,20 @@
             ((lines, full), f32, "tile"),
             ((maps, full), f32, "tile"),
             ((rows, maps), bf16, "whole"),
-        ],
-        [(wide_shape, f32)] * 4 + [((steps, lines, LANES), f32)] * 2 + [((rows, maps), f32)],
+            (by_out.shape[1:], bf16, "whole"),
+            (by_gate.shape[1:], bf16, "whole"),
+            (grad_pre.shape, bf16, "any"),
+        ],
+        [(wide_shape, f32)] * 2
+        + [((steps, lines, states * lines), f32)] * 2
+        + [((steps, lines, LANES), f32)] * 2
+        + [((rows, maps), f32)]
+        + [(by_out.shape, bf16)] * 2,
+        [pltpu.SemaphoreType.DMA((2,))]
+        + share_scratch(by_out, "seq", across)
+        + share_scratch(by_gate, "seq", across)
+        + sems_of(items_of([rider])[0]),
+        {"collective_id": 15, "has_side_effects": True},
     )
     grad_mapped = summed_over(low_part, "chan", 10).astype(bf16)
     grad_conv_in, rims, grad_xproj, conv_sums = by_tiles(
@@ -1300,56 +1557,56 @@
         ],
         [((steps + rim, lines, LANES), f32)],
     )
-    grad_in_conv, normed_part, grad_gain_one = ends(
-        tokens, grad_conv_in, rims, grad_z, normed_one, w_in, 14
+    grad_in_conv, normed_part, grad_gain_one, by_gate = ends(
+        tokens, grad_conv_in, rims, grad_z, normed_one, w_in, 14, (by_gate, across, "seq")
     )
     normed_part = normed_part.reshape(n_chan, owned, width)
     sums_all = jnp.concatenate([conv_sums, bias_sums[None], skip_sums[None], log_sums], axis=0)
     sums_all = jnp.sum(sums_all, axis=1)
-
-    def cut_rows(x, unit):
-        each = -(-x.shape[0] // (unit * n_seq)) * unit
-        return jnp.pad(x, ((0, each * n_seq - x.shape[0]), (0, 0))).reshape(n_seq, each, -1)
-
-    large = cut_rows(grad_in_conv, 16)
+    small_rows = sums_all.shape[0] * full // LANES
+    small = jnp.concatenate([sums_all.reshape(small_rows, LANES), shared], axis=0)
+
+    by_conv = cut_rows(grad_in_conv, 16)
     middle = cut_rows(jnp.concatenate([grad_xproj, grad_dt_w[:rank]], axis=0).astype(bf16), 16)
-    across = n_chan // 2
-    grad_normed_one, large, middle, sums_all, shared, grad_gain_one, grad_pre_all = share_of(
+    grad_normed_one, by_conv, middle, small, grad_gain_one, by_out = share_of(
         11,
         [
             (normed_part, "chan", 2, f32),
-            (large, "seq", across, bf16),
+            (by_conv, "seq", across, bf16),
             (middle, "seq", across, bf16),
         ],
-        (cut_rows(sums_all, 8), "scatter", "seq"),
-        (cut_rows(shared, 8), "scatter", "seq"),
+        (cut_rows(small, 8), "scatter", "seq"),
         (grad_gain_one, "gather", "chan"),
-        by_units(grad_pre),
-    )
-    sums_all = jnp.sum(sums_all, axis=0)
-    shared = jnp.sum(shared, axis=0)
+        (by_out, across, "seq"),
+    )
+    small = jnp.sum(small, axis=0)
     grad_gain_one = jnp.sum(grad_gain_one, axis=0)
-    grad_own = grad_hidden_one + norm_back(grad_normed_one, unit_one, inverse_one, gain_one)
-    large, grad_tokens, layer_out, middle, sums_all, shared, grad_gain_one = exchange(
-        12,
-        (large, across, "seq"),
+    tokens_full = tokens_own.astype(f32)
+    inverse_one = lax.rsqrt(jnp.mean(tokens_full * tokens_full, axis=-1, keepdims=True) + epsilon)
+    grad_own = grad_hidden_one + norm_back(
+        grad_normed_one, tokens_full * inverse_one, inverse_one, gain_one
+    )
+    moved = [
         (grad_own.astype(bf16), 2, "chan"),
         (layer_low, 2, "chan"),
+        (by_conv, across, "seq"),
         (middle, across, "seq"),
-        (sums_all, "gather", "seq"),
-        (shared, "gather", "seq"),
+        (small, "gather", "seq"),
         (grad_gain_one, "gather", "seq"),
-    )
+    ]
+    moved = exchange(12, *moved)
     grad_first = dot_tn(flat(rows_all), flat(grad_pre_all))
     grad_second = dot_tn(flat(hidden_all), flat(grad_rows_all))
+    grad_tokens, layer_out, by_conv, middle, small, grad_gain_one = moved
     grad_gain_one = jnp.sum(grad_gain_one, axis=(0, 1))
-    summed_in = jnp.stack([flat(large)[:inner], summed_gate[:inner]]).astype(f32)
+    summed_in = jnp.stack([flat(by_conv)[:inner], flat(by_gate)[:inner]]).astype(f32)
     middle = flat(middle)[:, :inner].astype(f32)
-    small = flat(sums_all)[:, :inner]
-    tiny = unpacked_rows(flat(shared), [(width,), grad_router.shape, ()])
+    small = flat(small)
+    shared = small[small_rows : small_rows + shared_rows * width // LANES].reshape(shared_rows, width)
+    small = small[:small_rows].reshape(-1, full)[:, :inner]
     return (
         layer_out.reshape(seqs, group, width),
-        tiny[2],
+        shared[experts + 1, 0],
         grad_tokens.reshape(seqs, group, width).astype(f32),
         grad_gain_one,
         summed_in.transpose(2, 0, 1),
@@ -1360,9 +1617,9 @@
         small[taps + 1],
         (small[taps + 3 : taps + 3 + states] * rate).T,
         small[taps + 2],
-        summed_out[:inner].astype(f32),
-        tiny[0],
-        tiny[1].T,
+        flat(by_out)[:inner].astype(f32),
+        shared[experts],
+        shared[:experts].T,
         grad_first[None],
         grad_second[None],
     )

time: 486 us -> 437 us (0.90); the launches traced: 479 us -> 435 us
  Pallas kernels: 347 us -> 379 us
  matrix products: 36.3 us -> 9.34 us
  local copies, waits for them, and re-layouts: 54.2 us -> 33.9 us
  between operations: 16.6 us -> 1.61 us
  other arithmetic: 24.9 us -> 11.4 us
    pallas_call x1 -> x6, Pallas kernels: 10.1 us -> 53.4 us  [the longest x1 29.4 us: ends(): pl.pallas_call(functools.partial(ends_kernel, lax.axis_size('seq'), items...]
    dot_general x9 -> x0, matrix products: 24.6 us -> none  [the longest x6 16.6 us: dot(): return jnp.dot(a, b, preferred_element_type=f32)]
    pallas_call x5, Pallas kernels: 79 us -> 94.3 us  [by_tiles(): pl.pallas_call(kernel, grid=(full // LANES,), in_specs=[block_of(a.shape,...]
    pallas_call x2, Pallas kernels: 40.5 us -> 26.6 us  [carried(): pl.pallas_call(functools.partial(carry_kernel, axis, count, back, items),...]
    pallas_call x2, Pallas kernels: 66.2 us -> 56.9 us  [share_of(): pl.pallas_call(functools.partial(share_kernel, [(axis, lax.axis_size(axis...]
    unnamed x141 -> x135, local copies, waits for them, and re-layouts: 25.6 us -> 19 us
    dot_general x5 -> x2, matrix products: 11.6 us -> 9.34 us  [dot_tn(): lax.dot_general(a, b, (((0,), (0,)), ((), ())), preferred_element_type=f32)]
  transfers between devices with their start and end apart: 1 -> 0, of which waited for: 0 -> 0; matrix products, arithmetic and copies ran while one was open for 7% -> 0% of each run, Pallas kernels for 36% -> 0%
where the time goes in v3:
time: 437 us; the launch traced here: 435 us
  Pallas kernels  379 us (87%)
  local copies, waits for them, and re-layouts  33.9 us (8%)
  other arithmetic  11.4 us (3%)
  matrix products  9.34 us (2%)
    pallas_call x6, Pallas kernels, exchange(): pl.pallas_call(functools.partial(exchange_kernel, items), out_shape=[land...  124 us
    pallas_call x5, Pallas kernels, by_tiles(): pl.pallas_call(kernel, grid=(full // LANES,), in_specs=[block_of(a.shape,...  94.3 us
    pallas_call x2, Pallas kernels, share_of(): pl.pallas_call(functools.partial(share_kernel, [(axis, lax.axis_size(axis...  56.9 us
    pallas_call x1, Pallas kernels, ends(): pl.pallas_call(functools.partial(ends_kernel, lax.axis_size('seq'), items...  29.4 us
    pallas_call x2, Pallas kernels, carried(): pl.pallas_call(functools.partial(carry_kernel, axis, count, back, items),...  26.6 us
    pallas_call x2, Pallas kernels, expert(): pl.pallas_call(expert_back_kernel if back else expert_kernel, grid=(parts...  21.4 us
    unnamed x135, local copies, waits for them, and re-layouts  19 us
    pallas_call x1, Pallas kernels, front(): pl.pallas_call(functools.partial(front_kernel, lax.axis_size('seq'), coun...  16.6 us

profile of v3, /device:TPU:0, one launch (start us, length us, event | category | flops | bytes accessed | tf_op | source)
XLA Modules:
  0.0 435.2 jit_solution(8296726677627201033)
XLA Ops:
  4.4 16.6 %shard_map.314 = (bf16[512,1152]{1,0:T(8,128)(2,1)S(1)}, f32[67,8,640]{2,1,0:T(8,128)}, f32[64,8,640]{2,1,0:T(8,128)S(1)}, f32[64,8,640]{2,1,0:T(8,128)S(1)}, bf16[512,104]{1,0:T(8,128)(2,1)S(1)}) custom-call(bf16[4,128,1152]{2,1,0:T(8,128)(2,1)S(1)} %copy-done.3, f32[1,1152]{1,0:T(1,128)S(1)} %broadcast_in_dim.38.gain_ref, bf16[2,576,1152]{2,1,0:T(8,128)(2,1)} %bitcast.91, ...), custom_call_target="tpu_custom_call" | custom-call | tf_op jit(solution)/shard_map/pallas_call | solution.py:686
  26.2 9.5 %shard_map.315 = (f32[64,8,640]{2,1,0:T(8,128)}, f32[64,8,640]{2,1,0:T(8,128)}, f32[64,8,640]{2,1,0:T(8,128)}, f32[16,8,640]{2,1,0:T(8,128)}, f32[8,640]{1,0:T(8,128)}) custom-call(f32[64,8,640]{2,1,0:T(8,128)} %copy-done.2, bf16[512,104]{1,0:T(8,128)(2,1)} %copy-done.17, bf16[104,640]{1,0:T(8,128)(2,1)} %pad.69.dtw_ref, f32[1,640]{1,0:T(1,128)} %pad.53.bias_ref, ...), custom_call_target="tpu_custom_call" | custom-call | flops 1000 | bytes 1000 | tf_op jit(solution)/shard_map/pallas_call | solution.py:1228
  37.5 11.5 %shard_map.316.enter_ref.first_ref = f32[16,8,640]{2,1,0:T(8,128)S(1)} custom-call(f32[16,8,640]{2,1,0:T(8,128)S(1)} %copy-done.38, f32[8,640]{1,0:T(8,128)S(1)} %copy-done.47, f32[16,640]{1,0:T(8,128)S(1)} %copy-done.18), custom_call_target="tpu_custom_call" | custom-call | tf_op jit(solution)/shard_map/pallas_call | solution.py:493
  51.5 17.2 %shard_map.317 = (f32[64,8,640]{2,1,0:T(8,128)}, bf16[512,640]{1,0:T(8,128)(2,1)}, f32[64,16,8,640]{3,2,1,0:T(8,128)}, bf16[512,1152]{1,0:T(8,128)(2,1)}) custom-call(f32[64,8,640]{2,1,0:T(8,128)} %get-tuple-element.94.step_ref, f32[64,8,640]{2,1,0:T(8,128)} %get-tuple-element.95.drive_ref, bf16[512,104]{1,0:T(8,128)(2,1)} %copy-done.17, ...), custom_call_target="tpu_custom_call" | custom-call | flops 1000 | bytes 1000 | tf_op jit(solution)/shard_map/pallas_call | solution.py:1228
  69.9 10.9 %shard_map.318.mixed_ref = f32[128,1152]{1,0:T(8,128)S(1)} custom-call(bf16[4,128,1152]{2,1,0:T(8,128)(2,1)S(1)} %bitcast.72), custom_call_target="tpu_custom_call" | custom-call | tf_op jit(solution)/shard_map/pallas_call | solution.py:352
  82.8 21.8 %shard_map.320 = bf16[8,32,1152]{2,1,0:T(8,128)(2,1)S(1)} custom-call(bf16[8,32,1152]{2,1,0:T(8,128)(2,1)S(1)} %bitcast.76), custom_call_target="tpu_custom_call" | custom-call | tf_op jit(solution)/shard_map/pallas_call | solution.py:159
  105.5 10.6 %shard_map.321 = (bf16[4,256,768]{2,1,0:T(8,128)(2,1)}, bf16[256,3072]{1,0:T(8,128)(2,1)}, bf16[256,1152]{1,0:T(8,128)(2,1)}) custom-call(bf16[256,1152]{1,0:T(8,128)(2,1)} %bitcast.62, bf16[1152,3072]{1,0:T(8,128)(2,1)} %bitcast.87, bf16[3072,1152]{1,0:T(8,128)(2,1)} %bitcast.89), custom_call_target="tpu_custom_call" | custom-call | flops 1000 | bytes 1000 | tf_op jit(solution)/shard_map/pallas_call | solution.py:1189
  117.2 17.9 %shard_map.322 = (bf16[8,32,1152]{2,1,0:T(8,128)(2,1)S(1)}, bf16[4,256,1152]{2,1,0:T(8,128)(2,1)S(1)}) custom-call(bf16[8,32,1152]{2,1,0:T(8,128)(2,1)S(1)} %bitcast.77, bf16[256,1152]{1,0:T(8,128)(2,1)S(1)} %bitcast.63), custom_call_target="tpu_custom_call" | custom-call | tf_op jit(solution)/shard_map/pallas_call | solution.py:159
  137.8 22.2 %shard_map.324 = (bf16[8,32,1152]{2,1,0:T(8,128)(2,1)S(1)}, bf16[4,256,768]{2,1,0:T(8,128)(2,1)S(1)}) custom-call(bf16[8,32,1152]{2,1,0:T(8,128)(2,1)S(1)} %bitcast.79, bf16[4,256,768]{2,1,0:T(8,128)(2,1)S(1)} %copy-done.20), custom_call_target="tpu_custom_call" | custom-call | tf_op jit(solution)/shard_map/pallas_call | solution.py:159
  160.8 10.8 %shard_map.325 = (bf16[4,256,768]{2,1,0:T(8,128)(2,1)}, bf16[256,1152]{1,0:T(8,128)(2,1)}) custom-call(bf16[256,1152]{1,0:T(8,128)(2,1)} %bitcast.65, bf16[1152,3072]{1,0:T(8,128)(2,1)} %bitcast.88, bf16[3072,1152]{1,0:T(8,128)(2,1)} %bitcast.90, bf16[256,3072]{1,0:T(8,128)(2,1)} %get-tuple-element.110.slope_ref), custom_call_target="tpu_custom_call" | custom-call | flops 1000 | bytes 1000 | tf_op jit(solution)/shard_map/pallas_call | solution.py:1189
  172.7 17.7 %shard_map.326 = (bf16[8,32,1152]{2,1,0:T(8,128)(2,1)S(1)}, bf16[4,256,1152]{2,1,0:T(8,128)(2,1)S(1)}) custom-call(bf16[8,32,1152]{2,1,0:T(8,128)(2,1)S(1)} %bitcast.78, bf16[256,1152]{1,0:T(8,128)(2,1)S(1)} %bitcast.66), custom_call_target="tpu_custom_call" | custom-call | tf_op jit(solution)/shard_map/pallas_call | solution.py:159
  190.4 4.0 convolution_bitcast_fusion
  195.1 10.7 %shard_map.328 = bf16[4,128,1152]{2,1,0:T(8,128)(2,1)S(1)} custom-call(bf16[128,1152]{1,0:T(8,128)(2,1)S(1)} %get-tuple-element.118.refs_0_), custom_call_target="tpu_custom_call" | custom-call | tf_op jit(solution)/shard_map/pallas_call | solution.py:159
  206.8 15.4 %shard_map.329 = (f32[64,8,640]{2,1,0:T(8,128)}, bf16[512,640]{1,0:T(8,128)(2,1)}, bf16[640,1152]{1,0:T(8,128)(2,1)}, bf16[640,1152]{1,0:T(8,128)(2,1)}, f32[8,640]{1,0:T(8,128)}, /*index=5*/f32[16,8,640]{2,1,0:T(8,128)}) custom-call(f32[64,8,640]{2,1,0:T(8,128)} %get-tuple-element.94.step_ref, bf16[512,104]{1,0:T(8,128)(2,1)} %copy-done.17, ...), custom_call_target="tpu_custom_call" | custom-call | flops 1000 | bytes 1000 | tf_op jit(solution)/shard_map/pallas_call | solution.py:1228
  223.2 15.2 %shard_map.330 = (f32[16,8,640]{2,1,0:T(8,128)S(1)}, f32[4,16,1152]{2,1,0:T(8,128)S(1)}) custom-call(f32[16,8,640]{2,1,0:T(8,128)S(1)} %copy-done.37, f32[8,640]{1,0:T(8,128)S(1)} %copy-done.48, f32[16,640]{1,0:T(8,128)S(1)} %copy-done.19, f32[16,1152]{1,0:T(8,128)S(1)} %get-tuple-element.125.refs_3_), custom_call_target="tpu_custom_call" | custom-call | tf_op jit(solution)/shard_map/pallas_call | solution.py:493
  239.1 45.8 %shard_map.331 = (f32[64,8,640]{2,1,0:T(8,128)}, f32[16,8,640]{2,1,0:T(8,128)}, f32[8,640]{1,0:T(8,128)}, f32[104,640]{1,0:T(8,128)}, bf16[512,104]{1,0:T(8,128)...) custom-call(f32[64,8,640]{2,1,0:T(8,128)} %get-tuple-element.94.step_ref, ...), custom_call_target="tpu_custom_call" | custom-call | flops 1000 | bytes 1000 | tf_op jit(solution)/shard_map/pallas_call | solution.py:1228
  285.0 5.3 %convolution_bitcast_fusion.1 = f32[1,1152,768]{2,1,0:T(8,128)} fusion(bf16[4,256,1152]{2,1,0:T(8,128)(2,1)S(1)} %copy-done.53, bf16[4,256,768]{2,1,0:T(8,128)(2,1)} %get-tuple-element.164), kind=kOutput, calls=%fused_computation.2 | convolution fusion | flops 1811939328 | bytes 7471104 | tf_op jit(solution)/shard_map/dot_general | solution.py:565
  290.3 6.5 %shard_map.332 = f32[512,104]{1,0:T(8,128)S(1)} custom-call(bf16[512,104]{1,0:T(8,128)(2,1)S(1)} %copy-done.45), custom_call_target="tpu_custom_call" | custom-call | tf_op jit(solution)/shard_map/pallas_call | solution.py:224
  297.5 6.3 %shard_map.333 = (f32[64,8,640]{2,1,0:T(8,128)}, f32[3,8,640]{2,1,0:T(8,128)}, f32[104,640]{1,0:T(8,128)}, f32[5,8,640]{2,1,0:T(8,128)}) custom-call(bf16[512,104]{1,0:T(8,128)(2,1)} %convert_element_type.194.grad_mapped_ref, f32[64,8,640]{2,1,0:T(8,128)} %get-tuple-element.122.grad_y_ref, f32[64,8,640]{2,1,0:T(8,128)} %get-tuple-element.132.side_ref, ...), custom_call_target="tpu_custom_call" | custom-call | flops 1000 | bytes 1000 | tf_op jit(solution)/shard_map/pallas_call | solution.py:1228
  308.2 29.4 %shard_map.334 = (bf16[640,1152]{1,0:T(8,128)(2,1)}, bf16[512,1152]{1,0:T(8,128)(2,1)S(1)}, f32[1,1152]{1,0:T(1,128)S(1)}, bf16[8,80,1152]{2,1,0:T(8,128)(2,1)}) custom-call(bf16[4,128,1152]{2,1,0:T(8,128)(2,1)S(1)} %copy-done.3, f32[64,8,640]{2,1,0:T(8,128)S(1)} %copy-done.22, f32[3,8,640]{2,1,0:T(8,128)S(1)} %copy-done.50, ...), custom_call_target="tpu_custom_call" | custom-call | tf_op jit(solution)/shard_map/pallas_call | solution.py:1019
  339.0 46.0 %shard_map.335 = (f32[128,1152]{1,0:T(8,128)S(1)}, bf16[80,1152]{1,0:T(8,128)(2,1)S(1)}, bf16[32,640]{1,0:T(8,128)(2,1)S(1)}, f32[8,40,128]{2,1,0:T(8,128)S(1)},...) custom-call(bf16[4,128,1152]{2,1,0:T(8,128)(2,1)S(1)} %bitcast.71, bf16[8,80,1152]{2,1,0:T(8,128)(2,1)S(1)} %bitcast.67, ...), custom_call_target="tpu_custom_call" | custom-call | tf_op jit(solution)/shard_map/pallas_call | solution.py:352
  386.1 34.3 %shard_map.336 = (bf16[4,128,1152]{2,1,0:T(8,128)(2,1)S(1)}, bf16[4,128,1152]{2,1,0:T(8,128)(2,1)S(1)}, bf16[8,80,1152]{2,1,0:T(8,128)(2,1)S(1)}, bf16[8,32,640]...) custom-call(bf16[128,1152]{1,0:T(8,128)(2,1)S(1)} %fusion.8.refs_0_, ...), custom_call_target="tpu_custom_call" | custom-call | tf_op jit(solution)/shard_map/pallas_call | solution.py:159
  420.4 2.0 slice_bitcast_fusion
  422.4 2.7 convert_bitcast_fusion
  (202 shorter events, 43.3 us)
Async XLA Ops:
  0.7 135.8 %copy-start = (bf16[4,128,1152]{2,1,0:T(8,128)(2,1)S(1)}, bf16[4,128,1152]{2,1,0:T(8,128)(2,1)}, u32[]{:S(2)}) copy-start(bf16[4,128,1152]{2,1,0:T(8,128)(2,1)} %param.20) | copy-start | bytes 3538948
  3.2 17.8 %copy-start.10 = (f32[64,8,8]{2,1,0:T(8,128)}, f32[64,8,8]{2,1,0:T(8,128)S(1)}, u32[]{:S(2)}) copy-start(f32[64,8,8]{2,1,0:T(8,128)S(1)} %convert_element_type.192.valid_ref) | copy-start | bytes 49156
  4.3 16.8 %copy-start.23 = (bf16[104,640]{1,0:T(8,128)(2,1)}, bf16[104,640]{1,0:T(8,128)(2,1)S(1)}, u32[]{:S(2)}) copy-start(bf16[104,640]{1,0:T(8,128)(2,1)S(1)} %pad.50.xproj_ref) | copy-start | bytes 399364
  4.3 16.8 %copy-start.46 = (f32[4,640]{1,0:T(4,128)}, f32[4,640]{1,0:T(4,128)S(1)}, u32[]{:S(2)}) copy-start(f32[4,640]{1,0:T(4,128)S(1)} %pad_convert_fusion.taps_ref) | copy-start | bytes 30724
  4.4 19.9 %copy-start.56 = (f32[576,16]{0,1:T(8,128)S(1)}, f32[576,16]{0,1:T(8,128)}, u32[]{:S(2)}) copy-start(f32[576,16]{0,1:T(8,128)} %param.31) | copy-start | bytes 110596
  4.4 20.5 %copy-start.58 = (bf16[72,576]{1,0:T(8,128)(2,1)S(1)}, bf16[72,576]{1,0:T(8,128)(2,1)}, u32[]{:S(2)}) copy-start(bf16[72,576]{1,0:T(8,128)(2,1)} %param.29) | copy-start | bytes 248836
  4.4 21.2 %copy-start.64 = (f32[576]{0:T(1024)S(1)}, f32[576]{0:T(1024)}, u32[]{:S(2)}) copy-start(f32[576]{0:T(1024)} %param.30) | copy-start | bytes 6916
  24.3 25.4 %copy-start.54 = (bf16[576,1152]{1,0:T(8,128)(2,1)S(1)}, bf16[576,1152]{1,0:T(8,128)(2,1)}, u32[]{:S(2)}) copy-start(bf16[576,1152]{1,0:T(8,128)(2,1)} %param.33) | copy-start | bytes 3981316
  24.9 10.8 %copy-start.18 = (f32[16,640]{1,0:T(8,128)S(1)}, f32[16,640]{1,0:T(8,128)}, u32[]{:S(2)}) copy-start(f32[16,640]{1,0:T(8,128)} %pad.54.rate_ref.refs_2_) | copy-start | bytes 122884
  51.5 30.4 %copy-start.63 = (bf16[1152]{0:T(1024)(128)(2,1)S(1)}, bf16[1152]{0:T(1024)(128)(2,1)}, u32[]{:S(2)}) copy-start(bf16[1152]{0:T(1024)(128)(2,1)} %param.34) | copy-start | bytes 6916
  51.5 30.4 %copy-start.49 = (bf16[1152,8]{0,1:T(8,128)(2,1)S(1)}, bf16[1152,8]{0,1:T(8,128)(2,1)}, u32[]{:S(2)}) copy-start(bf16[1152,8]{0,1:T(8,128)(2,1)} %param.35) | copy-start | bytes 55300
  82.8 22.6 %copy-start.14 = (f32[128,1152]{1,0:T(8,128)}, f32[128,1152]{1,0:T(8,128)S(1)}, u32[]{:S(2)}) copy-start(f32[128,1152]{1,0:T(8,128)S(1)} %get-tuple-element.104.hidden_ref) | copy-start | bytes 1769476
  82.8 22.6 %copy-start.39 = (bf16[128,1152]{1,0:T(8,128)(2,1)}, bf16[128,1152]{1,0:T(8,128)(2,1)S(1)}, u32[]{:S(2)}) copy-start(bf16[128,1152]{1,0:T(8,128)(2,1)S(1)} %get-tuple-element.114.normed_ref) | copy-start | bytes 884740
  105.4 31.1 %copy-start.51 = (s32[4]{0:T(128)S(1)}, s32[4]{0:T(128)}, u32[]{:S(2)}) copy-start(s32[4]{0:T(128)} %lengths_ref.1) | copy-start | bytes 52
  116.1 20.5 %copy-start.15 = (f32[128,1152]{1,0:T(8,128)S(1)}, f32[128,1152]{1,0:T(8,128)}, u32[]{:S(2)}) copy-start(f32[128,1152]{1,0:T(8,128)} %copy-done.14) | copy-start | bytes 1769476
  117.2 20.6 %copy-start.20 = (bf16[4,256,768]{2,1,0:T(8,128)(2,1)S(1)}, bf16[4,256,768]{2,1,0:T(8,128)(2,1)}, u32[]{:S(2)}) copy-start(bf16[4,256,768]{2,1,0:T(8,128)(2,1)} %get-tuple-element.108.refs_1_) | copy-start | bytes 4718596
  137.8 23.0 %copy-start.32 = (f32[128,1152]{1,0:T(8,128)}, f32[128,1152]{1,0:T(8,128)S(1)}, u32[]{:S(2)}) copy-start(f32[128,1152]{1,0:T(8,128)S(1)} %get-tuple-element.115.grad_layer_ref) | copy-start | bytes 1769476
  137.8 23.0 %copy-start.41 = (bf16[128,1152]{1,0:T(8,128)(2,1)}, bf16[128,1152]{1,0:T(8,128)(2,1)S(1)}, u32[]{:S(2)}) copy-start(bf16[128,1152]{1,0:T(8,128)(2,1)S(1)} %get-tuple-element.150.refs_1_) | copy-start | bytes 884740
  195.0 11.7 %copy-start.30 = (f32[128,1152]{1,0:T(8,128)}, f32[128,1152]{1,0:T(8,128)S(1)}, u32[]{:S(2)}) copy-start(f32[128,1152]{1,0:T(8,128)S(1)} %get-tuple-element.117) | copy-start | bytes 1769476
  206.8 15.5 %copy-start.19 = (f32[16,640]{1,0:T(8,128)S(1)}, f32[16,640]{1,0:T(8,128)}, u32[]{:S(2)}) copy-start(f32[16,640]{1,0:T(8,128)} %pad.54.rate_ref.refs_2_) | copy-start | bytes 122884
  206.8 15.5 %copy-start.48 = (f32[8,640]{1,0:T(8,128)S(1)}, f32[8,640]{1,0:T(8,128)}, u32[]{:S(2)}) copy-start(f32[8,640]{1,0:T(8,128)} %get-tuple-element.97.refs_1_) | copy-start | bytes 61444
  239.1 45.8 %copy-start.53 = (bf16[4,256,1152]{2,1,0:T(8,128)(2,1)S(1)}, bf16[4,256,1152]{2,1,0:T(8,128)(2,1)}, u32[]{:S(2)}) copy-start(bf16[4,256,1152]{2,1,0:T(8,128)(2,1)} %copy-done.52) | copy-start | bytes 7077892
  308.2 29.4 %copy-start.44 = (bf16[80,1152]{1,0:T(8,128)(2,1)S(1)}, bf16[80,1152]{1,0:T(8,128)(2,1)}, u32[]{:S(2)}) copy-start(bf16[80,1152]{1,0:T(8,128)(2,1)} %get-tuple-element.148.refs_5_) | copy-start | bytes 552964
  339.0 46.3 %copy-start.31 = (f32[128,1152]{1,0:T(8,128)S(1)}, f32[128,1152]{1,0:T(8,128)}, u32[]{:S(2)}) copy-start(f32[128,1152]{1,0:T(8,128)} %copy-done.30) | copy-start | bytes 1769476
  (43 other events, 127.4 us)

commit v4 on v3

--- a/solution.py
+++ b/solution.py
@@ -15,6 +15,7 @@
 bf16 = jnp.bfloat16
 LANES = 128
 MIB = 1024 * 1024
+AHEAD = 12
 
 
 def greet(axes):
@@ -30,9 +31,14 @@
     return told
 
 
+def cuts_of(size):
+    half = -(-size // 32) * 16
+    return [(0, half), (half, size - half)] if half < size and size % 16 == 0 else [(0, size)]
+
+
 def sems_of(item):
-    count = item[2]
-    return [pltpu.SemaphoreType.DMA] + [pltpu.SemaphoreType.DMA((count - 1,))] * 2
+    copies = 2 * (item[2] - 1)
+    return [pltpu.SemaphoreType.DMA] + [pltpu.SemaphoreType.DMA((copies,))] * 2
 
 
 def flipped(i, mask):
@@ -63,7 +69,7 @@
         for copy in self.copies + self.own:
             copy.start()
         for chain in self.chains.values():
-            for first, _ in chain[:2]:
+            for first, _ in chain[:AHEAD]:
                 first.start()
         return self
 
@@ -71,10 +77,13 @@
         mode, axis, count = item
         me = lax.axis_index(axis)
 
-        def remote(source, row, slot, to):
+        def remote(source, row, slot, to, cut=None):
+            target = o_ref.at[row]
+            if cut is not None:
+                source, target = source.at[pl.ds(*cut)], o_ref.at[row, pl.ds(*cut)]
             return pltpu.make_async_remote_copy(
                 src_ref=source,
-                dst_ref=o_ref.at[row],
+                dst_ref=target,
                 send_sem=send_sem.at[slot],
                 recv_sem=recv_sem.at[slot],
                 device_id={axis: to},
@@ -92,26 +101,28 @@
         groups = count // mode
         side, place = lax.rem(me, mode), me // mode
         mates = [place * mode + lax.rem(side + j, mode) for j in range(1, mode)]
-        slot = groups - 1
+        slot = 0
         for mate in mates:
             self.copies.append(remote(x_ref, me, slot, mate))
             slot += 1
         chain = self.chains.setdefault(axis, [])
         for mask in order_of(groups):
             row = flipped(place, mask) * mode + side
-            first = remote(x_ref, me, mask - 1, row)
-            passed = []
-            for mate in mates:
-                passed.append(remote(o_ref.at[row], row, slot, mate))
+            for cut in cuts_of(x_ref.shape[0]):
+                first = remote(x_ref, me, slot, row, cut)
                 slot += 1
-            chain.append((first, passed))
+                passed = []
+                for mate in mates:
+                    passed.append(remote(o_ref.at[row], row, slot, mate, cut))
+                    slot += 1
+                chain.append((first, passed))
 
     def left(self):
-        return max([len(chain) - self.at[axis] for axis, chain in self.chains.items()] + [0])
+        return any(self.at[axis] < len(chain) for axis, chain in self.chains.items())
 
     def step(self):
-        for axis, chain in self.chains.items():
-            i = self.at[axis]
+        for axis in sorted(self.chains, reverse=True):
+            i, chain = self.at[axis], self.chains[axis]
             if i == len(chain):
                 continue
             self.at[axis] = i + 1
@@ -119,8 +130,9 @@
             first.wait_recv()
             for copy in passed:
                 copy.start()
-            if i + 2 < len(chain):
-                chain[i + 2][0].start()
+            if i + AHEAD < len(chain):
+                chain[i + AHEAD][0].start()
+            return
 
     def finish(self):
         while self.left():
@@ -288,7 +300,7 @@
 
     def pass_on(self, k):
         if k < self.groups - 1:
-            self.pairs[k] = self.near_sum(k).astype(bf16)
+            self.pairs[k] = self.near_sum(k).astype(self.pairs.dtype)
             self.far[k].start()
         else:
             for copy in self.near[k]:
@@ -323,7 +335,7 @@
     for (axis, _, _), task in zip(shares, tasks):
         turns.setdefault(axis, []).extend((task, k) for k in range(task.groups))
     for turn in turns.values():
-        for task, k in turn[:2]:
+        for task, k in turn[:AHEAD]:
             task.begin(k)
     under_way = Riders(items, riders, rider_outs, take(3 * number)).start()
     for i in range(max(len(turn) for turn in turns.values())):
@@ -331,8 +343,8 @@
             if i < len(turn):
                 task, k = turn[i]
                 task.pass_on(k)
-                if i + 2 < len(turn):
-                    task, k = turn[i + 2]
+                if i + AHEAD < len(turn):
+                    task, k = turn[i + AHEAD]
                     task.begin(k)
         under_way.step()
     for task, out in zip(tasks, outs):
@@ -850,7 +862,7 @@
         pl.semaphore_wait(pltpu.get_barrier_semaphore(), greet(sorted(axes)))
         for copy in copies:
             copy.wait()
-        for task, k in turn[:2]:
+        for task, k in turn[:3]:
             task.begin(k)
         under_way.start()
         spread(mapped_ref, rank, wide_in)
@@ -859,16 +871,21 @@
         sum_read[...] = jnp.zeros_like(sum_read)
         total[...] = jnp.zeros_like(total)
 
-    each = -(-len(turn) // (pieces - 1))
-    for piece in range(1, pieces):
-
-        @pl.when(place == piece)
-        def _():
-            for i in range((piece - 1) * each, min(piece * each, len(turn))):
-                turn[i][0].pass_on(turn[i][1])
-                if i + 2 < len(turn):
-                    turn[i + 2][0].begin(turn[i + 2][1])
-
+    moments = 2 * (pieces - 1)
+    each = -(-len(turn) // moments)
+
+    def pass_on(late):
+        for piece in range(1, pieces):
+            moment = 2 * (piece - 1) + late
+
+            @pl.when(place == piece)
+            def _():
+                for i in range(moment * each, min((moment + 1) * each, len(turn))):
+                    turn[i][0].pass_on(turn[i][1])
+                    if i + 3 < len(turn):
+                        turn[i + 3][0].begin(turn[i + 3][1])
+
+    pass_on(0)
     rates = [rows_of(rate_ref, n, rows) for n in range(count)]
     for n in range(count):
         log_ref[n] = jnp.zeros((rows, lanes), f32)
@@ -899,7 +916,12 @@
         p = steps - 1 - turn
         return step_back(p, carry, lambda n: state_ref[p - 1, n])
 
-    carry = lax.fori_loop(0, steps - 1, one, tuple(enter_ref[n] for n in range(count)), unroll=7 if (steps - 1) % 7 == 0 else 1)
+    carry = tuple(enter_ref[n] for n in range(count))
+    unroll = 7 if (steps - 1) % 7 == 0 else 1
+    middle = (steps - 1) // unroll // 2 * unroll
+    carry = lax.fori_loop(0, middle, one, carry, unroll=unroll)
+    pass_on(1)
+    carry = lax.fori_loop(middle, steps - 1, one, carry, unroll=unroll)
     step_back(0, carry, lambda n: first_ref[n])
     dt_pre, pre = dt_ref[...], pre_ref[...]
     inputs = to_input[...]
@@ -981,7 +1003,9 @@
 
     under_way = Riders(items, xs, outs, sems).start()
     unit = unit_of(tokens_ref[...].reshape(rows, width).astype(f32))
+    under_way.step()
     by_gate = dot(grad_z_ref[:, pl.ds(0, inner)], w_ref[1])
+    under_way.step()
 
     @pl.when(here == count - 1)
     def _():
@@ -997,13 +1021,19 @@
     ]
     grad = jnp.concatenate([grad_ref[pl.ds(0, steps - rim)]] + last, axis=0)
     grad = grad.reshape(rows, full).astype(bf16)
-    under_way.step()
-    grad_conv_ref[...] = dot_tn(grad, normed_ref[...]).astype(bf16)
-    under_way.step()
-    part = (dot(grad[:, :inner], w_ref[0]) + by_gate).astype(bf16)
-    part = dot_tn(perm_of(steps, lines, seqs), part)
-    part_ref[...] = part.astype(bf16)
-    gain_ref[...] = jnp.sum(part * unit, axis=0, keepdims=True)
+    for j in range(0, inner, LANES):
+        many = min(LANES, inner - j)
+        piece = dot_tn(grad[:, j : j + many], normed_ref[...])
+        grad_conv_ref[pl.ds(j, many), :] = piece.astype(bf16)
+        under_way.step()
+    perm = perm_of(steps, lines, seqs)
+    tile = next(t for t in (384, LANES, width) if width % t == 0)
+    for j in range(0, width, tile):
+        piece = dot(grad[:, :inner], w_ref[0, :, pl.ds(j, tile)]) + by_gate[:, j : j + tile]
+        piece = dot_tn(perm, piece.astype(bf16))
+        part_ref[:, pl.ds(j, tile)] = piece.astype(bf16)
+        gain_ref[:, pl.ds(j, tile)] = jnp.sum(piece * unit[:, j : j + tile], axis=0, keepdims=True)
+        under_way.step()
     under_way.finish()
 
     @pl.when(here > 0)
@@ -1019,7 +1049,7 @@
     return pl.pallas_call(
         functools.partial(ends_kernel, lax.axis_size("seq"), items),
         out_shape=[
-            jax.ShapeDtypeStruct((full, width), bf16),
+            jax.ShapeDtypeStruct((w_in.shape[1], width), bf16),
             jax.ShapeDtypeStruct((rows, width), bf16),
             jax.ShapeDtypeStruct((1, width), f32),
         ]
@@ -1200,6 +1230,34 @@
     )(x, first, second, *([slope] if back else []))
 
 
+def widen_kernel(conv_ref, gate_ref, out_ref, tokens_ref, grad_in_ref, grad_out_ref, grad_tokens_ref):
+    grad_in_ref[0] = conv_ref[...].astype(f32)
+    grad_in_ref[1] = gate_ref[...].astype(f32)
+    grad_out_ref[...] = out_ref[...].astype(f32)
+    grad_tokens_ref[...] = tokens_ref[...].astype(f32)
+
+
+def widened(conv, gate, out, tokens, inner):
+    width, rows = conv.shape[1], tokens.shape[0]
+    pieces = next(n for n in (4, 2, 1) if inner % (16 * n) == 0 and rows % (16 * n) == 0)
+    each, lines = inner // pieces, rows // pieces
+    block = pl.BlockSpec((each, width), lambda i: (i, 0))
+    row_block = pl.BlockSpec((lines, width), lambda i: (i, 0))
+    return pl.pallas_call(
+        widen_kernel,
+        grid=(pieces,),
+        in_specs=[block] * 3 + [row_block],
+        out_specs=[pl.BlockSpec((2, each, width), lambda i: (0, i, 0)), block, row_block],
+        out_shape=[
+            jax.ShapeDtypeStruct((2, inner, width), f32),
+            jax.ShapeDtypeStruct((inner, width), f32),
+            jax.ShapeDtypeStruct((rows, width), f32),
+        ],
+        compiler_params=pltpu.CompilerParams(vmem_limit_bytes=48 * MIB),
+        cost_estimate=pl.CostEstimate(flops=1000, bytes_accessed=1000, transcendentals=0),
+    )(conv, gate, out, tokens)
+
+
 def block_of(shape, kind):
     if kind == "tile":
         return pl.BlockSpec(shape[:-1] + (LANES,), lambda i: (0,) * (len(shape) - 1) + (i,))
@@ -1214,9 +1272,9 @@
     groups = lax.axis_size(axis) // size
     part = x.shape[1:]
     return [
-        pltpu.VMEM((groups, size - 1) + part, bf16),
-        pltpu.VMEM((groups - 1,) + part, bf16),
-        pltpu.VMEM((groups - 1,) + part, bf16),
+        pltpu.VMEM((groups, size - 1) + part, x.dtype),
+        pltpu.VMEM((groups - 1,) + part, x.dtype),
+        pltpu.VMEM((groups - 1,) + part, x.dtype),
         pltpu.SemaphoreType.DMA((groups, size - 1)),
         pltpu.SemaphoreType.DMA((groups, size - 1)),
         pltpu.SemaphoreType.DMA((groups - 1,)),
@@ -1412,7 +1470,7 @@
     first_slab, second_slab = expert_in[0], expert_out[0]
     arrived = flat(exchange(4, to_slabs(packed))[0])
     hidden, slope, result = expert(arrived, first_slab, second_slab, n_chan)
-    result_rows, rows_all = exchange(5, to_rows(result), (arrived, 2, "chan"))
+    (result_rows,) = exchange(5, to_rows(result))
     layer_low, grad_layer, grad_logit, loss_row, packed = at_once(
         functools.partial(loss_kernel, group),
         [
@@ -1434,10 +1492,9 @@
         ],
         scalars=1,
     )
-    grad_rows, hidden_all = exchange(6, to_slabs(packed), (hidden, "scatter", "chan"))
-    grad_rows = flat(grad_rows)
+    grad_rows = flat(exchange(6, to_slabs(packed))[0])
     grad_pre, grad_slab_rows = expert(grad_rows, first_slab, second_slab, n_chan, slope)
-    grad_expert, grad_rows_all = exchange(7, to_rows(grad_slab_rows), (grad_rows, 2, "chan"))
+    (grad_expert,) = exchange(7, to_rows(grad_slab_rows))
     shared_rows = -(-(experts + 2) // 8) * 8
     grad_hidden_one, grad_low, shared = at_once(
         norm_back_kernel,
@@ -1474,8 +1531,8 @@
         [
             (act_shape, f32, "tile"),
             ((rows, full), bf16, "tile"),
-            ((full, width), bf16, "rows"),
-            ((full, width), bf16, "rows"),
+            ((inner, width), bf16, "rows"),
+            ((inner, width), bf16, "rows"),
             ((lines, full), f32, "tile"),
             (state_shape, f32, "tile"),
         ],
@@ -1490,12 +1547,11 @@
         return jnp.pad(x, ((0, each * n_seq - x.shape[0]), (0, 0))).reshape(n_seq, each, -1)
 
     across = n_chan // 2
-    by_out, by_gate = cut_rows(grad_out_w, 16), cut_rows(grad_in_gate, 16)
-    rider = (grad_pre, "scatter", "chan")
-    side, log_sums, bias_sums, grad_dt_w, low_part, by_out, by_gate, grad_pre_all = by_tiles(
-        functools.partial(
-            back_kernel, rank, full // LANES, [("seq", n_seq, across)] * 2, items_of([rider])
-        ),
+    by_out, by_gate = cut_rows(grad_out_w, 8), cut_rows(grad_in_gate, 8)
+    riders = [(hidden, "scatter", "chan"), (grad_pre, "scatter", "chan")]
+    items = items_of(riders)
+    side, log_sums, bias_sums, grad_dt_w, low_part, by_out, by_gate, hidden_all, grad_pre_all = by_tiles(
+        functools.partial(back_kernel, rank, full // LANES, [("seq", n_seq, across)] * 2, items),
         full,
         [
             (step_size, "tile"),
@@ -1511,6 +1567,7 @@
             (dt_rows, "tile"),
             (by_out, "any"),
             (by_gate, "any"),
+            (hidden, "any"),
             (grad_pre, "any"),
         ],
         [
@@ -1521,6 +1578,7 @@
             ((rows, maps), bf16, "whole"),
             (by_out.shape[1:], bf16, "whole"),
             (by_gate.shape[1:], bf16, "whole"),
+            (hidden.shape, bf16, "any"),
             (grad_pre.shape, bf16, "any"),
         ],
         [(wide_shape, f32)] * 2
@@ -1531,7 +1589,7 @@
         [pltpu.SemaphoreType.DMA((2,))]
         + share_scratch(by_out, "seq", across)
         + share_scratch(by_gate, "seq", across)
-        + sems_of(items_of([rider])[0]),
+        + [sem for item in items for sem in sems_of(item)],
         {"collective_id": 15, "has_side_effects": True},
     )
     grad_mapped = summed_over(low_part, "chan", 10).astype(bf16)
@@ -1557,8 +1615,16 @@
         ],
         [((steps + rim, lines, LANES), f32)],
     )
-    grad_in_conv, normed_part, grad_gain_one, by_gate = ends(
-        tokens, grad_conv_in, rims, grad_z, normed_one, w_in, 14, (by_gate, across, "seq")
+    grad_in_conv, normed_part, grad_gain_one, by_gate, rows_all = ends(
+        tokens,
+        grad_conv_in,
+        rims,
+        grad_z,
+        normed_one,
+        w_in,
+        14,
+        (by_gate, across, "seq"),
+        (arrived, 2, "chan"),
     )
     normed_part = normed_part.reshape(n_chan, owned, width)
     sums_all = jnp.concatenate([conv_sums, bias_sums[None], skip_sums[None], log_sums], axis=0)
@@ -1566,20 +1632,20 @@
     small_rows = sums_all.shape[0] * full // LANES
     small = jnp.concatenate([sums_all.reshape(small_rows, LANES), shared], axis=0)
 
-    by_conv = cut_rows(grad_in_conv, 16)
+    by_conv = cut_rows(grad_in_conv, 8)
     middle = cut_rows(jnp.concatenate([grad_xproj, grad_dt_w[:rank]], axis=0).astype(bf16), 16)
-    grad_normed_one, by_conv, middle, small, grad_gain_one, by_out = share_of(
+    grad_normed_one, small, middle, by_conv, grad_gain_one, by_out, grad_rows_all = share_of(
         11,
         [
             (normed_part, "chan", 2, f32),
+            (cut_rows(small, 8), "seq", across, f32),
+            (middle, "seq", across, bf16),
             (by_conv, "seq", across, bf16),
-            (middle, "seq", across, bf16),
-        ],
-        (cut_rows(small, 8), "scatter", "seq"),
+        ],
         (grad_gain_one, "gather", "chan"),
         (by_out, across, "seq"),
-    )
-    small = jnp.sum(small, axis=0)
+        (grad_rows, 2, "chan"),
+    )
     grad_gain_one = jnp.sum(grad_gain_one, axis=0)
     tokens_full = tokens_own.astype(f32)
     inverse_one = lax.rsqrt(jnp.mean(tokens_full * tokens_full, axis=-1, keepdims=True) + epsilon)
@@ -1589,17 +1655,19 @@
     moved = [
         (grad_own.astype(bf16), 2, "chan"),
         (layer_low, 2, "chan"),
+        (small, across, "seq"),
+        (middle, across, "seq"),
         (by_conv, across, "seq"),
-        (middle, across, "seq"),
-        (small, "gather", "seq"),
         (grad_gain_one, "gather", "seq"),
     ]
     moved = exchange(12, *moved)
     grad_first = dot_tn(flat(rows_all), flat(grad_pre_all))
     grad_second = dot_tn(flat(hidden_all), flat(grad_rows_all))
-    grad_tokens, layer_out, by_conv, middle, small, grad_gain_one = moved
+    grad_tokens, layer_out, small, middle, by_conv, grad_gain_one = moved
     grad_gain_one = jnp.sum(grad_gain_one, axis=(0, 1))
-    summed_in = jnp.stack([flat(by_conv)[:inner], flat(by_gate)[:inner]]).astype(f32)
+    summed_in, summed_out, grad_tokens = widened(
+        flat(by_conv), flat(by_gate), flat(by_out), flat(grad_tokens), inner
+    )
     middle = flat(middle)[:, :inner].astype(f32)
     small = flat(small)
     shared = small[small_rows : small_rows + shared_rows * width // LANES].reshape(shared_rows, width)
@@ -1607,7 +1675,7 @@
     return (
         layer_out.reshape(seqs, group, width),
         shared[experts + 1, 0],
-        grad_tokens.reshape(seqs, group, width).astype(f32),
+        grad_tokens.reshape(seqs, group, width),
         grad_gain_one,
         summed_in.transpose(2, 0, 1),
         small[:taps],
@@ -1617,7 +1685,7 @@
         small[taps + 1],
         (small[taps + 3 : taps + 3 + states] * rate).T,
         small[taps + 2],
-        flat(by_out)[:inner].astype(f32),
+        summed_out,
         shared[experts],
         shared[:experts].T,
         grad_first[None],

time: 437 us -> 412 us (0.943)
  Pallas kernels: 379 us -> 357 us
    pallas_call x6, Pallas kernels: 124 us -> 111 us  [exchange(): pl.pallas_call(functools.partial(exchange_kernel, items), out_shape=[land...]
    pallas_call x2, Pallas kernels: 56.9 us -> 49.9 us  [share_of(): pl.pallas_call(functools.partial(share_kernel, [(axis, lax.axis_size(axis...]
    unnamed x135 -> x133, local copies, waits for them, and re-layouts: 19 us -> 22.9 us
where the time goes in v4:
time: 412 us; the launch traced here: 411 us
  Pallas kernels  357 us (87%)
  local copies, waits for them, and re-layouts  37.1 us (9%)
  matrix products  7.91 us (2%)
  other arithmetic  7.88 us (2%)
    pallas_call x6, Pallas kernels, exchange(): pl.pallas_call(functools.partial(exchange_kernel, items), out_shape=[land...  111 us
    pallas_call x5, Pallas kernels, by_tiles(): pl.pallas_call(kernel, grid=(full // LANES,), in_specs=[block_of(a.shape,...  91 us
    pallas_call x2, Pallas kernels, share_of(): pl.pallas_call(functools.partial(share_kernel, [(axis, lax.axis_size(axis...  49.9 us
    pallas_call x1, Pallas kernels, ends(): pl.pallas_call(functools.partial(ends_kernel, lax.axis_size('seq'), items...  27.3 us
    pallas_call x2, Pallas kernels, carried(): pl.pallas_call(functools.partial(carry_kernel, axis, count, back, items),...  26.7 us
    unnamed x133, local copies, waits for them, and re-layouts  22.9 us
    pallas_call x2, Pallas kernels, expert(): pl.pallas_call(expert_back_kernel if back else expert_kernel, grid=(parts...  21.3 us
    pallas_call x1, Pallas kernels, front(): pl.pallas_call(functools.partial(front_kernel, lax.axis_size('seq'), coun...  16.7 us

profile of v4, /device:TPU:0, one launch (start us, length us, event | category | flops | bytes accessed | tf_op | source)
XLA Modules:
  0.0 411.2 jit_solution(6775056060463403359)
XLA Ops:
  5.1 16.7 %shard_map.314 = (bf16[512,1152]{1,0:T(8,128)(2,1)S(1)}, f32[67,8,640]{2,1,0:T(8,128)}, f32[64,8,640]{2,1,0:T(8,128)S(1)}, f32[64,8,640]{2,1,0:T(8,128)S(1)}, bf16[512,104]{1,0:T(8,128)(2,1)S(1)}) custom-call(bf16[4,128,1152]{2,1,0:T(8,128)(2,1)S(1)} %copy-done.3, f32[1,1152]{1,0:T(1,128)S(1)} %broadcast_in_dim.38.gain_ref, bf16[2,576,1152]{2,1,0:T(8,128)(2,1)} %bitcast.90, ...), custom_call_target="tpu_custom_call" | custom-call | tf_op jit(solution)/shard_map/pallas_call | solution.py:698
  26.9 9.6 %shard_map.315 = (f32[64,8,640]{2,1,0:T(8,128)}, f32[64,8,640]{2,1,0:T(8,128)}, f32[64,8,640]{2,1,0:T(8,128)}, f32[16,8,640]{2,1,0:T(8,128)}, f32[8,640]{1,0:T(8,128)}) custom-call(f32[64,8,640]{2,1,0:T(8,128)} %copy-done.2, bf16[512,104]{1,0:T(8,128)(2,1)} %copy-done.18, bf16[104,640]{1,0:T(8,128)(2,1)} %pad.67.dtw_ref, f32[1,640]{1,0:T(1,128)} %pad.53.bias_ref, ...), custom_call_target="tpu_custom_call" | custom-call | flops 1000 | bytes 1000 | tf_op jit(solution)/shard_map/pallas_call | solution.py:1286
  38.1 11.5 %shard_map.316.enter_ref.first_ref = f32[16,8,640]{2,1,0:T(8,128)S(1)} custom-call(f32[16,8,640]{2,1,0:T(8,128)S(1)} %copy-done.34, f32[8,640]{1,0:T(8,128)S(1)} %copy-done.46, f32[16,640]{1,0:T(8,128)S(1)} %copy-done.19), custom_call_target="tpu_custom_call" | custom-call | tf_op jit(solution)/shard_map/pallas_call | solution.py:505
  52.2 17.2 %shard_map.317 = (f32[64,8,640]{2,1,0:T(8,128)}, bf16[512,640]{1,0:T(8,128)(2,1)}, f32[64,16,8,640]{3,2,1,0:T(8,128)}, bf16[512,1152]{1,0:T(8,128)(2,1)}) custom-call(f32[64,8,640]{2,1,0:T(8,128)} %get-tuple-element.94.step_ref, f32[64,8,640]{2,1,0:T(8,128)} %get-tuple-element.95.drive_ref, bf16[512,104]{1,0:T(8,128)(2,1)} %copy-done.18, ...), custom_call_target="tpu_custom_call" | custom-call | flops 1000 | bytes 1000 | tf_op jit(solution)/shard_map/pallas_call | solution.py:1286
  70.6 10.9 %shard_map.318.mixed_ref = f32[128,1152]{1,0:T(8,128)S(1)} custom-call(bf16[4,128,1152]{2,1,0:T(8,128)(2,1)S(1)} %bitcast.72), custom_call_target="tpu_custom_call" | custom-call | tf_op jit(solution)/shard_map/pallas_call | solution.py:364
  85.4 21.9 %shard_map.320 = bf16[8,32,1152]{2,1,0:T(8,128)(2,1)S(1)} custom-call(bf16[8,32,1152]{2,1,0:T(8,128)(2,1)S(1)} %bitcast.76), custom_call_target="tpu_custom_call" | custom-call | tf_op jit(solution)/shard_map/pallas_call | solution.py:171
  108.2 10.5 %shard_map.321 = (bf16[4,256,768]{2,1,0:T(8,128)(2,1)}, bf16[256,3072]{1,0:T(8,128)(2,1)}, bf16[256,1152]{1,0:T(8,128)(2,1)}) custom-call(bf16[256,1152]{1,0:T(8,128)(2,1)} %bitcast.59, bf16[1152,3072]{1,0:T(8,128)(2,1)} %bitcast.86, bf16[3072,1152]{1,0:T(8,128)(2,1)} %bitcast.88), custom_call_target="tpu_custom_call" | custom-call | flops 1000 | bytes 1000 | tf_op jit(solution)/shard_map/pallas_call | solution.py:1219
  119.8 16.8 %shard_map.322 = bf16[8,32,1152]{2,1,0:T(8,128)(2,1)S(1)} custom-call(bf16[8,32,1152]{2,1,0:T(8,128)(2,1)S(1)} %bitcast.77), custom_call_target="tpu_custom_call" | custom-call | tf_op jit(solution)/shard_map/pallas_call | solution.py:171
  137.9 16.1 %shard_map.324 = bf16[8,32,1152]{2,1,0:T(8,128)(2,1)S(1)} custom-call(bf16[8,32,1152]{2,1,0:T(8,128)(2,1)S(1)} %bitcast.75), custom_call_target="tpu_custom_call" | custom-call | tf_op jit(solution)/shard_map/pallas_call | solution.py:171
  154.8 10.8 %shard_map.325 = (bf16[4,256,768]{2,1,0:T(8,128)(2,1)}, bf16[256,1152]{1,0:T(8,128)(2,1)}) custom-call(bf16[256,1152]{1,0:T(8,128)(2,1)} %bitcast.61, bf16[1152,3072]{1,0:T(8,128)(2,1)} %bitcast.87, bf16[3072,1152]{1,0:T(8,128)(2,1)} %bitcast.89, bf16[256,3072]{1,0:T(8,128)(2,1)} %get-tuple-element.107.slope_ref), custom_call_target="tpu_custom_call" | custom-call | flops 1000 | bytes 1000 | tf_op jit(solution)/shard_map/pallas_call | solution.py:1219
  166.7 15.8 %shard_map.326 = bf16[8,32,1152]{2,1,0:T(8,128)(2,1)S(1)} custom-call(bf16[8,32,1152]{2,1,0:T(8,128)(2,1)S(1)} %bitcast.78), custom_call_target="tpu_custom_call" | custom-call | tf_op jit(solution)/shard_map/pallas_call | solution.py:171
  183.0 10.5 %shard_map.328 = bf16[4,128,1152]{2,1,0:T(8,128)(2,1)S(1)} custom-call(bf16[128,1152]{1,0:T(8,128)(2,1)S(1)} %get-tuple-element.114.refs_0_), custom_call_target="tpu_custom_call" | custom-call | tf_op jit(solution)/shard_map/pallas_call | solution.py:171
  194.6 15.2 %shard_map.329 = (f32[64,8,640]{2,1,0:T(8,128)}, bf16[512,640]{1,0:T(8,128)(2,1)}, bf16[576,1152]{1,0:T(8,128)(2,1)}, bf16[576,1152]{1,0:T(8,128)(2,1)}, f32[8,640]{1,0:T(8,128)}, /*index=5*/f32[16,8,640]{2,1,0:T(8,128)}) custom-call(f32[64,8,640]{2,1,0:T(8,128)} %get-tuple-element.94.step_ref, bf16[512,104]{1,0:T(8,128)(2,1)} %copy-done.18, ...), custom_call_target="tpu_custom_call" | custom-call | flops 1000 | bytes 1000 | tf_op jit(solution)/shard_map/pallas_call | solution.py:1286
  210.8 15.3 %shard_map.330 = (f32[16,8,640]{2,1,0:T(8,128)S(1)}, f32[4,16,1152]{2,1,0:T(8,128)S(1)}) custom-call(f32[16,8,640]{2,1,0:T(8,128)S(1)} %copy-done.33, f32[8,640]{1,0:T(8,128)S(1)} %copy-done.47, f32[16,640]{1,0:T(8,128)S(1)} %copy-done.20, f32[16,1152]{1,0:T(8,128)S(1)} %get-tuple-element.121.refs_3_), custom_call_target="tpu_custom_call" | custom-call | tf_op jit(solution)/shard_map/pallas_call | solution.py:505
  226.8 42.7 %shard_map.331 = (f32[64,8,640]{2,1,0:T(8,128)}, f32[16,8,640]{2,1,0:T(8,128)}, f32[8,640]{1,0:T(8,128)}, f32[104,640]{1,0:T(8,128)}, bf16[512,104]{1,0:T(8,128)...) custom-call(f32[64,8,640]{2,1,0:T(8,128)} %get-tuple-element.94.step, ...), custom_call_target="tpu_custom_call" | custom-call | flops 1000 | bytes 1000 | tf_op jit(solution)/shard_map/pallas_call | solution.py:1286
  270.5 6.3 %shard_map.332 = f32[512,104]{1,0:T(8,128)S(1)} custom-call(bf16[512,104]{1,0:T(8,128)(2,1)S(1)} %copy-done.44), custom_call_target="tpu_custom_call" | custom-call | tf_op jit(solution)/shard_map/pallas_call | solution.py:236
  277.4 6.3 %shard_map.333 = (f32[64,8,640]{2,1,0:T(8,128)}, f32[3,8,640]{2,1,0:T(8,128)}, f32[104,640]{1,0:T(8,128)}, f32[5,8,640]{2,1,0:T(8,128)}) custom-call(bf16[512,104]{1,0:T(8,128)(2,1)} %convert_element_type.187.grad_mapped_ref, f32[64,8,640]{2,1,0:T(8,128)} %get-tuple-element.118.grad_y_ref, f32[64,8,640]{2,1,0:T(8,128)} %get-tuple-element.129.side_ref, ...), custom_call_target="tpu_custom_call" | custom-call | flops 1000 | bytes 1000 | tf_op jit(solution)/shard_map/pallas_call | solution.py:1286
  292.1 27.3 %shard_map.334 = (bf16[576,1152]{1,0:T(8,128)(2,1)}, bf16[512,1152]{1,0:T(8,128)(2,1)S(1)}, f32[1,1152]{1,0:T(1,128)S(1)}, bf16[8,72,1152]{2,1,0:T(8,128)(2,1)}, bf16[4,256,1152]{2,1,0:T(8,128)(2,1)}) custom-call(bf16[4,128,1152]{2,1,0:T(8,128)(2,1)S(1)} %copy-done.3, f32[64,8,640]{2,1,0:T(8,128)} %get-tuple-element.131.grad_ref, ...), custom_call_target="tpu_custom_call" | custom-call | tf_op jit(solution)/shard_map/pallas_call | solution.py:1049
  319.5 1.3 copy-done.22
  320.8 38.9 %shard_map.335 = (f32[128,1152]{1,0:T(8,128)S(1)}, f32[40,128]{1,0:T(8,128)S(1)}, bf16[32,640]{1,0:T(8,128)(2,1)S(1)}, bf16[72,1152]{1,0:T(8,128)(2,1)S(1)}, f32...) custom-call(bf16[4,128,1152]{2,1,0:T(8,128)(2,1)S(1)} %bitcast.73, ...), custom_call_target="tpu_custom_call" | custom-call | tf_op jit(solution)/shard_map/pallas_call | solution.py:364
  359.8 4.0 convolution_bitcast_fusion
  363.8 3.9 convolution_bitcast_fusion.1
  369.6 29.8 %shard_map.336 = (bf16[4,128,1152]{2,1,0:T(8,128)(2,1)S(1)}, bf16[4,128,1152]{2,1,0:T(8,128)(2,1)S(1)}, f32[8,40,128]{2,1,0:T(8,128)S(1)}, bf16[8,32,640]{2,1,0:...) custom-call(bf16[128,1152]{1,0:T(8,128)(2,1)S(1)} %fusion.8.refs_0_, ...), custom_call_target="tpu_custom_call" | custom-call | tf_op jit(solution)/shard_map/pallas_call | solution.py:171
  400.4 4.1 shard_map.337
  (196 shorter events, 46.3 us)
Async XLA Ops:
  0.7 136.0 %copy-start = (bf16[4,128,1152]{2,1,0:T(8,128)(2,1)S(1)}, bf16[4,128,1152]{2,1,0:T(8,128)(2,1)}, u32[]{:S(2)}) copy-start(bf16[4,128,1152]{2,1,0:T(8,128)(2,1)} %param.20) | copy-start | bytes 3538948
  3.2 18.6 %copy-start.14 = (f32[64,8,8]{2,1,0:T(8,128)}, f32[64,8,8]{2,1,0:T(8,128)S(1)}, u32[]{:S(2)}) copy-start(f32[64,8,8]{2,1,0:T(8,128)S(1)} %convert_element_type.185.valid_ref) | copy-start | bytes 49156
  4.2 17.5 %copy-start.23 = (bf16[104,640]{1,0:T(8,128)(2,1)}, bf16[104,640]{1,0:T(8,128)(2,1)S(1)}, u32[]{:S(2)}) copy-start(bf16[104,640]{1,0:T(8,128)(2,1)S(1)} %pad.50.xproj_ref) | copy-start | bytes 399364
  5.0 16.8 %copy-start.45 = (f32[4,640]{1,0:T(4,128)}, f32[4,640]{1,0:T(4,128)S(1)}, u32[]{:S(2)}) copy-start(f32[4,640]{1,0:T(4,128)S(1)} %pad_convert_fusion.taps_ref) | copy-start | bytes 30724
  5.0 19.9 %copy-start.54 = (f32[576,16]{0,1:T(8,128)S(1)}, f32[576,16]{0,1:T(8,128)}, u32[]{:S(2)}) copy-start(f32[576,16]{0,1:T(8,128)} %param.31) | copy-start | bytes 110596
  5.1 20.6 %copy-start.56 = (bf16[72,576]{1,0:T(8,128)(2,1)S(1)}, bf16[72,576]{1,0:T(8,128)(2,1)}, u32[]{:S(2)}) copy-start(bf16[72,576]{1,0:T(8,128)(2,1)} %param.29) | copy-start | bytes 248836
  5.1 21.2 %copy-start.61 = (f32[576]{0:T(1024)S(1)}, f32[576]{0:T(1024)}, u32[]{:S(2)}) copy-start(f32[576]{0:T(1024)} %param.30) | copy-start | bytes 6916
  25.0 25.4 %copy-start.52 = (bf16[576,1152]{1,0:T(8,128)(2,1)S(1)}, bf16[576,1152]{1,0:T(8,128)(2,1)}, u32[]{:S(2)}) copy-start(bf16[576,1152]{1,0:T(8,128)(2,1)} %param.33) | copy-start | bytes 3981316
  25.6 10.8 %copy-start.19 = (f32[16,640]{1,0:T(8,128)S(1)}, f32[16,640]{1,0:T(8,128)}, u32[]{:S(2)}) copy-start(f32[16,640]{1,0:T(8,128)} %pad.54.rate_ref.refs_2_) | copy-start | bytes 122884
  52.2 31.3 %copy-start.60 = (bf16[1152]{0:T(1024)(128)(2,1)S(1)}, bf16[1152]{0:T(1024)(128)(2,1)}, u32[]{:S(2)}) copy-start(bf16[1152]{0:T(1024)(128)(2,1)} %param.34) | copy-start | bytes 6916
  52.2 31.3 %copy-start.48 = (bf16[1152,8]{0,1:T(8,128)(2,1)S(1)}, bf16[1152,8]{0,1:T(8,128)(2,1)}, u32[]{:S(2)}) copy-start(bf16[1152,8]{0,1:T(8,128)(2,1)} %param.35) | copy-start | bytes 55300
  82.5 36.2 %copy-start.11 = (bf16[128,1152]{1,0:T(8,128)(2,1)}, bf16[128,1152]{1,0:T(8,128)(2,1)S(1)}, u32[]{:S(2)}) copy-start(bf16[128,1152]{1,0:T(8,128)(2,1)S(1)} %get-tuple-element.173.tokens_ref) | copy-start | bytes 884740
  85.4 21.9 %copy-start.35 = (bf16[128,1152]{1,0:T(8,128)(2,1)}, bf16[128,1152]{1,0:T(8,128)(2,1)S(1)}, u32[]{:S(2)}) copy-start(bf16[128,1152]{1,0:T(8,128)(2,1)S(1)} %get-tuple-element.110.normed_ref) | copy-start | bytes 884740
  118.7 17.9 %copy-start.50 = (s32[4]{0:T(128)S(1)}, s32[4]{0:T(128)}, u32[]{:S(2)}) copy-start(s32[4]{0:T(128)} %lengths_ref.1) | copy-start | bytes 52
  137.9 16.9 %copy-start.38 = (bf16[128,1152]{1,0:T(8,128)(2,1)}, bf16[128,1152]{1,0:T(8,128)(2,1)S(1)}, u32[]{:S(2)}) copy-start(bf16[128,1152]{1,0:T(8,128)(2,1)S(1)} %get-tuple-element.147.refs_1_) | copy-start | bytes 884740
  154.8 27.7 %copy-start.36 = (bf16[128,1152]{1,0:T(8,128)(2,1)S(1)}, bf16[128,1152]{1,0:T(8,128)(2,1)}, u32[]{:S(2)}) copy-start(bf16[128,1152]{1,0:T(8,128)(2,1)} %copy-done.35) | copy-start | bytes 884740
  183.0 11.6 %copy-start.28 = (f32[128,1152]{1,0:T(8,128)}, f32[128,1152]{1,0:T(8,128)S(1)}, u32[]{:S(2)}) copy-start(f32[128,1152]{1,0:T(8,128)S(1)} %get-tuple-element.113) | copy-start | bytes 1769476
  194.6 15.2 %copy-start.20 = (f32[16,640]{1,0:T(8,128)S(1)}, f32[16,640]{1,0:T(8,128)}, u32[]{:S(2)}) copy-start(f32[16,640]{1,0:T(8,128)} %pad.54.rate_ref.refs_2_) | copy-start | bytes 122884
  194.6 15.2 %copy-start.47 = (f32[8,640]{1,0:T(8,128)S(1)}, f32[8,640]{1,0:T(8,128)}, u32[]{:S(2)}) copy-start(f32[8,640]{1,0:T(8,128)} %get-tuple-element.97.refs_1_) | copy-start | bytes 61444
  226.8 42.7 %copy-start.37 = (f32[4,16,1152]{2,1,0:T(8,128)}, f32[4,16,1152]{2,1,0:T(8,128)S(1)}, u32[]{:S(2)}) copy-start(f32[4,16,1152]{2,1,0:T(8,128)S(1)} %get-tuple-element.140) | copy-start | bytes 884740
  292.1 27.3 %copy-start.7 = (bf16[8,32,1152]{2,1,0:T(8,128)(2,1)S(1)}, bf16[8,32,1152]{2,1,0:T(8,128)(2,1)}, u32[]{:S(2)}) copy-start(bf16[8,32,1152]{2,1,0:T(8,128)(2,1)} %copy-done.6) | copy-start | bytes 1769476
  292.1 27.3 %copy-start.41 = (bf16[72,1152]{1,0:T(8,128)(2,1)S(1)}, bf16[72,1152]{1,0:T(8,128)(2,1)}, u32[]{:S(2)}) copy-start(bf16[72,1152]{1,0:T(8,128)(2,1)} %get-tuple-element.145.refs_5_) | copy-start | bytes 497668
  320.8 38.9 %copy-start.51 = (bf16[4,256,768]{2,1,0:T(8,128)(2,1)S(1)}, bf16[4,256,768]{2,1,0:T(8,128)(2,1)}, u32[]{:S(2)}) copy-start(bf16[4,256,768]{2,1,0:T(8,128)(2,1)} %get-tuple-element.165) | copy-start | bytes 4718596
  367.7 32.6 %copy-start.21 = (bf16[8,72,1152]{2,1,0:T(8,128)(2,1)S(1)}, bf16[8,72,1152]{2,1,0:T(8,128)(2,1)}, u32[]{:S(2)}) copy-start(bf16[8,72,1152]{2,1,0:T(8,128)(2,1)} %get-tuple-element.155) | copy-start | bytes 3981316
  (42 other events, 115.6 us)

commit v5 on v4

--- a/solution.py
+++ b/solution.py
@@ -175,7 +175,7 @@
         out_specs=[pl.BlockSpec(memory_space=pl.ANY)] * len(items),
         scratch_shapes=[sem for item in items for sem in sems_of(item)],
         compiler_params=pltpu.CompilerParams(
-            collective_id=number, has_side_effects=True, vmem_limit_bytes=16 * MIB
+            collective_id=number, has_side_effects=True, vmem_limit_bytes=4 * MIB
         ),
     )(*[x for x, _, _ in exchanges])
 
@@ -246,7 +246,7 @@
             pltpu.SemaphoreType.DMA((count // 2,)),
         ],
         compiler_params=pltpu.CompilerParams(
-            collective_id=number, has_side_effects=True, vmem_limit_bytes=16 * MIB
+            collective_id=number, has_side_effects=True, vmem_limit_bytes=8 * MIB
         ),
     )(x)
 
@@ -330,14 +330,16 @@
     xs, riders, outs, rider_outs = take(many), take(number), take(many), take(number)
     tasks = [Share(axis, count, size, x, *take(7)) for (axis, count, size), x in zip(shares, xs)]
     axes = set(axes_of(items)) | {(axis, count) for axis, count, _ in shares}
-    pl.semaphore_wait(pltpu.get_barrier_semaphore(), greet(sorted(axes)))
+    told = greet(sorted(axes))
+    rider_sems = take(3 * number)
+    pl.semaphore_wait(pltpu.get_barrier_semaphore(), told)
     turns = {}
     for (axis, _, _), task in zip(shares, tasks):
         turns.setdefault(axis, []).extend((task, k) for k in range(task.groups))
     for turn in turns.values():
         for task, k in turn[:AHEAD]:
             task.begin(k)
-    under_way = Riders(items, riders, rider_outs, take(3 * number)).start()
+    under_way = Riders(items, riders, rider_outs, rider_sems).start()
     for i in range(max(len(turn) for turn in turns.values())):
         for turn in turns.values():
             if i < len(turn):
@@ -361,17 +363,19 @@
     scratch = []
     for x, axis, size, _ in shares:
         scratch += share_scratch(x, axis, size)
+    outs = [jax.ShapeDtypeStruct(x.shape[1:], kind) for x, _, _, kind in shares]
+    outs += [landed(x, item) for (x, _, _), item in zip(exchanges, items)]
+    scratch += [sem for item in items for sem in sems_of(item)]
     return pl.pallas_call(
         functools.partial(
             share_kernel, [(axis, lax.axis_size(axis), size) for _, axis, size, _ in shares], items
         ),
-        out_shape=[jax.ShapeDtypeStruct(x.shape[1:], kind) for x, _, _, kind in shares]
-        + [landed(x, item) for (x, _, _), item in zip(exchanges, items)],
+        out_shape=outs,
         in_specs=held + anywhere,
         out_specs=held + anywhere,
-        scratch_shapes=scratch + [sem for item in items for sem in sems_of(item)],
+        scratch_shapes=scratch,
         compiler_params=pltpu.CompilerParams(
-            collective_id=number, has_side_effects=True, vmem_limit_bytes=32 * MIB
+            collective_id=number, has_side_effects=True, vmem_limit_bytes=18 * MIB
         ),
     )(*[share[0] for share in shares], *[x for x, _, _ in exchanges])
 
@@ -522,7 +526,7 @@
         ]
         + [sem for item in items for sem in sems_of(item)],
         compiler_params=pltpu.CompilerParams(
-            collective_id=number, has_side_effects=True, vmem_limit_bytes=24 * MIB
+            collective_id=number, has_side_effects=True, vmem_limit_bytes=10 * MIB
         ),
     )(local, sums, rate, *[x for x, _, _ in exchanges])
 
@@ -577,12 +581,12 @@
     return lax.dot_general(a, b, (((0,), (0,)), ((), ())), preferred_element_type=f32)
 
 
-def front_kernel(seq_count, chan_count, tokens_ref, gain_ref, w_ref, taps_ref, bias_ref, xproj_ref, valid_ref,
+def front_kernel(seq_count, chan_count, states, taps, tokens_ref, gain_ref, w_ref, params_ref, xproj_ref, valid_ref,
                  normed_ref, ext_ref, pre_ref, gate_ref, mapped_ref,
                  halo, part, beside_in, pair, far_in, halo_send, halo_recv, send_sem, recv_sem):
     seqs, group, width = tokens_ref.shape
     steps, lines, full = pre_ref.shape
-    taps, inner = taps_ref.shape[0], w_ref.shape[1]
+    inner = w_ref.shape[1]
     rim, rows, tail = taps - 1, steps * lines, halo.shape[1]
     here, me = lax.axis_index("seq"), lax.axis_index("chan")
     beside = me + 1 - 2 * lax.rem(me, 2)
@@ -645,9 +649,10 @@
     for j in range(rim):
         own = turned(ext_ref[steps + j, :, pl.ds(0, inner)])
         ext_ref[j, :, pl.ds(0, inner)] = jnp.where(upper, own, prior[j])
-    pre = jnp.broadcast_to(bias_ref[...], (steps, lines, full))
+    pre = jnp.broadcast_to(params_ref[pl.ds(states + taps, 1), :], (steps, lines, full))
     for k in range(taps):
-        pre = pre + taps_ref[k : k + 1, :] * ext_ref[pl.ds(k, steps)] * valid_ref[:, :, k : k + 1]
+        tap = params_ref[pl.ds(states + k, 1), :]
+        pre = pre + tap * ext_ref[pl.ds(k, steps)] * valid_ref[:, :, k : k + 1]
     pre_ref[...] = pre
     act_low = (pre * sigmoid(pre)).astype(bf16).reshape(rows, full)
     part[...] = dot_nt(act_low, xproj_ref[...]).astype(bf16)
@@ -690,21 +695,21 @@
         ends.wait_send()
 
 
-def front(tokens, gain, w_in, taps, bias, xproj, valid, full, number):
+def front(tokens, gain, w_in, params, states, taps, xproj, valid, full, number):
     seqs, group, width = tokens.shape
     steps, lines = valid.shape[:2]
     count, rows, maps = lax.axis_size("chan"), steps * lines, xproj.shape[0]
     tail = min(16, group)
     return pl.pallas_call(
-        functools.partial(front_kernel, lax.axis_size("seq"), count),
+        functools.partial(front_kernel, lax.axis_size("seq"), count, states, taps),
         out_shape=[
             jax.ShapeDtypeStruct((rows, width), bf16),
-            jax.ShapeDtypeStruct((steps + taps.shape[0] - 1, lines, full), f32),
+            jax.ShapeDtypeStruct((steps + taps - 1, lines, full), f32),
             jax.ShapeDtypeStruct((steps, lines, full), f32),
             jax.ShapeDtypeStruct((steps, lines, full), f32),
             jax.ShapeDtypeStruct((rows, maps), bf16),
         ],
-        in_specs=[pl.BlockSpec(memory_space=pltpu.VMEM)] * 7,
+        in_specs=[pl.BlockSpec(memory_space=pltpu.VMEM)] * 6,
         out_specs=[pl.BlockSpec(memory_space=pltpu.VMEM)] * 5,
         scratch_shapes=[
             pltpu.VMEM((seqs, tail, width), bf16),
@@ -718,12 +723,12 @@
             pltpu.SemaphoreType.DMA((count // 2,)),
         ],
         compiler_params=pltpu.CompilerParams(
-            collective_id=number, has_side_effects=True, vmem_limit_bytes=48 * MIB
+            collective_id=number, has_side_effects=True, vmem_limit_bytes=36 * MIB
         ),
-    )(tokens, gain, w_in, taps, bias, xproj, valid)
-
-
-def totals_kernel(rank, taps, pre_ref, mapped_ref, dtw_ref, bias_ref, valid_ref, rate_ref,
+    )(tokens, gain, w_in, params, xproj, valid)
+
+
+def totals_kernel(rank, taps, pre_ref, mapped_ref, dtw_ref, valid_ref, rate_ref,
                   dt_ref, step_ref, drive_ref, last_ref, sums_ref, wide):
     count, steps, rows, lanes = wide.shape
 
@@ -731,7 +736,8 @@
     def _():
         spread(mapped_ref, rank, wide)
 
-    dt_pre = (dot(mapped_ref[...], dtw_ref[...]) + bias_ref[...]).reshape(steps, rows, lanes)
+    bias = rate_ref[pl.ds(count + taps + 1, 1), :]
+    dt_pre = (dot(mapped_ref[...], dtw_ref[...]) + bias).reshape(steps, rows, lanes)
     delta = softplus(dt_pre)
     pre = pre_ref[...]
     dt_ref[...] = dt_pre
@@ -754,7 +760,12 @@
     sums_ref[...] = sums
 
 
-def states_kernel(rank, seqs, step_ref, drive_ref, mapped_ref, rate_ref, enter_ref, pre_ref, gate_ref, skip_ref, out_w_ref,
+def known(rows_ref, size):
+    row = pl.program_id(0) * rows_ref.shape[0] + lax.broadcasted_iota(jnp.int32, rows_ref.shape, 0)
+    return jnp.where(row < size, rows_ref[...].astype(f32), 0.0).astype(rows_ref.dtype)
+
+
+def states_kernel(rank, seqs, taps, inner, step_ref, drive_ref, mapped_ref, rate_ref, enter_ref, pre_ref, gate_ref, out_w_ref,
                   y_ref, gated_ref, state_ref, out_ref, wide_in, wide_read, total):
     count, steps, rows, lanes = wide_in.shape
     place = pl.program_id(0)
@@ -782,11 +793,11 @@
 
     lax.fori_loop(0, steps, one, tuple(enter_ref[n] for n in range(count)), unroll=2)
     pre, gate = pre_ref[...], gate_ref[...]
-    y_full = y_ref[...] + skip_ref[...] * (pre * sigmoid(pre))
+    y_full = y_ref[...] + rate_ref[pl.ds(count + taps + 2, 1), :] * (pre * sigmoid(pre))
     y_ref[...] = y_full
     gated = (y_full * (gate * sigmoid(gate))).astype(bf16).reshape(steps * rows, lanes)
     gated_ref[...] = gated
-    total[...] += dot(gated, out_w_ref[...])
+    total[...] += dot(gated, known(out_w_ref, inner))
 
     @pl.when(place == pl.num_programs(0) - 1)
     def _():
@@ -794,7 +805,7 @@
         out_ref[...] = dot_tn(perm, total[...].astype(bf16)).astype(bf16)
 
 
-def back_totals_kernel(rank, seqs, step_ref, mapped_ref, rate_ref, mixed_ref, normed_ref, out_w_ref, gate_ref, y_ref, gated_ref,
+def back_totals_kernel(rank, seqs, inner, step_ref, mapped_ref, rate_ref, mixed_ref, normed_ref, out_w_ref, gate_ref, y_ref, gated_ref,
                        pre_ref, grad_y_ref, grad_z_ref, grad_out_ref, grad_gate_ref, skip_ref, last_ref,
                        wide, mixed):
     count, steps, rows, lanes = wide.shape
@@ -804,7 +815,7 @@
         spread(mapped_ref, rank + count, wide)
         mixed[...] = dot(perm_of(steps, rows, seqs), mixed_ref[...]).astype(bf16)
 
-    grad_gated = dot_nt(mixed[...], out_w_ref[...]).reshape(steps, rows, lanes)
+    grad_gated = dot_nt(mixed[...], known(out_w_ref, inner)).reshape(steps, rows, lanes)
     gate, pre = gate_ref[...], pre_ref[...]
     sigma = sigmoid(gate)
     grad_y = grad_gated * (gate * sigma)
@@ -952,14 +963,14 @@
         under_way.finish()
 
 
-def conv_back_kernel(taps, grad_mapped_ref, grad_y_ref, side_ref, pre_ref, ext_ref, skip_ref, xproj_ref, taps_ref, valid_ref,
+def conv_back_kernel(states, taps, grad_mapped_ref, grad_y_ref, side_ref, pre_ref, ext_ref, params_ref, xproj_ref, valid_ref,
                      grad_ref, rim_ref, grad_xproj_ref, sums_ref, ext_grad):
     steps, rows, lanes = pre_ref.shape
     rim = taps - 1
     pre = pre_ref[...]
     sigma = sigmoid(pre)
     grad_act = dot(grad_mapped_ref[...], xproj_ref[...]).reshape(steps, rows, lanes)
-    grad_act = grad_act + grad_y_ref[...] * skip_ref[...] + side_ref[...]
+    grad_act = grad_act + grad_y_ref[...] * params_ref[pl.ds(states + taps + 2, 1), :] + side_ref[...]
     grad_pre = grad_act * silu_slope(pre, sigma)
     act_low = (pre * sigma).astype(bf16).reshape(steps * rows, lanes)
     grad_xproj_ref[...] = dot_tn(grad_mapped_ref[...], act_low)
@@ -967,7 +978,7 @@
     for k in range(taps):
         masked = grad_pre * valid_ref[:, :, k : k + 1]
         sums_ref[k] = jnp.sum(masked * ext_ref[pl.ds(k, steps)], axis=0)
-        ext_grad[pl.ds(k, steps)] += masked * taps_ref[k : k + 1, :]
+        ext_grad[pl.ds(k, steps)] += masked * params_ref[pl.ds(states + k, 1), :]
     sums_ref[taps] = jnp.sum(grad_pre, axis=0)
     upper = lax.broadcasted_iota(jnp.int32, (rows, lanes), 0) >= rows // 2
     for j in range(rim):
@@ -1063,7 +1074,7 @@
         ]
         + [sem for item in items for sem in sems_of(item)],
         compiler_params=pltpu.CompilerParams(
-            collective_id=number, has_side_effects=True, vmem_limit_bytes=48 * MIB
+            collective_id=number, has_side_effects=True, vmem_limit_bytes=36 * MIB
         ),
     )(tokens, grad, rim, grad_z, normed, w_in, *[x for x, _, _ in exchanges])
 
@@ -1148,7 +1159,7 @@
         in_specs=[pl.BlockSpec(memory_space=space) for space in spaces],
         out_specs=[pl.BlockSpec(memory_space=pltpu.VMEM)] * len(outs),
         out_shape=[jax.ShapeDtypeStruct(shape, dtype) for shape, dtype in outs],
-        compiler_params=pltpu.CompilerParams(vmem_limit_bytes=32 * MIB),
+        compiler_params=pltpu.CompilerParams(vmem_limit_bytes=12 * MIB),
         cost_estimate=pl.CostEstimate(flops=1000, bytes_accessed=1000, transcendentals=0),
     )(*ins)
 
@@ -1230,32 +1241,32 @@
     )(x, first, second, *([slope] if back else []))
 
 
-def widen_kernel(conv_ref, gate_ref, out_ref, tokens_ref, grad_in_ref, grad_out_ref, grad_tokens_ref):
-    grad_in_ref[0] = conv_ref[...].astype(f32)
-    grad_in_ref[1] = gate_ref[...].astype(f32)
-    grad_out_ref[...] = out_ref[...].astype(f32)
-    grad_tokens_ref[...] = tokens_ref[...].astype(f32)
-
-
-def widened(conv, gate, out, tokens, inner):
-    width, rows = conv.shape[1], tokens.shape[0]
-    pieces = next(n for n in (4, 2, 1) if inner % (16 * n) == 0 and rows % (16 * n) == 0)
-    each, lines = inner // pieces, rows // pieces
-    block = pl.BlockSpec((each, width), lambda i: (i, 0))
-    row_block = pl.BlockSpec((lines, width), lambda i: (i, 0))
+def widen_kernel(conv_ref, gate_ref, *refs):
+    half = len(refs) // 2
+    refs[half][0] = conv_ref[...].astype(f32)
+    refs[half][1] = gate_ref[...].astype(f32)
+    for x_ref, o_ref in zip(refs[:half], refs[half + 1 :]):
+        o_ref[...] = x_ref[...].astype(f32)
+
+
+def widened(conv, gate, *arrays):
+    sizes = [x.shape[0] for x in (conv, *arrays)]
+    pieces = next(n for n in (6, 4, 3, 2, 1) if all(size % (16 * n) == 0 for size in sizes) or n == 1)
+
+    def block(x):
+        return pl.BlockSpec((x.shape[0] // pieces, x.shape[1]), lambda i: (i, 0))
+
+    each, width = conv.shape[0] // pieces, conv.shape[1]
     return pl.pallas_call(
         widen_kernel,
         grid=(pieces,),
-        in_specs=[block] * 3 + [row_block],
-        out_specs=[pl.BlockSpec((2, each, width), lambda i: (0, i, 0)), block, row_block],
-        out_shape=[
-            jax.ShapeDtypeStruct((2, inner, width), f32),
-            jax.ShapeDtypeStruct((inner, width), f32),
-            jax.ShapeDtypeStruct((rows, width), f32),
-        ],
-        compiler_params=pltpu.CompilerParams(vmem_limit_bytes=48 * MIB),
+        in_specs=[block(x) for x in (conv, gate, *arrays)],
+        out_specs=[pl.BlockSpec((2, each, width), lambda i: (0, i, 0))] + [block(x) for x in arrays],
+        out_shape=[jax.ShapeDtypeStruct((2,) + conv.shape, f32)]
+        + [jax.ShapeDtypeStruct(x.shape, f32) for x in arrays],
+        compiler_params=pltpu.CompilerParams(vmem_limit_bytes=20 * MIB),
         cost_estimate=pl.CostEstimate(flops=1000, bytes_accessed=1000, transcendentals=0),
-    )(conv, gate, out, tokens)
+    )(conv, gate, *arrays)
 
 
 def block_of(shape, kind):
@@ -1282,7 +1293,7 @@
     ]
 
 
-def by_tiles(kernel, full, ins, outs, scratch, more=(), params=None):
+def by_tiles(kernel, room, full, ins, outs, scratch, more=(), params=None):
     return pl.pallas_call(
         kernel,
         grid=(full // LANES,),
@@ -1290,7 +1301,7 @@
         out_specs=[block_of(shape, kind) for shape, _, kind in outs],
         out_shape=[jax.ShapeDtypeStruct(shape, dtype) for shape, dtype, _ in outs],
         scratch_shapes=[pltpu.VMEM(shape, dtype) for shape, dtype in scratch] + list(more),
-        compiler_params=pltpu.CompilerParams(vmem_limit_bytes=58 * MIB, **(params or {})),
+        compiler_params=pltpu.CompilerParams(vmem_limit_bytes=room * MIB, **(params or {})),
         cost_estimate=pl.CostEstimate(flops=1000, bytes_accessed=1000, transcendentals=0),
     )(*[a for a, _ in ins])
 
@@ -1370,19 +1381,19 @@
     w_in = in_weight.transpose(1, 2, 0)
     router_rows = router_weight.T
     gain_one = norm1_gain.astype(f32)
-    taps_full = padded(conv_weight.astype(f32))
     xproj_rows = padded(xproj_weight.T)
     dt_rows = jnp.pad(padded(dt_weight), ((0, maps - rank), (0, 0)))
-    skip_row = padded(skip_weight[None])
-    out_rows = jnp.pad(out_weight, ((0, full - inner), (0, 0)))
     rate = -jnp.exp(a_log.T)
-    rate_two = padded(rate * log2e)
+    params = [rate * log2e, conv_weight, conv_bias[None], dt_bias[None], skip_weight[None]]
+    params = jnp.concatenate([x.astype(f32) for x in params], axis=0)
+    params = jnp.pad(params, ((0, -params.shape[0] % 8), (0, full - inner)))
     normed_one, extended, pre_act, gate_z, mapped = front(
         tokens,
         gain_one[None],
         w_in,
-        taps_full,
-        padded(conv_bias.astype(f32)[None]),
+        params,
+        states,
+        taps,
         xproj_rows,
         valid,
         full,
@@ -1391,14 +1402,14 @@
     act_shape, state_shape, wide_shape = (steps, lines, full), (states, lines, full), (states, steps, lines, LANES)
     dt_pre, step_size, drive, own_states, sums = by_tiles(
         functools.partial(totals_kernel, rank, taps),
+        20,
         full,
         [
             (pre_act, "tile"),
             (mapped, "whole"),
             (dt_rows, "tile"),
-            (padded(dt_bias[None]), "tile"),
             (valid, "whole"),
-            (rate_two, "tile"),
+            (params, "tile"),
         ],
         [
             (act_shape, f32, "tile"),
@@ -1409,20 +1420,20 @@
         ],
         [(wide_shape, f32)],
     )
-    (enter,) = carried(own_states, sums, rate_two, "seq", False, 2)
+    (enter,) = carried(own_states, sums, params, "seq", False, 2)
     y_full, gated, state, out_part = by_tiles(
-        functools.partial(states_kernel, rank, seqs),
+        functools.partial(states_kernel, rank, seqs, taps, inner),
+        36,
         full,
         [
             (step_size, "tile"),
             (drive, "tile"),
             (mapped, "whole"),
-            (rate_two, "tile"),
+            (params, "tile"),
             (enter, "tile"),
             (pre_act, "tile"),
             (gate_z, "tile"),
-            (skip_row, "tile"),
-            (out_rows, "rows"),
+            (out_weight, "rows"),
         ],
         [
             (act_shape, f32, "tile"),
@@ -1514,15 +1525,16 @@
 
     (grad_mixed,) = exchange(8, (grad_low, 2, "chan"))
     grad_y, grad_z, grad_out_w, grad_in_gate, skip_sums, back_last = by_tiles(
-        functools.partial(back_totals_kernel, rank, seqs),
+        functools.partial(back_totals_kernel, rank, seqs, inner),
+        28,
         full,
         [
             (step_size, "tile"),
             (mapped, "whole"),
-            (rate_two, "tile"),
+            (params, "tile"),
             (grad_mixed.reshape(rows, width), "whole"),
             (normed_one, "whole"),
-            (out_rows, "rows"),
+            (out_weight, "rows"),
             (gate_z, "tile"),
             (y_full, "tile"),
             (gated, "tile"),
@@ -1539,7 +1551,7 @@
         [(wide_shape, f32), ((rows, width), bf16)],
     )
     back_enter, shared = carried(
-        back_last, sums, rate_two, "seq", True, 9, (shared, "gather", "chan")
+        back_last, sums, params, "seq", True, 9, (shared, "gather", "chan")
     )
     shared = jnp.sum(shared, axis=0).reshape(-1, LANES)
     def cut_rows(x, unit):
@@ -1552,13 +1564,14 @@
     items = items_of(riders)
     side, log_sums, bias_sums, grad_dt_w, low_part, by_out, by_gate, hidden_all, grad_pre_all = by_tiles(
         functools.partial(back_kernel, rank, full // LANES, [("seq", n_seq, across)] * 2, items),
+        46,
         full,
         [
             (step_size, "tile"),
             (drive, "tile"),
             (grad_y, "tile"),
             (mapped, "whole"),
-            (rate_two, "tile"),
+            (params, "tile"),
             (enter, "tile"),
             (state, "tile"),
             (back_enter, "tile"),
@@ -1594,7 +1607,8 @@
     )
     grad_mapped = summed_over(low_part, "chan", 10).astype(bf16)
     grad_conv_in, rims, grad_xproj, conv_sums = by_tiles(
-        functools.partial(conv_back_kernel, taps),
+        functools.partial(conv_back_kernel, states, taps),
+        20,
         full,
         [
             (grad_mapped, "whole"),
@@ -1602,9 +1616,8 @@
             (side, "tile"),
             (pre_act, "tile"),
             (extended, "tile"),
-            (skip_row, "tile"),
+            (params, "tile"),
             (xproj_rows, "tile"),
-            (taps_full, "tile"),
             (valid, "whole"),
         ],
         [
@@ -1646,6 +1659,8 @@
         (by_out, across, "seq"),
         (grad_rows, 2, "chan"),
     )
+    grad_first = dot_tn(flat(rows_all), flat(grad_pre_all))
+    grad_second = dot_tn(flat(hidden_all), flat(grad_rows_all))
     grad_gain_one = jnp.sum(grad_gain_one, axis=0)
     tokens_full = tokens_own.astype(f32)
     inverse_one = lax.rsqrt(jnp.mean(tokens_full * tokens_full, axis=-1, keepdims=True) + epsilon)
@@ -1660,13 +1675,13 @@
         (by_conv, across, "seq"),
         (grad_gain_one, "gather", "seq"),
     ]
+    grad_first, grad_second, grad_low = lax.optimization_barrier((grad_first, grad_second, moved[0][0]))
+    moved[0] = (grad_low,) + moved[0][1:]
     moved = exchange(12, *moved)
-    grad_first = dot_tn(flat(rows_all), flat(grad_pre_all))
-    grad_second = dot_tn(flat(hidden_all), flat(grad_rows_all))
     grad_tokens, layer_out, small, middle, by_conv, grad_gain_one = moved
     grad_gain_one = jnp.sum(grad_gain_one, axis=(0, 1))
     summed_in, summed_out, grad_tokens = widened(
-        flat(by_conv), flat(by_gate), flat(by_out), flat(grad_tokens), inner
+        flat(by_conv)[:inner], flat(by_gate)[:inner], flat(by_out)[:inner], flat(grad_tokens)
     )
     middle = flat(middle)[:, :inner].astype(f32)
     small = flat(small)

time: 412 us -> 403 us (0.978)
  Pallas kernels: 357 us -> 338 us
  local copies, waits for them, and re-layouts: 37.1 us -> 46.5 us
    pallas_call x5, Pallas kernels: 91 us -> 79 us  [by_tiles(): pl.pallas_call(kernel, grid=(full // LANES,), in_specs=[block_of(a.shape,...]
    unnamed x133 -> x171, local copies, waits for them, and re-layouts: 22.9 us -> 33.5 us
where the time goes in v5:
time: 403 us; the launch traced here: 402 us
  Pallas kernels  338 us (84%)
  local copies, waits for them, and re-layouts  46.5 us (12%)
  other arithmetic  8.23 us (2%)
  matrix products  7.92 us (2%)
    pallas_call x6, Pallas kernels, exchange(): pl.pallas_call(functools.partial(exchange_kernel, items), out_shape=[land...  110 us
    pallas_call x5, Pallas kernels, by_tiles(): pl.pallas_call(kernel, grid=(full // LANES,), in_specs=[block_of(a.shape,...  79 us
    pallas_call x2, Pallas kernels, share_of(): pl.pallas_call(functools.partial(share_kernel, [(axis, lax.axis_size(axis...  49.4 us
    unnamed x171, local copies, waits for them, and re-layouts  33.5 us
    pallas_call x2, Pallas kernels, carried(): pl.pallas_call(functools.partial(carry_kernel, axis, count, back, items),...  26.7 us
    pallas_call x1, Pallas kernels, ends(): pl.pallas_call(functools.partial(ends_kernel, lax.axis_size('seq'), items...  24.4 us
    pallas_call x2, Pallas kernels, expert(): pl.pallas_call(expert_back_kernel if back else expert_kernel, grid=(parts...  21.4 us
    pallas_call x1, Pallas kernels, front(): pl.pallas_call(functools.partial(front_kernel, lax.axis_size('seq'), coun...  13.8 us

profile of v5, /device:TPU:0, one launch (start us, length us, event | category | flops | bytes accessed | tf_op | source)
XLA Modules:
  0.0 402.2 jit_solution(9540979981089988828)
XLA Ops:
  6.8 1.8 copy-done.6
  9.9 13.8 %shard_map.314 = (bf16[512,1152]{1,0:T(8,128)(2,1)S(1)}, f32[67,8,640]{2,1,0:T(8,128)S(1)}, f32[64,8,640]{2,1,0:T(8,128)S(1)}, f32[64,8,640]{2,1,0:T(8,128)S(1)}, bf16[512,104]{1,0:T(8,128)(2,1)S(1)}) custom-call(bf16[4,128,1152]{2,1,0:T(8,128)(2,1)S(1)} %copy-done.8, f32[1,1152]{1,0:T(1,128)S(1)} %broadcast_in_dim.35.gain_ref, ...), custom_call_target="tpu_custom_call" | custom-call | tf_op jit(solution)/shard_map/pallas_call | solution.py:703
  25.8 7.9 %shard_map.315 = (f32[64,8,640]{2,1,0:T(8,128)S(1)}, f32[64,8,640]{2,1,0:T(8,128)S(1)}, f32[64,8,640]{2,1,0:T(8,128)S(1)}, f32[16,8,640]{2,1,0:T(8,128)S(1)}, f32[8,640]{1,0:T(8,128)S(1)}) custom-call(f32[64,8,640]{2,1,0:T(8,128)S(1)} %get-tuple-element.95.pre_ref, bf16[512,104]{1,0:T(8,128)(2,1)S(1)} %get-tuple-element.96.mapped_ref, ...), custom_call_target="tpu_custom_call" | custom-call | flops 1000 | bytes 1000 | tf_op jit(solution)/shard_map/pallas_call | solution.py:1297
  34.8 11.5 %shard_map.316.enter_ref.first_ref = f32[16,8,640]{2,1,0:T(8,128)S(1)} custom-call(f32[16,8,640]{2,1,0:T(8,128)S(1)} %get-tuple-element.99.refs_0_, f32[8,640]{1,0:T(8,128)S(1)} %get-tuple-element.100.refs_1_, f32[24,640]{1,0:T(8,128)S(1)} %pad.24.params_ref.rate_ref.refs_2_), custom_call_target="tpu_custom_call" | custom-call | tf_op jit(solution)/shard_map/pallas_call | solution.py:509
  46.3 14.7 %shard_map.317 = (f32[64,8,640]{2,1,0:T(8,128)S(1)}, bf16[512,640]{1,0:T(8,128)(2,1)S(1)}, f32[64,16,8,640]{3,2,1,0:T(8,128)}, bf16[512,1152]{1,0:T(8,128)(2,1)S(1)}) custom-call(f32[64,8,640]{2,1,0:T(8,128)S(1)} %get-tuple-element.97.step_ref, f32[64,8,640]{2,1,0:T(8,128)S(1)} %get-tuple-element.98.drive_ref, ...), custom_call_target="tpu_custom_call" | custom-call | flops 1000 | bytes 1000 | tf_op jit(solution)/shard_map/pallas_call | solution.py:1297
  62.9 10.9 %shard_map.318.mixed_ref = f32[128,1152]{1,0:T(8,128)S(1)} custom-call(bf16[4,128,1152]{2,1,0:T(8,128)(2,1)S(1)} %bitcast.76), custom_call_target="tpu_custom_call" | custom-call | tf_op jit(solution)/shard_map/pallas_call | solution.py:369
  79.4 21.9 %shard_map.320 = bf16[8,32,1152]{2,1,0:T(8,128)(2,1)S(1)} custom-call(bf16[8,32,1152]{2,1,0:T(8,128)(2,1)S(1)} %bitcast.80), custom_call_target="tpu_custom_call" | custom-call | tf_op jit(solution)/shard_map/pallas_call | solution.py:171
  102.1 10.5 %shard_map.321 = (bf16[4,256,768]{2,1,0:T(8,128)(2,1)}, bf16[256,3072]{1,0:T(8,128)(2,1)}, bf16[256,1152]{1,0:T(8,128)(2,1)}) custom-call(bf16[256,1152]{1,0:T(8,128)(2,1)} %bitcast.61, bf16[1152,3072]{1,0:T(8,128)(2,1)} %bitcast.92, bf16[3072,1152]{1,0:T(8,128)(2,1)} %bitcast.94), custom_call_target="tpu_custom_call" | custom-call | flops 1000 | bytes 1000 | tf_op jit(solution)/shard_map/pallas_call | solution.py:1230
  113.8 16.8 %shard_map.322 = bf16[8,32,1152]{2,1,0:T(8,128)(2,1)S(1)} custom-call(bf16[8,32,1152]{2,1,0:T(8,128)(2,1)S(1)} %bitcast.81), custom_call_target="tpu_custom_call" | custom-call | tf_op jit(solution)/shard_map/pallas_call | solution.py:171
  131.9 16.1 %shard_map.324 = bf16[8,32,1152]{2,1,0:T(8,128)(2,1)S(1)} custom-call(bf16[8,32,1152]{2,1,0:T(8,128)(2,1)S(1)} %bitcast.79), custom_call_target="tpu_custom_call" | custom-call | tf_op jit(solution)/shard_map/pallas_call | solution.py:171
  148.9 10.8 %shard_map.325 = (bf16[4,256,768]{2,1,0:T(8,128)(2,1)}, bf16[256,1152]{1,0:T(8,128)(2,1)}) custom-call(bf16[256,1152]{1,0:T(8,128)(2,1)} %bitcast.63, bf16[1152,3072]{1,0:T(8,128)(2,1)} %bitcast.93, bf16[3072,1152]{1,0:T(8,128)(2,1)} %bitcast.95, bf16[256,3072]{1,0:T(8,128)(2,1)} %get-tuple-element.110.slope_ref), custom_call_target="tpu_custom_call" | custom-call | flops 1000 | bytes 1000 | tf_op jit(solution)/shard_map/pallas_call | solution.py:1230
  160.9 15.8 %shard_map.326 = bf16[8,32,1152]{2,1,0:T(8,128)(2,1)S(1)} custom-call(bf16[8,32,1152]{2,1,0:T(8,128)(2,1)S(1)} %bitcast.82), custom_call_target="tpu_custom_call" | custom-call | tf_op jit(solution)/shard_map/pallas_call | solution.py:171
  178.4 10.5 %shard_map.328 = bf16[4,128,1152]{2,1,0:T(8,128)(2,1)S(1)} custom-call(bf16[128,1152]{1,0:T(8,128)(2,1)S(1)} %get-tuple-element.116.refs_0_), custom_call_target="tpu_custom_call" | custom-call | tf_op jit(solution)/shard_map/pallas_call | solution.py:171
  191.4 13.1 %shard_map.329 = (f32[64,8,640]{2,1,0:T(8,128)S(1)}, bf16[512,640]{1,0:T(8,128)(2,1)S(1)}, bf16[576,1152]{1,0:T(8,128)(2,1)S(1)}, bf16[576,1152]{1,0:T(8,128)(2,...) custom-call(f32[64,8,640]{2,1,0:T(8,128)S(1)} %copy-done.5, bf16[512,104]{1,0:T(8,128)(2,1)S(1)} %get-tuple-element.96.mapped_ref, ...), custom_call_target="tpu_custom_call" | custom-call | flops 1000 | bytes 1000 | tf_op jit(solution)/shard_map/pallas_call | solution.py:1297
  207.5 15.3 %shard_map.330 = (f32[16,8,640]{2,1,0:T(8,128)S(1)}, f32[4,16,1152]{2,1,0:T(8,128)S(1)}) custom-call(f32[16,8,640]{2,1,0:T(8,128)S(1)} %get-tuple-element.122.refs_0_, f32[8,640]{1,0:T(8,128)S(1)} %get-tuple-element.100.refs_1_, f32[24,640]{1,0:T(8,128)S(1)} %pad.24.params_ref.rate_ref.refs_2_, f32[16,1152]{1,0:T(8,128)S(1)} %get-tuple-element.123.refs_3_), custom_call_target="tpu_custom_call" | custom-call | tf_op jit(solution)/shard_map/pallas_call | solution.py:509
  222.9 40.3 %shard_map.331 = (f32[64,8,640]{2,1,0:T(8,128)S(1)}, f32[16,8,640]{2,1,0:T(8,128)S(1)}, f32[8,640]{1,0:T(8,128)S(1)}, f32[104,640]{1,0:T(8,128)S(1)}, bf16[512,1...) custom-call(f32[64,8,640]{2,1,0:T(8,128)S(1)} %copy-done.5, ...), custom_call_target="tpu_custom_call" | custom-call | flops 1000 | bytes 1000 | tf_op jit(solution)/shard_map/pallas_call | solution.py:1297
  263.3 5.9 %shard_map.332 = f32[512,104]{1,0:T(8,128)S(1)} custom-call(bf16[512,104]{1,0:T(8,128)(2,1)S(1)} %get-tuple-element.130.x_ref), custom_call_target="tpu_custom_call" | custom-call | tf_op jit(solution)/shard_map/pallas_call | solution.py:236
  269.2 2.9 shard_map.333
  287.5 24.4 %shard_map.334 = (bf16[576,1152]{1,0:T(8,128)(2,1)S(1)}, bf16[512,1152]{1,0:T(8,128)(2,1)S(1)}, f32[1,1152]{1,0:T(1,128)S(1)}, bf16[8,72,1152]{2,1,0:T(8,128)(2,1)S(1)}, bf16[4,256,1152]{2,1,0:T(8,128)(2,1)S(1)}) custom-call(bf16[4,128,1152]{2,1,0:T(8,128)(2,1)S(1)} %copy-done.9, f32[64,8,640]{2,1,0:T(8,128)S(1)} %copy-done.40, f32[3,8,640]{2,1,0:T(8,128)S(1)} %copy-done.70, ...), custom_call_target="tpu_custom_call" | custom-call | tf_op jit(solution)/shard_map/pallas_call | solution.py:1060
  312.0 38.4 %shard_map.335 = (f32[128,1152]{1,0:T(8,128)S(1)}, f32[40,128]{1,0:T(8,128)S(1)}, bf16[32,640]{1,0:T(8,128)(2,1)S(1)}, bf16[72,1152]{1,0:T(8,128)(2,1)S(1)}, f32...) custom-call(bf16[4,128,1152]{2,1,0:T(8,128)(2,1)S(1)} %bitcast.77, ...), custom_call_target="tpu_custom_call" | custom-call | tf_op jit(solution)/shard_map/pallas_call | solution.py:369
  352.0 4.0 %convolution_bitcast_fusion = f32[768,1152]{1,0:T(8,128)} fusion(bf16[4,256,768]{2,1,0:T(8,128)(2,1)S(1)} %copy-done.78, bf16[4,256,1152]{2,1,0:T(8,128)(2,1)S(1)} %get-tuple-element.151), kind=kOutput, calls=%fused_computation | convolution fusion | flops 1811939328 | bytes 7471104 | tf_op jit(solution)/shard_map/dot_general | solution.py:581
  356.1 3.9 convolution_bitcast_fusion.1
  361.0 29.3 %shard_map.336 = (bf16[4,128,1152]{2,1,0:T(8,128)(2,1)S(1)}, bf16[4,128,1152]{2,1,0:T(8,128)(2,1)S(1)}, f32[8,40,128]{2,1,0:T(8,128)S(1)}, bf16[8,32,640]{2,1,0:...) custom-call(bf16[128,1152]{1,0:T(8,128)(2,1)S(1)} %fusion.8.refs_0_, ...), custom_call_target="tpu_custom_call" | custom-call | tf_op jit(solution)/shard_map/pallas_call | solution.py:171
  391.3 4.1 %shard_map.337 = (f32[2,576,1152]{2,1,0:T(8,128)}, f32[576,1152]{1,0:T(8,128)}, f32[512,1152]{1,0:T(8,128)}) custom-call(bf16[576,1152]{1,0:T(8,128)(2,1)S(1)} %bitcast.72, bf16[576,1152]{1,0:T(8,128)(2,1)S(1)} %bitcast.70, bf16[576,1152]{1,0:T(8,128)(2,1)S(1)} %bitcast.71, bf16[512,1152]{1,0:T(8,128)(2,1)S(1)} %bitcast.75), custom_call_target="tpu_custom_call" | custom-call | flops 1000 | bytes 1000 | tf_op jit(solution)/shard_map/pallas_call | solution.py:1260
  (230 shorter events, 55.7 us)
Async XLA Ops:
  0.7 129.9 %copy-start = (bf16[4,128,1152]{2,1,0:T(8,128)(2,1)S(1)}, bf16[4,128,1152]{2,1,0:T(8,128)(2,1)}, u32[]{:S(2)}) copy-start(bf16[4,128,1152]{2,1,0:T(8,128)(2,1)} %param.20) | copy-start | bytes 3538948
  25.8 35.2 %copy-start.18 = (f32[64,8,640]{2,1,0:T(8,128)}, f32[64,8,640]{2,1,0:T(8,128)S(1)}, u32[]{:S(2)}) copy-start(f32[64,8,640]{2,1,0:T(8,128)S(1)} %get-tuple-element.101.gate_ref) | copy-start | bytes 3932164
  25.8 163.2 %copy-start.2 = (f32[64,8,640]{2,1,0:T(8,128)}, f32[64,8,640]{2,1,0:T(8,128)S(1)}, u32[]{:S(2)}) copy-start(f32[64,8,640]{2,1,0:T(8,128)S(1)} %get-tuple-element.95.pre_ref) | copy-start | bytes 3932164
  34.8 26.2 %copy-start.4 = (f32[64,8,640]{2,1,0:T(8,128)}, f32[64,8,640]{2,1,0:T(8,128)S(1)}, u32[]{:S(2)}) copy-start(f32[64,8,640]{2,1,0:T(8,128)S(1)} %get-tuple-element.97.step_ref) | copy-start | bytes 3932164
  34.8 26.2 %copy-start.16 = (f32[64,8,640]{2,1,0:T(8,128)}, f32[64,8,640]{2,1,0:T(8,128)S(1)}, u32[]{:S(2)}) copy-start(f32[64,8,640]{2,1,0:T(8,128)S(1)} %get-tuple-element.98.drive_ref) | copy-start | bytes 3932164
  79.3 21.9 %copy-start.25 = (f32[128,1152]{1,0:T(8,128)}, f32[128,1152]{1,0:T(8,128)S(1)}, u32[]{:S(2)}) copy-start(f32[128,1152]{1,0:T(8,128)S(1)} %get-tuple-element.106.hidden_ref) | copy-start | bytes 1769476
  79.4 22.8 %copy-start.56 = (bf16[128,1152]{1,0:T(8,128)(2,1)}, bf16[128,1152]{1,0:T(8,128)(2,1)S(1)}, u32[]{:S(2)}) copy-start(bf16[128,1152]{1,0:T(8,128)(2,1)S(1)} %get-tuple-element.113.normed_ref) | copy-start | bytes 884740
  102.1 28.5 %copy-start.77 = (s32[4]{0:T(128)S(1)}, s32[4]{0:T(128)}, u32[]{:S(2)}) copy-start(s32[4]{0:T(128)} %lengths_ref.1) | copy-start | bytes 52
  148.9 27.8 %copy-start.57 = (bf16[128,1152]{1,0:T(8,128)(2,1)S(1)}, bf16[128,1152]{1,0:T(8,128)(2,1)}, u32[]{:S(2)}) copy-start(bf16[128,1152]{1,0:T(8,128)(2,1)} %copy-done.56) | copy-start | bytes 884740
  148.9 27.8 %copy-start.68 = (bf16[1152,8]{0,1:T(8,128)(2,1)S(1)}, bf16[1152,8]{0,1:T(8,128)(2,1)}, u32[]{:S(2)}) copy-start(bf16[1152,8]{0,1:T(8,128)(2,1)} %param.35) | copy-start | bytes 55300
  148.9 40.1 %copy-start.21 = (bf16[512,1152]{1,0:T(8,128)(2,1)S(1)}, bf16[512,1152]{1,0:T(8,128)(2,1)}, u32[]{:S(2)}) copy-start(bf16[512,1152]{1,0:T(8,128)(2,1)} %copy-done.20) | copy-start | bytes 3538948
  160.9 28.1 %copy-start.19 = (f32[64,8,640]{2,1,0:T(8,128)S(1)}, f32[64,8,640]{2,1,0:T(8,128)}, u32[]{:S(2)}) copy-start(f32[64,8,640]{2,1,0:T(8,128)} %copy-done.18) | copy-start | bytes 3932164
  191.4 31.4 %copy-start.17 = (f32[64,8,640]{2,1,0:T(8,128)S(1)}, f32[64,8,640]{2,1,0:T(8,128)}, u32[]{:S(2)}) copy-start(f32[64,8,640]{2,1,0:T(8,128)} %copy-done.16) | copy-start | bytes 3932164
  191.4 31.4 %copy-start.24 = (f32[16,8,640]{2,1,0:T(8,128)S(1)}, f32[16,8,640]{2,1,0:T(8,128)}, u32[]{:S(2)}) copy-start(f32[16,8,640]{2,1,0:T(8,128)} %copy-done.23) | copy-start | bytes 983044
  222.8 40.4 %copy-start.58 = (f32[4,16,1152]{2,1,0:T(8,128)}, f32[4,16,1152]{2,1,0:T(8,128)S(1)}, u32[]{:S(2)}) copy-start(f32[4,16,1152]{2,1,0:T(8,128)S(1)} %get-tuple-element.145) | copy-start | bytes 884740
  222.8 46.3 %copy-start.3 = (f32[64,8,640]{2,1,0:T(8,128)S(1)}, f32[64,8,640]{2,1,0:T(8,128)}, u32[]{:S(2)}) copy-start(f32[64,8,640]{2,1,0:T(8,128)} %copy-done.2) | copy-start | bytes 3932164
  222.8 46.3 %copy-start.31 = (f32[67,8,640]{2,1,0:T(8,128)S(1)}, f32[67,8,640]{2,1,0:T(8,128)}, u32[]{:S(2)}) copy-start(f32[67,8,640]{2,1,0:T(8,128)} %copy-done.30) | copy-start | bytes 4116484
  222.9 46.3 %copy-start.43 = (bf16[104,640]{1,0:T(8,128)(2,1)S(1)}, bf16[104,640]{1,0:T(8,128)(2,1)}, u32[]{:S(2)}) copy-start(bf16[104,640]{1,0:T(8,128)(2,1)} %copy-done.42) | copy-start | bytes 399364
  287.5 24.4 %copy-start.13 = (bf16[8,32,1152]{2,1,0:T(8,128)(2,1)S(1)}, bf16[8,32,1152]{2,1,0:T(8,128)(2,1)}, u32[]{:S(2)}) copy-start(bf16[8,32,1152]{2,1,0:T(8,128)(2,1)} %copy-done.12) | copy-start | bytes 1769476
  287.5 24.5 %copy-start.41 = (bf16[256,640]{1,0:T(8,128)(2,1)S(1)}, bf16[256,640]{1,0:T(8,128)(2,1)}, u32[]{:S(2)}) copy-start(bf16[256,640]{1,0:T(8,128)(2,1)} %fusion.16) | copy-start | bytes 983044
  287.5 24.5 %copy-start.64 = (bf16[72,1152]{1,0:T(8,128)(2,1)S(1)}, bf16[72,1152]{1,0:T(8,128)(2,1)}, u32[]{:S(2)}) copy-start(bf16[72,1152]{1,0:T(8,128)(2,1)} %copy-done.63) | copy-start | bytes 497668
  312.0 38.5 %copy-start.34 = (bf16[8,72,1152]{2,1,0:T(8,128)(2,1)}, bf16[8,72,1152]{2,1,0:T(8,128)(2,1)S(1)}, u32[]{:S(2)}) copy-start(bf16[8,72,1152]{2,1,0:T(8,128)(2,1)S(1)} %get-tuple-element.163) | copy-start | bytes 3981316
  312.0 38.8 %copy-start.51 = (f32[128,1152]{1,0:T(8,128)S(1)}, f32[128,1152]{1,0:T(8,128)}, u32[]{:S(2)}) copy-start(f32[128,1152]{1,0:T(8,128)} %copy-done.50) | copy-start | bytes 1769476
  356.1 35.2 %copy-start.35 = (bf16[8,72,1152]{2,1,0:T(8,128)(2,1)S(1)}, bf16[8,72,1152]{2,1,0:T(8,128)(2,1)}, u32[]{:S(2)}) copy-start(bf16[8,72,1152]{2,1,0:T(8,128)(2,1)} %copy-done.34) | copy-start | bytes 3981316
  (61 other events, 320.4 us)

commit v6 on v5

--- a/solution.py
+++ b/solution.py
@@ -106,7 +106,8 @@
             self.copies.append(remote(x_ref, me, slot, mate))
             slot += 1
         chain = self.chains.setdefault(axis, [])
-        for mask in order_of(groups):
+        masks = order_of(groups)
+        for mask in masks[1::2] + masks[::2]:
             row = flipped(place, mask) * mode + side
             for cut in cuts_of(x_ref.shape[0]):
                 first = remote(x_ref, me, slot, row, cut)
@@ -723,7 +724,7 @@
             pltpu.SemaphoreType.DMA((count // 2,)),
         ],
         compiler_params=pltpu.CompilerParams(
-            collective_id=number, has_side_effects=True, vmem_limit_bytes=36 * MIB
+            collective_id=number, has_side_effects=True, vmem_limit_bytes=30 * MIB
         ),
     )(tokens, gain, w_in, params, xproj, valid)
 
@@ -1074,7 +1075,7 @@
         ]
         + [sem for item in items for sem in sems_of(item)],
         compiler_params=pltpu.CompilerParams(
-            collective_id=number, has_side_effects=True, vmem_limit_bytes=36 * MIB
+            collective_id=number, has_side_effects=True, vmem_limit_bytes=30 * MIB
         ),
     )(tokens, grad, rim, grad_z, normed, w_in, *[x for x, _, _ in exchanges])
 
@@ -1402,7 +1403,7 @@
     act_shape, state_shape, wide_shape = (steps, lines, full), (states, lines, full), (states, steps, lines, LANES)
     dt_pre, step_size, drive, own_states, sums = by_tiles(
         functools.partial(totals_kernel, rank, taps),
-        20,
+        16,
         full,
         [
             (pre_act, "tile"),
@@ -1423,7 +1424,7 @@
     (enter,) = carried(own_states, sums, params, "seq", False, 2)
     y_full, gated, state, out_part = by_tiles(
         functools.partial(states_kernel, rank, seqs, taps, inner),
-        36,
+        30,
         full,
         [
             (step_size, "tile"),
@@ -1526,7 +1527,7 @@
     (grad_mixed,) = exchange(8, (grad_low, 2, "chan"))
     grad_y, grad_z, grad_out_w, grad_in_gate, skip_sums, back_last = by_tiles(
         functools.partial(back_totals_kernel, rank, seqs, inner),
-        28,
+        22,
         full,
         [
             (step_size, "tile"),
@@ -1564,7 +1565,7 @@
     items = items_of(riders)
     side, log_sums, bias_sums, grad_dt_w, low_part, by_out, by_gate, hidden_all, grad_pre_all = by_tiles(
         functools.partial(back_kernel, rank, full // LANES, [("seq", n_seq, across)] * 2, items),
-        46,
+        38,
         full,
         [
             (step_size, "tile"),
@@ -1608,7 +1609,7 @@
     grad_mapped = summed_over(low_part, "chan", 10).astype(bf16)
     grad_conv_in, rims, grad_xproj, conv_sums = by_tiles(
         functools.partial(conv_back_kernel, states, taps),
-        20,
+        14,
         full,
         [
             (grad_mapped, "whole"),

time: 403 us -> 402 us (level)
    unnamed x171 -> x159, local copies, waits for them, and re-layouts: 33.5 us -> 35.5 us
where the time goes in v6:
time: 402 us; the launch traced here: 401 us
  Pallas kernels  339 us (84%)
  local copies, waits for them, and re-layouts  47.5 us (12%)
  matrix products  7.92 us (2%)
  other arithmetic  5.62 us (1%)
    pallas_call x6, Pallas kernels, exchange(): pl.pallas_call(functools.partial(exchange_kernel, items), out_shape=[land...  111 us
    pallas_call x5, Pallas kernels, by_tiles(): pl.pallas_call(kernel, grid=(full // LANES,), in_specs=[block_of(a.shape,...  79.1 us
    pallas_call x2, Pallas kernels, share_of(): pl.pallas_call(functools.partial(share_kernel, [(axis, lax.axis_size(axis...  50.6 us
    unnamed x159, local copies, waits for them, and re-layouts  35.5 us
    pallas_call x2, Pallas kernels, carried(): pl.pallas_call(functools.partial(carry_kernel, axis, count, back, items),...  26.2 us
    pallas_call x1, Pallas kernels, ends(): pl.pallas_call(functools.partial(ends_kernel, lax.axis_size('seq'), items...  24.4 us
    pallas_call x2, Pallas kernels, expert(): pl.pallas_call(expert_back_kernel if back else expert_kernel, grid=(parts...  21.3 us
    pallas_call x1, Pallas kernels, front(): pl.pallas_call(functools.partial(front_kernel, lax.axis_size('seq'), coun...  13.7 us

profile of v6, /device:TPU:0, one launch (start us, length us, event | category | flops | bytes accessed | tf_op | source)
XLA Modules:
  0.0 401.2 jit_solution(3437383687803794807)
XLA Ops:
  9.8 13.7 %shard_map.314 = (bf16[512,1152]{1,0:T(8,128)(2,1)S(1)}, f32[67,8,640]{2,1,0:T(8,128)S(1)}, f32[64,8,640]{2,1,0:T(8,128)S(1)}, f32[64,8,640]{2,1,0:T(8,128)S(1)}, bf16[512,104]{1,0:T(8,128)(2,1)S(1)}) custom-call(bf16[4,128,1152]{2,1,0:T(8,128)(2,1)S(1)} %copy-done.6, f32[1,1152]{1,0:T(1,128)S(1)} %broadcast_in_dim.35.gain_ref, ...), custom_call_target="tpu_custom_call" | custom-call | tf_op jit(solution)/shard_map/pallas_call | solution.py:704
  25.7 7.9 %shard_map.315 = (f32[64,8,640]{2,1,0:T(8,128)S(1)}, f32[64,8,640]{2,1,0:T(8,128)S(1)}, f32[64,8,640]{2,1,0:T(8,128)S(1)}, f32[16,8,640]{2,1,0:T(8,128)S(1)}, f32[8,640]{1,0:T(8,128)S(1)}) custom-call(f32[64,8,640]{2,1,0:T(8,128)S(1)} %get-tuple-element.95.pre_ref, bf16[512,104]{1,0:T(8,128)(2,1)S(1)} %get-tuple-element.96.mapped_ref, ...), custom_call_target="tpu_custom_call" | custom-call | flops 1000 | bytes 1000 | tf_op jit(solution)/shard_map/pallas_call | solution.py:1298
  33.6 11.6 %shard_map.316.enter_ref.first_ref = f32[16,8,640]{2,1,0:T(8,128)S(1)} custom-call(f32[16,8,640]{2,1,0:T(8,128)S(1)} %get-tuple-element.99.refs_0_, f32[8,640]{1,0:T(8,128)S(1)} %get-tuple-element.100.refs_1_, f32[24,640]{1,0:T(8,128)S(1)} %pad.24.params_ref.rate_ref.refs_2_), custom_call_target="tpu_custom_call" | custom-call | tf_op jit(solution)/shard_map/pallas_call | solution.py:510
  45.2 14.7 %shard_map.317 = (f32[64,8,640]{2,1,0:T(8,128)S(1)}, bf16[512,640]{1,0:T(8,128)(2,1)S(1)}, f32[64,16,8,640]{3,2,1,0:T(8,128)}, bf16[512,1152]{1,0:T(8,128)(2,1)S(1)}) custom-call(f32[64,8,640]{2,1,0:T(8,128)S(1)} %get-tuple-element.97.step_ref, f32[64,8,640]{2,1,0:T(8,128)S(1)} %get-tuple-element.98.drive_ref, ...), custom_call_target="tpu_custom_call" | custom-call | flops 1000 | bytes 1000 | tf_op jit(solution)/shard_map/pallas_call | solution.py:1298
  61.8 10.9 %shard_map.318.mixed_ref = f32[128,1152]{1,0:T(8,128)S(1)} custom-call(bf16[4,128,1152]{2,1,0:T(8,128)(2,1)S(1)} %bitcast.76), custom_call_target="tpu_custom_call" | custom-call | tf_op jit(solution)/shard_map/pallas_call | solution.py:370
  80.6 21.9 %shard_map.320 = bf16[8,32,1152]{2,1,0:T(8,128)(2,1)S(1)} custom-call(bf16[8,32,1152]{2,1,0:T(8,128)(2,1)S(1)} %bitcast.80), custom_call_target="tpu_custom_call" | custom-call | tf_op jit(solution)/shard_map/pallas_call | solution.py:172
  103.4 10.5 %shard_map.321 = (bf16[4,256,768]{2,1,0:T(8,128)(2,1)}, bf16[256,3072]{1,0:T(8,128)(2,1)}, bf16[256,1152]{1,0:T(8,128)(2,1)}) custom-call(bf16[256,1152]{1,0:T(8,128)(2,1)} %bitcast.61, bf16[1152,3072]{1,0:T(8,128)(2,1)} %bitcast.92, bf16[3072,1152]{1,0:T(8,128)(2,1)} %bitcast.94), custom_call_target="tpu_custom_call" | custom-call | flops 1000 | bytes 1000 | tf_op jit(solution)/shard_map/pallas_call | solution.py:1231
  115.0 16.8 %shard_map.322 = bf16[8,32,1152]{2,1,0:T(8,128)(2,1)S(1)} custom-call(bf16[8,32,1152]{2,1,0:T(8,128)(2,1)S(1)} %bitcast.81), custom_call_target="tpu_custom_call" | custom-call | tf_op jit(solution)/shard_map/pallas_call | solution.py:172
  133.2 16.1 %shard_map.324 = bf16[8,32,1152]{2,1,0:T(8,128)(2,1)S(1)} custom-call(bf16[8,32,1152]{2,1,0:T(8,128)(2,1)S(1)} %bitcast.79), custom_call_target="tpu_custom_call" | custom-call | tf_op jit(solution)/shard_map/pallas_call | solution.py:172
  150.1 10.8 %shard_map.325 = (bf16[4,256,768]{2,1,0:T(8,128)(2,1)}, bf16[256,1152]{1,0:T(8,128)(2,1)}) custom-call(bf16[256,1152]{1,0:T(8,128)(2,1)} %bitcast.63, bf16[1152,3072]{1,0:T(8,128)(2,1)} %bitcast.93, bf16[3072,1152]{1,0:T(8,128)(2,1)} %bitcast.95, bf16[256,3072]{1,0:T(8,128)(2,1)} %get-tuple-element.110.slope_ref), custom_call_target="tpu_custom_call" | custom-call | flops 1000 | bytes 1000 | tf_op jit(solution)/shard_map/pallas_call | solution.py:1231
  162.0 15.9 %shard_map.326 = bf16[8,32,1152]{2,1,0:T(8,128)(2,1)S(1)} custom-call(bf16[8,32,1152]{2,1,0:T(8,128)(2,1)S(1)} %bitcast.82), custom_call_target="tpu_custom_call" | custom-call | tf_op jit(solution)/shard_map/pallas_call | solution.py:172
  179.1 10.5 %shard_map.328 = bf16[4,128,1152]{2,1,0:T(8,128)(2,1)S(1)} custom-call(bf16[128,1152]{1,0:T(8,128)(2,1)S(1)} %get-tuple-element.116.refs_0_), custom_call_target="tpu_custom_call" | custom-call | tf_op jit(solution)/shard_map/pallas_call | solution.py:172
  193.4 13.1 %shard_map.329 = (f32[64,8,640]{2,1,0:T(8,128)S(1)}, bf16[512,640]{1,0:T(8,128)(2,1)S(1)}, bf16[576,1152]{1,0:T(8,128)(2,1)S(1)}, bf16[576,1152]{1,0:T(8,128)(2,...) custom-call(f32[64,8,640]{2,1,0:T(8,128)S(1)} %copy-done.3, bf16[512,104]{1,0:T(8,128)(2,1)S(1)} %get-tuple-element.96.mapped_ref, ...), custom_call_target="tpu_custom_call" | custom-call | flops 1000 | bytes 1000 | tf_op jit(solution)/shard_map/pallas_call | solution.py:1298
  207.4 14.7 %shard_map.330 = (f32[16,8,640]{2,1,0:T(8,128)S(1)}, f32[4,16,1152]{2,1,0:T(8,128)S(1)}) custom-call(f32[16,8,640]{2,1,0:T(8,128)S(1)} %get-tuple-element.122.refs_0_, f32[8,640]{1,0:T(8,128)S(1)} %get-tuple-element.100.refs_1_, f32[24,640]{1,0:T(8,128)S(1)} %pad.24.params_ref.rate_ref.refs_2_, f32[16,1152]{1,0:T(8,128)S(1)} %get-tuple-element.123.refs_3_), custom_call_target="tpu_custom_call" | custom-call | tf_op jit(solution)/shard_map/pallas_call | solution.py:510
  222.1 40.5 %shard_map.331 = (f32[64,8,640]{2,1,0:T(8,128)S(1)}, f32[16,8,640]{2,1,0:T(8,128)S(1)}, f32[8,640]{1,0:T(8,128)S(1)}, f32[104,640]{1,0:T(8,128)S(1)}, bf16[512,1...) custom-call(f32[64,8,640]{2,1,0:T(8,128)S(1)} %copy-done.3, ...), custom_call_target="tpu_custom_call" | custom-call | flops 1000 | bytes 1000 | tf_op jit(solution)/shard_map/pallas_call | solution.py:1298
  264.0 5.9 %shard_map.332 = f32[512,104]{1,0:T(8,128)S(1)} custom-call(bf16[512,104]{1,0:T(8,128)(2,1)S(1)} %get-tuple-element.130.x_ref), custom_call_target="tpu_custom_call" | custom-call | tf_op jit(solution)/shard_map/pallas_call | solution.py:237
  269.9 2.9 shard_map.333
  275.7 1.7 copy-done.5
  282.4 24.4 %shard_map.334 = (bf16[576,1152]{1,0:T(8,128)(2,1)S(1)}, bf16[512,1152]{1,0:T(8,128)(2,1)S(1)}, f32[1,1152]{1,0:T(1,128)S(1)}, bf16[8,72,1152]{2,1,0:T(8,128)(2,1)S(1)}, bf16[4,256,1152]{2,1,0:T(8,128)(2,1)S(1)}) custom-call(bf16[4,128,1152]{2,1,0:T(8,128)(2,1)S(1)} %copy-done.7, f32[64,8,640]{2,1,0:T(8,128)S(1)} %copy-done.41, f32[3,8,640]{2,1,0:T(8,128)S(1)} %copy-done.66, ...), custom_call_target="tpu_custom_call" | custom-call | tf_op jit(solution)/shard_map/pallas_call | solution.py:1061
  306.9 39.7 %shard_map.335 = (f32[128,1152]{1,0:T(8,128)S(1)}, f32[40,128]{1,0:T(8,128)S(1)}, bf16[32,640]{1,0:T(8,128)(2,1)S(1)}, bf16[72,1152]{1,0:T(8,128)(2,1)S(1)}, f32...) custom-call(bf16[4,128,1152]{2,1,0:T(8,128)(2,1)S(1)} %bitcast.77, ...), custom_call_target="tpu_custom_call" | custom-call | tf_op jit(solution)/shard_map/pallas_call | solution.py:370
  349.1 4.0 %convolution_bitcast_fusion = f32[768,1152]{1,0:T(8,128)} fusion(bf16[4,256,768]{2,1,0:T(8,128)(2,1)S(1)} %copy-done.29, bf16[4,256,1152]{2,1,0:T(8,128)(2,1)S(1)} %get-tuple-element.151), kind=kOutput, calls=%fused_computation | convolution fusion | flops 1811939328 | bytes 7471104 | tf_op jit(solution)/shard_map/dot_general | solution.py:582
  353.2 3.9 convolution_bitcast_fusion.1
  357.1 29.6 %shard_map.336 = (bf16[4,128,1152]{2,1,0:T(8,128)(2,1)S(1)}, bf16[4,128,1152]{2,1,0:T(8,128)(2,1)S(1)}, f32[8,40,128]{2,1,0:T(8,128)S(1)}, bf16[8,32,640]{2,1,0:...) custom-call(bf16[128,1152]{1,0:T(8,128)(2,1)S(1)} %fusion.8.refs_0_, ...), custom_call_target="tpu_custom_call" | custom-call | tf_op jit(solution)/shard_map/pallas_call | solution.py:172
  390.4 4.1 %shard_map.337 = (f32[2,576,1152]{2,1,0:T(8,128)}, f32[576,1152]{1,0:T(8,128)}, f32[512,1152]{1,0:T(8,128)}) custom-call(bf16[576,1152]{1,0:T(8,128)(2,1)S(1)} %bitcast.72, bf16[576,1152]{1,0:T(8,128)(2,1)S(1)} %bitcast.70, bf16[576,1152]{1,0:T(8,128)(2,1)S(1)} %bitcast.71, bf16[512,1152]{1,0:T(8,128)(2,1)S(1)} %bitcast.75), custom_call_target="tpu_custom_call" | custom-call | flops 1000 | bytes 1000 | tf_op jit(solution)/shard_map/pallas_call | solution.py:1261
  (218 shorter events, 53.9 us)
Async XLA Ops:
  0.7 131.2 %copy-start = (bf16[4,128,1152]{2,1,0:T(8,128)(2,1)S(1)}, bf16[4,128,1152]{2,1,0:T(8,128)(2,1)}, u32[]{:S(2)}) copy-start(bf16[4,128,1152]{2,1,0:T(8,128)(2,1)} %param.20) | copy-start | bytes 3538948
  25.6 34.2 %copy-start.16 = (f32[64,8,640]{2,1,0:T(8,128)}, f32[64,8,640]{2,1,0:T(8,128)S(1)}, u32[]{:S(2)}) copy-start(f32[64,8,640]{2,1,0:T(8,128)S(1)} %get-tuple-element.101.gate_ref) | copy-start | bytes 3932164
  25.6 19.6 %copy-start.12 = (bf16[576,1152]{1,0:T(8,128)(2,1)S(1)}, bf16[576,1152]{1,0:T(8,128)(2,1)}, u32[]{:S(2)}) copy-start(bf16[576,1152]{1,0:T(8,128)(2,1)} %out_w_ref.3) | copy-start | bytes 3981316
  33.6 26.3 %copy-start.2 = (f32[64,8,640]{2,1,0:T(8,128)}, f32[64,8,640]{2,1,0:T(8,128)S(1)}, u32[]{:S(2)}) copy-start(f32[64,8,640]{2,1,0:T(8,128)S(1)} %get-tuple-element.97.step_ref) | copy-start | bytes 3932164
  33.6 26.3 %copy-start.14 = (f32[64,8,640]{2,1,0:T(8,128)}, f32[64,8,640]{2,1,0:T(8,128)S(1)}, u32[]{:S(2)}) copy-start(f32[64,8,640]{2,1,0:T(8,128)S(1)} %get-tuple-element.98.drive_ref) | copy-start | bytes 3932164
  33.6 26.3 %copy-start.36 = (f32[64,8,640]{2,1,0:T(8,128)}, f32[64,8,640]{2,1,0:T(8,128)S(1)}, u32[]{:S(2)}) copy-start(f32[64,8,640]{2,1,0:T(8,128)S(1)} %get-tuple-element.125.dt_ref) | copy-start | bytes 3932164
  80.6 21.9 %copy-start.23 = (f32[128,1152]{1,0:T(8,128)}, f32[128,1152]{1,0:T(8,128)S(1)}, u32[]{:S(2)}) copy-start(f32[128,1152]{1,0:T(8,128)S(1)} %get-tuple-element.106.hidden_ref) | copy-start | bytes 1769476
  103.4 28.6 %copy-start.69 = (s32[4]{0:T(128)S(1)}, s32[4]{0:T(128)}, u32[]{:S(2)}) copy-start(s32[4]{0:T(128)} %lengths_ref.1) | copy-start | bytes 52
  113.9 18.0 %copy-start.24 = (f32[128,1152]{1,0:T(8,128)S(1)}, f32[128,1152]{1,0:T(8,128)}, u32[]{:S(2)}) copy-start(f32[128,1152]{1,0:T(8,128)} %copy-done.23) | copy-start | bytes 1769476
  133.2 27.7 %copy-start.67 = (f32[1,1152]{1,0:T(1,128)}, f32[1,1152]{1,0:T(1,128)S(1)}, u32[]{:S(2)}) copy-start(f32[1,1152]{1,0:T(1,128)S(1)} %get-tuple-element.115.loss_ref) | copy-start | bytes 13828
  150.1 27.8 %copy-start.52 = (f32[128,1152]{1,0:T(8,128)S(1)}, f32[128,1152]{1,0:T(8,128)}, u32[]{:S(2)}) copy-start(f32[128,1152]{1,0:T(8,128)} %copy-done.51) | copy-start | bytes 1769476
  162.0 27.7 %copy-start.17 = (f32[64,8,640]{2,1,0:T(8,128)S(1)}, f32[64,8,640]{2,1,0:T(8,128)}, u32[]{:S(2)}) copy-start(f32[64,8,640]{2,1,0:T(8,128)} %copy-done.16) | copy-start | bytes 3932164
  193.4 28.7 %copy-start.15 = (f32[64,8,640]{2,1,0:T(8,128)S(1)}, f32[64,8,640]{2,1,0:T(8,128)}, u32[]{:S(2)}) copy-start(f32[64,8,640]{2,1,0:T(8,128)} %copy-done.14) | copy-start | bytes 3932164
  193.4 28.7 %copy-start.22 = (f32[16,8,640]{2,1,0:T(8,128)S(1)}, f32[16,8,640]{2,1,0:T(8,128)}, u32[]{:S(2)}) copy-start(f32[16,8,640]{2,1,0:T(8,128)} %copy-done.21) | copy-start | bytes 983044
  193.4 28.7 %copy-start.37 = (f32[64,8,640]{2,1,0:T(8,128)S(1)}, f32[64,8,640]{2,1,0:T(8,128)}, u32[]{:S(2)}) copy-start(f32[64,8,640]{2,1,0:T(8,128)} %copy-done.36) | copy-start | bytes 3932164
  222.1 40.5 %copy-start.55 = (f32[4,16,1152]{2,1,0:T(8,128)}, f32[4,16,1152]{2,1,0:T(8,128)S(1)}, u32[]{:S(2)}) copy-start(f32[4,16,1152]{2,1,0:T(8,128)S(1)} %get-tuple-element.145) | copy-start | bytes 884740
  222.1 47.8 %copy-start.31 = (f32[67,8,640]{2,1,0:T(8,128)S(1)}, f32[67,8,640]{2,1,0:T(8,128)}, u32[]{:S(2)}) copy-start(f32[67,8,640]{2,1,0:T(8,128)} %copy-done.30) | copy-start | bytes 4116484
  282.4 24.4 %copy-start.11 = (bf16[8,32,1152]{2,1,0:T(8,128)(2,1)S(1)}, bf16[8,32,1152]{2,1,0:T(8,128)(2,1)}, u32[]{:S(2)}) copy-start(bf16[8,32,1152]{2,1,0:T(8,128)(2,1)} %copy-done.10) | copy-start | bytes 1769476
  282.4 24.4 %copy-start.42 = (bf16[256,640]{1,0:T(8,128)(2,1)S(1)}, bf16[256,640]{1,0:T(8,128)(2,1)}, u32[]{:S(2)}) copy-start(bf16[256,640]{1,0:T(8,128)(2,1)} %fusion.16) | copy-start | bytes 983044
  282.4 24.4 %copy-start.63 = (bf16[72,1152]{1,0:T(8,128)(2,1)S(1)}, bf16[72,1152]{1,0:T(8,128)(2,1)}, u32[]{:S(2)}) copy-start(bf16[72,1152]{1,0:T(8,128)(2,1)} %copy-done.62) | copy-start | bytes 497668
  306.8 39.8 %copy-start.32 = (bf16[8,72,1152]{2,1,0:T(8,128)(2,1)}, bf16[8,72,1152]{2,1,0:T(8,128)(2,1)S(1)}, u32[]{:S(2)}) copy-start(bf16[8,72,1152]{2,1,0:T(8,128)(2,1)S(1)} %get-tuple-element.163) | copy-start | bytes 3981316
  306.9 40.8 %copy-start.78 = (f32[128]{0:T(128)S(1)}, f32[128]{0:T(128)}, u32[]{:S(2)}) copy-start(f32[128]{0:T(128)} %get-tuple-element.178) | copy-start | bytes 1540
  306.9 40.8 %copy-start.76 = (bf16[1152]{0:T(1024)(128)(2,1)S(1)}, bf16[1152]{0:T(1024)(128)(2,1)}, u32[]{:S(2)}) copy-start(bf16[1152]{0:T(1024)(128)(2,1)} %param.24) | copy-start | bytes 6916
  306.9 41.1 %copy-start.50 = (f32[128,1152]{1,0:T(8,128)S(1)}, f32[128,1152]{1,0:T(8,128)}, u32[]{:S(2)}) copy-start(f32[128,1152]{1,0:T(8,128)} %copy-done.49) | copy-start | bytes 1769476
  (55 other events, 235.3 us)
